TPU v7x, 32 devices: a whole 2x2x4 slice. The times are simulated.
32 devices in a mesh: region: 8 (over z, y), col: 4 (over x, core).
Axes of the slice: x: 2, y: 2, z: 4, core: 2. Of those that a mesh axis runs over, the one named last changes fastest.
Arguments:
- basis_v: bfloat16 [49152, 512], P('region', 'col'), may hold values from -6 to 6
- basis_w: bfloat16 [49152, 512], P(('region', 'col')), may hold values from -0.0546875 to 0.0546875
- couplings: bfloat16 [384, 48, 128, 128], P('region', 'col'), may hold values from -0.078125 to 0.078125
- coupling_cols: int32 [384, 48], P('region', 'col'), may hold values from 0 to 383, as said below
Outputs:
- reduced: float32 [512, 512], P(('region', 'col'))
Inputs may be any that keep to these rules, and one draw needn't show every extreme that they name: `coupling_cols`: the 48 block columns of one block row are distinct and differ from its row number by at most 48; every block row takes the columns at distance 48 on both sides where they exist.
All inputs are finite; a program needn't handle non-finite values.
Results may differ from a plain program's by a relative error of at most 0.0003.
Values may be sent and summed in bfloat16 or wider, within the bound.
No kernel may reach another device: no remote copies, remote signals or barrier semaphores. Data moves between devices by JAX's collectives and lax.ppermute only.
A program may use at most 192 MiB of HBM per device.

v0:
```python
import math

import jax
import jax.numpy as jnp
from jax import lax
from jax.sharding import PartitionSpec as P


def extended(block, sides, width):
    for axis, dim in sides:
        count = lax.axis_size(axis)
        forward = [(i, i + 1) for i in range(count - 1)]
        backward = [(target, source) for source, target in forward]
        low = lax.ppermute(
            lax.slice_in_dim(block, block.shape[dim] - width, None, axis=dim), axis, forward
        )
        high = lax.ppermute(lax.slice_in_dim(block, 0, width, axis=dim), axis, backward)
        block = jnp.concatenate([low, block, high], axis=dim)
    return block


def coupled_rows(couplings, local_cols, widened_blocks, length):
    block = couplings.shape[2]
    slots_here = couplings.shape[1]
    width = widened_blocks.shape[2]
    per_group = math.gcd(length, 8)
    a_part = couplings
    c_part = local_cols
    a_part = a_part.reshape(length // per_group, per_group, slots_here, block, block)
    c_part = c_part.reshape(length // per_group, per_group, slots_here)

    def one_group(operands):
        blocks, columns = operands
        picked = widened_blocks[columns]
        return jnp.einsum("gkrs,gksc->grc", blocks, picked, preferred_element_type=jnp.float32)

    results = lax.map(one_group, (a_part, c_part))
    return results.reshape(length * block, width)


def project_rows(w_rows, image_rows):
    upper_part = image_rows.astype(jnp.bfloat16)
    kept_upper = lax.optimization_barrier(upper_part)
    lower_part = (image_rows - kept_upper.astype(jnp.float32)).astype(jnp.bfloat16)
    first_term = jnp.einsum("rc,rd->cd", w_rows, upper_part, preferred_element_type=jnp.float32)
    second_term = jnp.einsum("rc,rd->cd", w_rows, lower_part, preferred_element_type=jnp.float32)
    return first_term + second_term


def shards(basis_v, basis_w, couplings, coupling_cols):
    blocks_dev = couplings.shape[0]
    block = couplings.shape[2]
    rows_dev = blocks_dev * block
    region = lax.axis_index("region")
    with_rims = extended(basis_v, (("region", 0),), rows_dev)
    widened = lax.all_gather(with_rims, "col", axis=1, tiled=True)
    width = widened.shape[1]
    widened_blocks = widened.reshape(3 * blocks_dev, block, width)
    local_cols = coupling_cols - (region * blocks_dev - blocks_dev)

    def image_rows(offset, length):
        return coupled_rows(couplings, local_cols, widened_blocks, length // block)

    coupled_image = lax.psum_scatter(
        image_rows(jnp.int32(0), rows_dev // lax.axis_size("col") * lax.axis_size("col")),
        "col",
        scatter_dimension=0,
        tiled=True,
    )
    partial_tile = project_rows(basis_w, coupled_image)
    return lax.psum_scatter(partial_tile, ("region", "col"), scatter_dimension=0, tiled=True)


def solution(mesh):
    in_specs = (
        P("region", "col"),
        P(("region", "col"), None),
        P("region", "col", None, None),
        P("region", "col"),
    )
    out_specs = P(("region", "col"), None)
    return jax.shard_map(shards, mesh=mesh, in_specs=in_specs, out_specs=out_specs, check_vma=False)
```

profile of v0, /device:TPU:0, one launch (start us, length us, event | category | flops | bytes accessed | tf_op | source)
XLA Modules:
  0.0 602.6 jit_solution(15244175232230994961)
XLA Ops:
  6.5 5.1 collective-permute-start
  11.6 1.3 collective-permute-start.1
  12.9 66.3 %collective-permute-done = bf16[6144,128]{1,0:T(8,128)(2,1)S(1)} collective-permute-done((bf16[6144,128]{1,0:T(8,128)(2,1)}, bf16[6144,128]{1,0:T(8,128)(2,1)S(1)}, u32[]{:S(2)}, u32[]{:S(2)}) %collective-permute-start) | collective-permute-done | bytes 1572896 | tf_op jit(solution)/shard_map/ppermute | solution.py:14
  79.2 19.5 %pad_maximum_fusion = bf16[18432,128]{1,0:T(8,128)(2,1)} fusion(bf16[6144,128]{1,0:T(8,128)(2,1)S(1)} %collective-permute-done.1, bf16[6144,128]{1,0:T(8,128)(2,1)} %param.6, bf16[6144,128]{1,0:T(8,128)(2,1)S(1)} %collective-permute-done), kind=kLoop, calls=%fused_computation.8 | loop fusion | flops 14155776 | bytes 9437184 | tf_op jit(solution)/shard_map/concatenate | solution.py:18
  99.5 124.0 %all-gather.2.cloned.1.call-done = bf16[18432,512]{1,0:T(8,128)(2,1)} async-done(((bf16[18432,128]{1,0:T(8,128)(2,1)}), bf16[18432,512]{1,0:T(8,128)(2,1)}) %all-gather.2.cloned.1.call-update) | async-done | bytes 18874384 | tf_op jit(solution)/shard_map/all_gather | solution.py:56
  223.4 132.2 %while.10 = (s32[]{:T(128)}, f32[6,8,128,512]{3,2,1,0:T(8,128)}, bf16[6,8,12,128,128]{4,3,2,1,0:T(8,128)(2,1)}, s32[6,8,12]{2,1,0:T(8,128)S(1)}, bf16[144,128,512]{2,1,0:T(8,128)(2,1)}, /*index=5*/s32[]{:T(128)}) while((s32[]{:T(128)}, f32[6,8,128,512]{3,2,1,0:T(8,128)}, bf16[6,8,12,128,128]{4,3,2,1,0:T(8,128)(2,1)}, ...), condition=%wide.region_1.2_spmd, body=%wide.region_0.1_spmd.sunk | while | flops 1610614016 | bytes 42999112 | solution.py:37
  223.5 13.3 %gather_fusion = bf16[96,128,512]{2,1,0:T(8,128)(2,1)} fusion(bf16[144,128,512]{2,1,0:T(8,128)(2,1)} %get-tuple-element.90, s32[1024]{0:T(1024)S(1)} %pad_clamp_fusion.2), kind=kCustom, calls=%fused_computation.clone.1 | custom fusion | bytes 25166208 | tf_op jit(solution)/shard_map/while/body/eval_jaxpr/gather | solution.py:34
  236.8 8.6 %bitcast_dynamic-update-slice_fusion.2 = f32[6,8,128,512]{3,2,1,0:T(8,128)} fusion(f32[6,8,128,512]{3,2,1,0:T(8,128)} %get-tuple-element.81, s32[]{:T(128)} %get-tuple-element.80, bf16[8,12,128,512]{3,2,1,0:T(8,128)(2,1)} %bitcast.35, bf16[6,8,12,128,128]{4,3,2,1,0:T(8,128)(2,1)} %get-tuple-element.88), kind=kOutput, calls=%fused_computation.4.clone.1 | convolution fusion | flops 1610612736 | bytes 17826816 | tf_op jit(solution)/shard_map/while/body/eval_jaxpr/gkrs,gksc->grc/dot_general | solution.py:35
  245.5 13.3 %gather_fusion = bf16[96,128,512]{2,1,0:T(8,128)(2,1)} fusion(bf16[144,128,512]{2,1,0:T(8,128)(2,1)} %get-tuple-element.90, s32[1024]{0:T(1024)S(1)} %pad_clamp_fusion.2), kind=kCustom, calls=%fused_computation.clone.1 | custom fusion | bytes 25166208 | tf_op jit(solution)/shard_map/while/body/eval_jaxpr/gather | solution.py:34
  258.8 8.7 %bitcast_dynamic-update-slice_fusion.2 = f32[6,8,128,512]{3,2,1,0:T(8,128)} fusion(f32[6,8,128,512]{3,2,1,0:T(8,128)} %get-tuple-element.81, s32[]{:T(128)} %get-tuple-element.80, bf16[8,12,128,512]{3,2,1,0:T(8,128)(2,1)} %bitcast.35, bf16[6,8,12,128,128]{4,3,2,1,0:T(8,128)(2,1)} %get-tuple-element.88), kind=kOutput, calls=%fused_computation.4.clone.1 | convolution fusion | flops 1610612736 | bytes 17826816 | tf_op jit(solution)/shard_map/while/body/eval_jaxpr/gkrs,gksc->grc/dot_general | solution.py:35
  267.6 13.3 %gather_fusion = bf16[96,128,512]{2,1,0:T(8,128)(2,1)} fusion(bf16[144,128,512]{2,1,0:T(8,128)(2,1)} %get-tuple-element.90, s32[1024]{0:T(1024)S(1)} %pad_clamp_fusion.2), kind=kCustom, calls=%fused_computation.clone.1 | custom fusion | bytes 25166208 | tf_op jit(solution)/shard_map/while/body/eval_jaxpr/gather | solution.py:34
  280.8 8.7 %bitcast_dynamic-update-slice_fusion.2 = f32[6,8,128,512]{3,2,1,0:T(8,128)} fusion(f32[6,8,128,512]{3,2,1,0:T(8,128)} %get-tuple-element.81, s32[]{:T(128)} %get-tuple-element.80, bf16[8,12,128,512]{3,2,1,0:T(8,128)(2,1)} %bitcast.35, bf16[6,8,12,128,128]{4,3,2,1,0:T(8,128)(2,1)} %get-tuple-element.88), kind=kOutput, calls=%fused_computation.4.clone.1 | convolution fusion | flops 1610612736 | bytes 17826816 | tf_op jit(solution)/shard_map/while/body/eval_jaxpr/gkrs,gksc->grc/dot_general | solution.py:35
  289.7 13.3 %gather_fusion = bf16[96,128,512]{2,1,0:T(8,128)(2,1)} fusion(bf16[144,128,512]{2,1,0:T(8,128)(2,1)} %get-tuple-element.90, s32[1024]{0:T(1024)S(1)} %pad_clamp_fusion.2), kind=kCustom, calls=%fused_computation.clone.1 | custom fusion | bytes 25166208 | tf_op jit(solution)/shard_map/while/body/eval_jaxpr/gather | solution.py:34
  302.9 8.7 %bitcast_dynamic-update-slice_fusion.2 = f32[6,8,128,512]{3,2,1,0:T(8,128)} fusion(f32[6,8,128,512]{3,2,1,0:T(8,128)} %get-tuple-element.81, s32[]{:T(128)} %get-tuple-element.80, bf16[8,12,128,512]{3,2,1,0:T(8,128)(2,1)} %bitcast.35, bf16[6,8,12,128,128]{4,3,2,1,0:T(8,128)(2,1)} %get-tuple-element.88), kind=kOutput, calls=%fused_computation.4.clone.1 | convolution fusion | flops 1610612736 | bytes 17826816 | tf_op jit(solution)/shard_map/while/body/eval_jaxpr/gkrs,gksc->grc/dot_general | solution.py:35
  311.7 13.3 %gather_fusion = bf16[96,128,512]{2,1,0:T(8,128)(2,1)} fusion(bf16[144,128,512]{2,1,0:T(8,128)(2,1)} %get-tuple-element.90, s32[1024]{0:T(1024)S(1)} %pad_clamp_fusion.2), kind=kCustom, calls=%fused_computation.clone.1 | custom fusion | bytes 25166208 | tf_op jit(solution)/shard_map/while/body/eval_jaxpr/gather | solution.py:34
  324.9 8.7 %bitcast_dynamic-update-slice_fusion.2 = f32[6,8,128,512]{3,2,1,0:T(8,128)} fusion(f32[6,8,128,512]{3,2,1,0:T(8,128)} %get-tuple-element.81, s32[]{:T(128)} %get-tuple-element.80, bf16[8,12,128,512]{3,2,1,0:T(8,128)(2,1)} %bitcast.35, bf16[6,8,12,128,128]{4,3,2,1,0:T(8,128)(2,1)} %get-tuple-element.88), kind=kOutput, calls=%fused_computation.4.clone.1 | convolution fusion | flops 1610612736 | bytes 17826816 | tf_op jit(solution)/shard_map/while/body/eval_jaxpr/gkrs,gksc->grc/dot_general | solution.py:35
  333.7 13.3 %gather_fusion = bf16[96,128,512]{2,1,0:T(8,128)(2,1)} fusion(bf16[144,128,512]{2,1,0:T(8,128)(2,1)} %get-tuple-element.90, s32[1024]{0:T(1024)S(1)} %pad_clamp_fusion.2), kind=kCustom, calls=%fused_computation.clone.1 | custom fusion | bytes 25166208 | tf_op jit(solution)/shard_map/while/body/eval_jaxpr/gather | solution.py:34
  347.0 8.7 %bitcast_dynamic-update-slice_fusion.2 = f32[6,8,128,512]{3,2,1,0:T(8,128)} fusion(f32[6,8,128,512]{3,2,1,0:T(8,128)} %get-tuple-element.81, s32[]{:T(128)} %get-tuple-element.80, bf16[8,12,128,512]{3,2,1,0:T(8,128)(2,1)} %bitcast.35, bf16[6,8,12,128,128]{4,3,2,1,0:T(8,128)(2,1)} %get-tuple-element.88), kind=kOutput, calls=%fused_computation.4.clone.1 | convolution fusion | flops 1610612736 | bytes 17826816 | tf_op jit(solution)/shard_map/while/body/eval_jaxpr/gkrs,gksc->grc/dot_general | solution.py:35
  355.7 99.2 %reduce-scatter.5.cloned.1.call-done = f32[1536,512]{1,0:T(8,128)} async-done(((f32[6144,512]{1,0:T(8,128)}), f32[1536,512]{1,0:T(8,128)}) %reduce-scatter.5.cloned.1.call-update) | async-done | bytes 3145744 | tf_op jit(solution)/shard_map/reduce_scatter | solution.py:64
  454.9 2.2 convert_element_type.9
  457.7 1.0 fusion.6
  458.8 1.0 fusion.7
  459.8 1.3 copy.10
  461.1 135.0 %reduce-scatter.7.cloned.1.call-done = f32[16,512]{1,0:T(8,128)} async-done(((f32[512,512]{1,0:T(8,128)}), f32[16,512]{1,0:T(8,128)}) %reduce-scatter.7.cloned.1.call-update) | async-done | bytes 32784 | tf_op jit(solution)/shard_map/reduce_scatter | solution.py:71
  (34 shorter events, 2.0 us)
Async XLA Ops:
  6.5 450.6 %copy-start = (bf16[1536,512]{1,0:T(8,128)(2,1)S(1)}, bf16[1536,512]{1,0:T(8,128)(2,1)}, u32[]{:S(2)}) copy-start(bf16[1536,512]{1,0:T(8,128)(2,1)} %param.7) | copy-start | bytes 4718596
  6.5 216.9 %all-gather.2.cloned.1.call-start = ((), (), s32[]{:S(2)}) async-start(), calls=%async_computation.2 | async-start | bytes 23592960 | tf_op jit(solution)/shard_map/all_gather | solution.py:56
  6.5 72.7 %collective-permute-start = (bf16[6144,128]{1,0:T(8,128)(2,1)}, bf16[6144,128]{1,0:T(8,128)(2,1)S(1)}, u32[]{:S(2)}, u32[]{:S(2)}) collective-permute-start(bf16[6144,128]{1,0:T(8,128)(2,1)} %param.6), channel_id=1, source_target_pairs={{0,4},{4,8},{8,12},{12,16},{16,20},{20,24},{24,28},{1,5},{5,9},{9,... | collective-permute-start | bytes 4718600 | tf_op jit(solution)/shard_map/ppermute | solution.py:14
  11.6 67.6 %collective-permute-start.1 = (bf16[6144,128]{1,0:T(8,128)(2,1)}, bf16[6144,128]{1,0:T(8,128)(2,1)S(1)}, u32[]{:S(2)}, u32[]{:S(2)}) collective-permute-start(bf16[6144,128]{1,0:T(8,128)(2,1)} %param.6), channel_id=1, source_target_pairs={{4,0},{8,4},{12,8},{16,12},{20,16},{24,20},{28,24},{5,1},{9,5},{13... | collective-permute-start | bytes 4718600 | tf_op jit(solution)/shard_map/ppermute | solution.py:17
  98.7 0.7 copy-start.2
  98.7 356.2 %reduce-scatter.5.cloned.1.call-start = ((), (), s32[]{:S(2)}) async-start(), calls=%async_computation.3 | async-start | bytes 15728640 | tf_op jit(solution)/shard_map/reduce_scatter | solution.py:64
  355.7 240.4 %reduce-scatter.7.cloned.1.call-start = ((), (), s32[]{:S(2)}) async-start(), calls=%async_computation.4 | async-start | bytes 1081344 | tf_op jit(solution)/shard_map/reduce_scatter | solution.py:71
  454.9 2.8 copy-start.1
Sparse Core Ops, SparseCore 0:
  98.8 124.5 all-gather.1
  355.8 99.0 reduce-scatter.4
  461.2 134.7 reduce-scatter.6
where the time goes:
time: 603 us
  waiting for transfers between devices  424 us (70%)
  local copies, waits for them, and re-layouts  82.6 us (14%)
  matrix products  54.1 us (9%)
  other arithmetic  21.8 us (4%)
  between operations  13.2 us (2%)
  starting transfers between devices  6.47 us (1%)
    reduce_scatter x1, waiting for transfers between devices, shards(): lax.psum_scatter(partial_tile, ('region', 'col'), scatter_dimension=0, ti...  135 us
    all_gather x1, waiting for transfers between devices, shards(): widened = lax.all_gather(with_rims, 'col', axis=1, tiled=True)  124 us
    reduce_scatter x1, waiting for transfers between devices, shards(): lax.psum_scatter(image_rows(jnp.int32(0), rows_dev // lax.axis_size('col'...  99.2 us
    gather x6, local copies, waits for them, and re-layouts, one_group(): picked = widened_blocks[columns]  79.6 us
    ppermute x1, waiting for transfers between devices, extended(): lax.ppermute(lax.slice_in_dim(block, block.shape[dim] - width, None, axis...  66.3 us
    dot_general x6, matrix products, one_group(): jnp.einsum('gkrs,gksc->grc', blocks, picked, preferred_element_type=jnp.f...  52.1 us
    concatenate x1, other arithmetic, extended(): block = jnp.concatenate([low, block, high], axis=dim)  19.5 us
  transfers between devices with their start and end apart: 5, of which 4 were waited for; matrix products, arithmetic and copies ran while one was open for 0% of the time, Pallas kernels for 0%

commit v1 on v0

v1 whole, which is shorter than its diff:
```python
import functools

import jax
import jax.numpy as jnp
from jax import lax
from jax.experimental import pallas as pl
from jax.experimental.pallas import tpu as pltpu
from jax.sharding import PartitionSpec as P

EVERY = ("region", "col")
VMEM = 60 * 2**20


def moved(array, axis, target):
    count = lax.axis_size(axis)
    pairs = [(i, target(i)) for i in range(count)]
    return lax.ppermute(array, axis, [(i, j) for i, j in pairs if 0 <= j < count])


def to_core(array):
    return moved(array, "col", lambda c: c ^ 1)


def to_side(array):
    return moved(array, "col", lambda c: c ^ 2)


def to_pair(array):
    return moved(array, "region", lambda r: r ^ 1)


def to_next(array):
    return moved(array, "region", lambda r: r + 2 if r % 2 == 0 else r - 2)


def largest_divisor(length, limit):
    return max(d for d in range(1, limit + 1) if length % d == 0)


def image_kernel(group, pieces, cols_ref, offs_ref, own_ref, other_ref, *refs):
    v_refs, (out_ref, v_all, sems) = refs[:pieces], refs[pieces:]
    step = pl.program_id(0)
    slots, block = own_ref.shape[1], own_ref.shape[2]

    @pl.when(step == 0)
    def _():
        copies = []
        for p in range(pieces):
            rows = v_refs[p].shape[0]
            start = pl.multiple_of(offs_ref[p] * block, block)
            copies.append(
                pltpu.make_async_copy(v_refs[p], v_all.at[pl.ds(start, rows)], sems.at[p])
            )
        for copy in copies:
            copy.start()
        for copy in copies:
            copy.wait()

    for g in range(group):
        row = step * group + g
        left, right = [], []
        for a_ref, base in ((own_ref, 0), (other_ref, slots)):
            for s in range(slots):
                start = pl.multiple_of(cols_ref[row, base + s] * block, block)
                left.append(a_ref[g, s])
                right.append(v_all[pl.ds(start, block), :])
        out_ref[g] = jnp.dot(
            jnp.concatenate(left, axis=1),
            jnp.concatenate(right, axis=0),
            preferred_element_type=jnp.float32,
        )


def image_of(cols, offs, own, other, v_pieces):
    rows, slots, block = own.shape[:3]
    width = v_pieces[0].shape[1]
    group = largest_divisor(rows, 8)
    a_spec = pl.BlockSpec((group, slots, block, block), lambda i, c, o: (i, 0, 0, 0))
    return pl.pallas_call(
        functools.partial(image_kernel, group, len(v_pieces)),
        out_shape=jax.ShapeDtypeStruct((rows, block, width), jnp.float32),
        grid_spec=pltpu.PrefetchScalarGridSpec(
            num_scalar_prefetch=2,
            grid=(rows // group,),
            in_specs=[a_spec, a_spec] + [pl.BlockSpec(memory_space=pl.ANY)] * len(v_pieces),
            out_specs=pl.BlockSpec((group, block, width), lambda i, c, o: (i, 0, 0)),
            scratch_shapes=[
                pltpu.VMEM((3 * rows * block, width), jnp.bfloat16),
                pltpu.SemaphoreType.DMA((len(v_pieces),)),
            ],
        ),
        compiler_params=pltpu.CompilerParams(vmem_limit_bytes=VMEM),
        cost_estimate=pl.CostEstimate(
            flops=4 * rows * slots * block * block * width,
            bytes_accessed=4 * rows * slots * block * block + 6 * rows * block * width,
            transcendentals=0,
        ),
        name="image",
    )(cols, offs, own, other, *v_pieces)


def project_kernel(me_ref, *refs):
    w_refs, (first_ref, second_ref, out_ref, w_all, total, sems) = refs[:4], refs[4:]
    step = pl.program_id(0)
    rows, block = first_ref.shape[0], first_ref.shape[1]
    copies = [
        pltpu.make_async_copy(w_refs[q], w_all.at[q], sems.at[q]) for q in range(4)
    ]

    @pl.when(step == 0)
    def _():
        for copy in copies:
            copy.start()
        total[...] = jnp.zeros_like(total)

    for q in range(4):
        @pl.when(step == q)
        def _():
            copies[q].wait()

    w_rows = w_all[step]
    for part, ref in enumerate((first_ref, second_ref)):
        flipped = jnp.concatenate([ref[i].T for i in range(rows)], axis=1)
        upper = flipped.astype(jnp.bfloat16)
        lower = (flipped - upper.astype(jnp.float32)).astype(jnp.bfloat16)
        both = jnp.concatenate([upper, lower], axis=0)
        product = jnp.dot(both, w_rows, preferred_element_type=jnp.float32)
        width = flipped.shape[0]
        total[part] += product[:width] + product[width:]

    @pl.when(step == 3)
    def _():
        width = total.shape[1]
        side = me_ref[0] // 2
        for part in range(2):
            place = jnp.where(side == 0, part, 1 - part)
            out_ref[place] = total[part].T


def projected(me, w_pieces, first, second):
    rows, block, width = first.shape
    length, basis = w_pieces[0].shape
    image_spec = pl.BlockSpec((rows // 4, block, width), lambda s, m: (m[0] ^ s, 0, 0))
    return pl.pallas_call(
        project_kernel,
        out_shape=jax.ShapeDtypeStruct((2, basis, width), jnp.float32),
        grid_spec=pltpu.PrefetchScalarGridSpec(
            num_scalar_prefetch=1,
            grid=(4,),
            in_specs=[pl.BlockSpec(memory_space=pl.ANY)] * 4 + [image_spec] * 2,
            out_specs=pl.BlockSpec((2, basis, width), lambda s, m: (0, 0, 0)),
            scratch_shapes=[
                pltpu.VMEM((4, length, basis), jnp.bfloat16),
                pltpu.VMEM((2, width, basis), jnp.float32),
                pltpu.SemaphoreType.DMA((4,)),
            ],
        ),
        compiler_params=pltpu.CompilerParams(vmem_limit_bytes=VMEM),
        cost_estimate=pl.CostEstimate(
            flops=8 * rows * block * basis * width,
            bytes_accessed=8 * length * basis + 8 * rows * block * width,
            transcendentals=0,
        ),
        name="project",
    )(me, *w_pieces, first, second)


def shards(basis_v, basis_w, couplings, coupling_cols):
    rows, slots, block = couplings.shape[:3]
    width = basis_v.shape[1]
    basis = basis_w.shape[1]
    regions, columns = lax.axis_size("region"), lax.axis_size("col")
    region, col = lax.axis_index("region"), lax.axis_index("col")
    odd = region % 2
    half = rows // 2

    here = coupling_cols - (region * rows - rows)
    cols = jnp.concatenate([here, to_core(here)], axis=1)
    other = to_core(couplings)

    def cut(array, which):
        start = jnp.where(odd == 1, 1 - which, which) * (half * block)
        return lax.dynamic_slice_in_dim(array, start, half * block, axis=0)

    v_parts = [cut(basis_v, 0), cut(basis_v, 1)]
    side_parts = [to_side(v) for v in v_parts]
    near_first = [to_pair(v) for v in v_parts]
    far_first = [to_next(v) for v in near_first]
    near_second = [to_pair(v) for v in side_parts]
    far_second = [to_next(v) for v in near_second]

    w_core = to_core(basis_w)
    w_side = to_side(basis_w)
    w_cross = to_core(w_side)

    near_base = jnp.where(odd == 1, 0, 2 * rows)
    far_base = jnp.where(odd == 1, 2 * rows, 0)
    own_at = [rows + odd * half, rows + (1 - odd) * half]
    near_at = [near_base + (1 - odd) * half, near_base + odd * half]
    far_at = [far_base + (1 - odd) * half, far_base + odd * half]
    first_offs = jnp.stack([jnp.int32(rows)] + near_at + far_at).astype(jnp.int32)
    second_offs = jnp.stack(own_at + near_at + far_at).astype(jnp.int32)

    first = image_of(cols, first_offs, couplings, other, [basis_v] + near_first + far_first)
    second = image_of(
        cols, second_offs, couplings, other, side_parts + near_second + far_second
    )
    me = jnp.reshape(col, (1,)).astype(jnp.int32)
    partial = projected(me, [basis_w, w_core, w_side, w_cross], first, second)

    devices = regions * columns
    tile = basis // devices
    sent = partial.reshape(2, devices, tile, width).transpose(1, 0, 2, 3)
    received = lax.all_to_all(sent, EVERY, 0, 0, tiled=True)
    summed = received.reshape(regions, columns // 2, 2, 2, tile, width).sum(axis=(0, 1))
    return summed.transpose(2, 1, 0, 3).reshape(tile, basis)


def solution(mesh):
    in_specs = (
        P("region", "col"),
        P(("region", "col"), None),
        P("region", "col", None, None),
        P("region", "col"),
    )
    out_specs = P(("region", "col"), None)
    return jax.shard_map(shards, mesh=mesh, in_specs=in_specs, out_specs=out_specs, check_vma=False)
```

time: 603 us -> 176 us (0.29)
  waiting for transfers between devices: 424 us -> 67.9 us
  local copies, waits for them, and re-layouts: 82.6 us -> 6.84 us
  matrix products: 54.1 us -> 0 us
  Pallas kernels: 0 us -> 52.3 us
  other arithmetic: 21.8 us -> 0.73 us
  starting transfers between devices: 6.47 us -> 27 us
  blocking collectives: 0 us -> 20.2 us
  between operations: 13.2 us -> 0.12 us
    reduce_scatter x2 -> x0, waiting for transfers between devices: 234 us -> none  [the longest x1 135 us: shards(): lax.psum_scatter(partial_tile, ('region', 'col'), scatter_dimension=0, ti...]
    all_gather x1 -> x0, waiting for transfers between devices: 124 us -> none  [shards(): widened = lax.all_gather(with_rims, 'col', axis=1, tiled=True)]
    gather x6 -> x0, local copies, waits for them, and re-layouts: 79.6 us -> none  [one_group(): picked = widened_blocks[columns]]
    dot_general x8 -> x0, matrix products: 54.1 us -> none  [the longest x6 52.1 us: one_group(): jnp.einsum('gkrs,gksc->grc', blocks, picked, preferred_element_type=jnp.f...]
    pallas_call x0 -> x3, Pallas kernels: none -> 52.3 us  [the longest x2 43.8 us: image_of(): pl.pallas_call(functools.partial(image_kernel, group, len(v_pieces)), out...]
    ppermute x2 -> x15, starting transfers between devices: 6.38 us -> 27 us  [moved(): lax.ppermute(array, axis, [(i, j) for i, j in pairs if 0 <= j < count])]
    all_to_all x0 -> x1, blocking collectives: none -> 20.2 us  [shards(): received = lax.all_to_all(sent, EVERY, 0, 0, tiled=True)]
    concatenate x1, other arithmetic: 19.5 us -> 0.68 us  [shards(): cols = jnp.concatenate([here, to_core(here)], axis=1)]
  transfers between devices with their start and end apart: 5 -> 15, of which waited for: 4 -> 6; matrix products, arithmetic and copies ran while one was open for 0% -> 3% of each run, Pallas kernels for 0% -> 25%
where the time goes in v1:
time: 176 us; the launch traced here: 175 us
  waiting for transfers between devices  67.9 us (39%)
  Pallas kernels  52.3 us (30%)
  starting transfers between devices  27 us (15%)
  blocking collectives  20.2 us (11%)
  local copies, waits for them, and re-layouts  6.84 us (4%)
    ppermute x15, waiting for transfers between devices, moved(): lax.ppermute(array, axis, [(i, j) for i, j in pairs if 0 <= j < count])  67.9 us
    pallas_call x2, Pallas kernels, image_of(): pl.pallas_call(functools.partial(image_kernel, group, len(v_pieces)), out...  43.8 us
    ppermute x15, starting transfers between devices, moved(): lax.ppermute(array, axis, [(i, j) for i, j in pairs if 0 <= j < count])  27 us
    all_to_all x1, blocking collectives, shards(): received = lax.all_to_all(sent, EVERY, 0, 0, tiled=True)  20.2 us
    pallas_call x1, Pallas kernels, projected(): pl.pallas_call(project_kernel, out_shape=jax.ShapeDtypeStruct((2, basis,...  8.52 us
  transfers between devices with their start and end apart: 15, of which 6 were waited for; matrix products, arithmetic and copies ran while one was open for 3% of the time, Pallas kernels for 25%

profile of v1, /device:TPU:0, one launch (start us, length us, event | category | flops | bytes accessed | tf_op | source)
XLA Modules:
  0.0 175.2 jit_solution(13435902378266282320)
XLA Ops:
  0.5 2.7 %constant_dynamic-slice_fusion = (bf16[3072,128]{1,0:T(8,128)(2,1)}, bf16[3072,128]{1,0:T(8,128)(2,1)}) fusion(bf16[6144,128]{1,0:T(8,128)(2,1)} %refs_0_.2, s32[]{:T(128)S(6)} %select_n.32, s32[]{:T(128)S(6)} %select_n.30), kind=kLoop, calls=%fused_computation.3 | loop fusion | bytes 3145736 | tf_op jit(solution)/shard_map/dynamic_slice | solution.py:183
  3.2 2.5 %collective-permute-start.9 = (bf16[3072,128]{1,0:T(8,128)(2,1)}, bf16[3072,128]{1,0:T(8,128)(2,1)}, u32[]{:S(2)}, u32[]{:S(2)}) collective-permute-start(bf16[3072,128]{1,0:T(8,128)(2,1)} %get-tuple-element.6), channel_id=1, source_target_pairs={{0,2},{1,3},{2,0},{3,1},{4,6},{5,7},{6,4},{7,5},{8,10},{9,11},{10,... | collective-permute-start | bytes 2359304 | tf_op jit(solution)/shard_map/ppermute | solution.py:17
  6.1 1.9 %collective-permute-start.5 = (bf16[3072,128]{1,0:T(8,128)(2,1)}, bf16[3072,128]{1,0:T(8,128)(2,1)}, u32[]{:S(2)}, u32[]{:S(2)}) collective-permute-start(bf16[3072,128]{1,0:T(8,128)(2,1)} %get-tuple-element.6), channel_id=1, source_target_pairs={{0,4},{4,0},{8,12},{12,8},{16,20},{20,16},{24,28},{28,24},{1,5},{5... | collective-permute-start | bytes 2359304 | tf_op jit(solution)/shard_map/ppermute | solution.py:17
  8.0 20.3 %collective-permute-done.3 = s32[48,12]{1,0:T(8,128)S(1)} collective-permute-done((s32[48,12]{1,0:T(8,128)S(1)}, s32[48,12]{1,0:T(8,128)S(1)}, u32[]{:S(2)}, u32[]{:S(2)}) %collective-permute-start.3) | collective-permute-done | bytes 2336 | tf_op jit(solution)/shard_map/ppermute | solution.py:17
  28.3 2.9 %collective-permute-start.1 = (bf16[1536,512]{1,0:T(8,128)(2,1)S(1)}, bf16[1536,512]{1,0:T(8,128)(2,1)S(1)}, u32[]{:S(2)}, u32[]{:S(2)}) collective-permute-start(bf16[1536,512]{1,0:T(8,128)(2,1)S(1)} %copy-done), channel_id=1, source_target_pairs={{0,2},{1,3},{2,0},{3,1},{4,6},{5,7},{6,4},{7,5},{8,10},{9,11},{10,... | collective-permute-start | bytes 4718600 | tf_op jit(solution)/shard_map/ppermute | solution.py:17
  31.1 1.5 collective-permute-start.11
  32.7 8.6 %collective-permute-done.10.refs_1_ = bf16[3072,128]{1,0:T(8,128)(2,1)} collective-permute-done((bf16[3072,128]{1,0:T(8,128)(2,1)}, bf16[3072,128]{1,0:T(8,128)(2,1)}, u32[]{:S(2)}, u32[]{:S(2)}) %collective-permute-start.10) | collective-permute-done | bytes 786464 | tf_op jit(solution)/shard_map/ppermute | solution.py:17
  41.3 2.0 %collective-permute-start.12 = (bf16[3072,128]{1,0:T(8,128)(2,1)}, bf16[3072,128]{1,0:T(8,128)(2,1)S(1)}, u32[]{:S(2)}, u32[]{:S(2)}) collective-permute-start(bf16[3072,128]{1,0:T(8,128)(2,1)} %collective-permute-done.10.refs_1_), channel_id=1, source_target_pairs={{0,4},{4,0},{8,12},{12,8},{16,20},{20,16},{24,28},{28,24},{1,5},{5... | collective-permute-start | bytes 2359304 | tf_op jit(solution)/shard_map/ppermute | solution.py:17
  43.3 8.5 %collective-permute-done.11.refs_2_ = bf16[3072,128]{1,0:T(8,128)(2,1)S(1)} collective-permute-done((bf16[3072,128]{1,0:T(8,128)(2,1)}, bf16[3072,128]{1,0:T(8,128)(2,1)S(1)}, u32[]{:S(2)}, u32[]{:S(2)}) %collective-permute-start.11) | collective-permute-done | bytes 786464 | tf_op jit(solution)/shard_map/ppermute | solution.py:17
  51.8 3.5 %collective-permute-start.13 = (bf16[3072,128]{1,0:T(8,128)(2,1)S(1)}, bf16[3072,128]{1,0:T(8,128)(2,1)S(1)}, u32[]{:S(2)}, u32[]{:S(2)}) collective-permute-start(bf16[3072,128]{1,0:T(8,128)(2,1)S(1)} %collective-permute-done.11.refs_2_), channel_id=1, source_target_pairs={{0,8},{8,16},{12,4},{16,24},{20,12},{28,20},{1,9},{9,17},{13,5},{1... | collective-permute-start | bytes 2359304 | tf_op jit(solution)/shard_map/ppermute | solution.py:17
  55.3 13.3 %collective-permute-done.12.refs_3_ = bf16[3072,128]{1,0:T(8,128)(2,1)S(1)} collective-permute-done((bf16[3072,128]{1,0:T(8,128)(2,1)}, bf16[3072,128]{1,0:T(8,128)(2,1)S(1)}, u32[]{:S(2)}, u32[]{:S(2)}) %collective-permute-start.12) | collective-permute-done | bytes 786464 | tf_op jit(solution)/shard_map/ppermute | solution.py:17
  68.6 3.5 %collective-permute-start.14 = (bf16[3072,128]{1,0:T(8,128)(2,1)S(1)}, bf16[3072,128]{1,0:T(8,128)(2,1)S(1)}, u32[]{:S(2)}, u32[]{:S(2)}) collective-permute-start(bf16[3072,128]{1,0:T(8,128)(2,1)S(1)} %collective-permute-done.12.refs_3_), channel_id=1, source_target_pairs={{0,8},{8,16},{12,4},{16,24},{20,12},{28,20},{1,9},{9,17},{13,5},{1... | collective-permute-start | bytes 2359304 | tf_op jit(solution)/shard_map/ppermute | solution.py:17
  72.2 12.3 %collective-permute-done.6.refs_2_ = bf16[3072,128]{1,0:T(8,128)(2,1)} collective-permute-done((bf16[3072,128]{1,0:T(8,128)(2,1)}, bf16[3072,128]{1,0:T(8,128)(2,1)}, u32[]{:S(2)}, u32[]{:S(2)}) %collective-permute-start.6) | collective-permute-done | bytes 786464 | tf_op jit(solution)/shard_map/ppermute | solution.py:17
  85.0 4.4 %collective-permute-start.7 = (bf16[3072,128]{1,0:T(8,128)(2,1)}, bf16[3072,128]{1,0:T(8,128)(2,1)}, u32[]{:S(2)}, u32[]{:S(2)}) collective-permute-start(bf16[3072,128]{1,0:T(8,128)(2,1)} %collective-permute-done.5.refs_1_), channel_id=1, source_target_pairs={{0,8},{8,16},{12,4},{16,24},{20,12},{28,20},{1,9},{9,17},{13,5},{1... | collective-permute-start | bytes 2359304 | tf_op jit(solution)/shard_map/ppermute | solution.py:17
  89.4 0.9 copy-done.5
  90.4 3.5 %collective-permute-start.8 = (bf16[3072,128]{1,0:T(8,128)(2,1)}, bf16[3072,128]{1,0:T(8,128)(2,1)}, u32[]{:S(2)}, u32[]{:S(2)}) collective-permute-start(bf16[3072,128]{1,0:T(8,128)(2,1)} %collective-permute-done.6.refs_2_), channel_id=1, source_target_pairs={{0,8},{8,16},{12,4},{16,24},{20,12},{28,20},{1,9},{9,17},{13,5},{1... | collective-permute-start | bytes 2359304 | tf_op jit(solution)/shard_map/ppermute | solution.py:17
  94.5 0.7 stack.35.offs_ref
  95.2 0.7 pad_add_fusion.cols_ref
  95.9 21.9 %image.3.refs_5_ = f32[48,128,128]{2,1,0:T(8,128)} custom-call(s32[48,24]{1,0:T(8,128)} %pad_add_fusion.cols_ref, s32[6]{0:T(128)} %stack.35.offs_ref, bf16[48,12,128,128]{3,2,1,0:T(8,128)(2,1)} %own_ref.3, bf16[48,12,128,128]{3,2,1,0:T(8,128)(2,1)} %collective-permute-done.4.other_ref, bf16[3072,128]{1,0:T(8,128)(2,1)} %collective-permute-done.9.refs_0_, ...), custom_call_target="tpu_custom_call" | custom-call | flops 4831838208 | bytes 42467328 | tf_op jit(solution)/shard_map/image/pallas_call | solution.py:79
  117.8 4.9 %collective-permute-done.8.refs_4_ = bf16[3072,128]{1,0:T(8,128)(2,1)} collective-permute-done((bf16[3072,128]{1,0:T(8,128)(2,1)}, bf16[3072,128]{1,0:T(8,128)(2,1)}, u32[]{:S(2)}, u32[]{:S(2)}) %collective-permute-start.8) | collective-permute-done | bytes 786464 | tf_op jit(solution)/shard_map/ppermute | solution.py:17
  122.7 21.9 %image.2.refs_4_ = f32[48,128,128]{2,1,0:T(8,128)} custom-call(s32[48,24]{1,0:T(8,128)} %pad_add_fusion.cols_ref, s32[5]{0:T(128)} %stack.32.offs_ref, bf16[48,12,128,128]{3,2,1,0:T(8,128)(2,1)} %own_ref.3, bf16[48,12,128,128]{3,2,1,0:T(8,128)(2,1)} %collective-permute-done.4.other_ref, bf16[6144,128]{1,0:T(8,128)(2,1)} %refs_0_.2, ...), custom_call_target="tpu_custom_call" | custom-call | flops 4831838208 | bytes 42467328 | tf_op jit(solution)/shard_map/image/pallas_call | solution.py:79
  144.6 8.5 %project.1 = f32[2,512,128]{2,1,0:T(8,128)} custom-call(s32[1]{0:T(128)} %bitcast.me_ref, bf16[1536,512]{1,0:T(8,128)(2,1)} %refs_0_.3, bf16[1536,512]{1,0:T(8,128)(2,1)} %collective-permute-done.refs_1_, bf16[1536,512]{1,0:T(8,128)(2,1)} %copy-done.1, bf16[1536,512]{1,0:T(8,128)(2,1)} %collective-permute-done.2.refs_3_, f32[48,128,128]{2,1,0:T(8,128)} %image.2.refs_4_, ...), custom_call_target="tpu_custom_call" | custom-call | flops 3221225472 | bytes 12582912 | tf_op jit(solution)/shard_map/project/pallas_call | solution.py:144
  153.2 1.1 copy.16
  154.3 20.2 %all_to_all.5 = f32[32,2,16,128]{3,2,1,0:T(8,128)S(1)} all-to-all(f32[32,2,16,128]{3,2,1,0:T(8,128)S(1)} %bitcast.16), channel_id=1, replica_groups=mesh['region'=8,'col'=4] {'region','col'}, dimensions={0} | all-to-all | bytes 1048576 | tf_op jit(solution)/shard_map/all_to_all | solution.py:214
  (34 shorter events, 2.9 us)
Async XLA Ops:
  0.0 95.9 %collective-permute-start.4 = (bf16[48,12,128,128]{3,2,1,0:T(8,128)(2,1)}, bf16[48,12,128,128]{3,2,1,0:T(8,128)(2,1)}, u32[]{:S(2)}, u32[]{:S(2)}) collective-permute-start(bf16[48,12,128,128]{3,2,1,0:T(8,128)(2,1)} %own_ref.3), channel_id=1, source_target_pairs={{0,1},{1,0},{2,3},{3,2},{4,5},{5,4},{6,7},{7,6},{8,9},{9,8},{10,11... | collective-permute-start | bytes 56623112 | tf_op jit(solution)/shard_map/ppermute | solution.py:17
  0.5 5.3 %copy-start.6 = (s32[48,12]{0,1:T(8,128)S(1)}, s32[48,12]{0,1:T(8,128)}, u32[]{:S(2)}) copy-start(s32[48,12]{0,1:T(8,128)} %param.7) | copy-start | bytes 6916
  0.5 27.8 %copy-start = (bf16[1536,512]{1,0:T(8,128)(2,1)S(1)}, bf16[1536,512]{1,0:T(8,128)(2,1)}, u32[]{:S(2)}) copy-start(bf16[1536,512]{1,0:T(8,128)(2,1)} %refs_0_.3) | copy-start | bytes 4718596
  3.2 27.9 %collective-permute-start.9 = (bf16[3072,128]{1,0:T(8,128)(2,1)}, bf16[3072,128]{1,0:T(8,128)(2,1)}, u32[]{:S(2)}, u32[]{:S(2)}) collective-permute-start(bf16[3072,128]{1,0:T(8,128)(2,1)} %get-tuple-element.6), channel_id=1, source_target_pairs={{0,2},{1,3},{2,0},{3,1},{4,6},{5,7},{6,4},{7,5},{8,10},{9,11},{10,... | collective-permute-start | bytes 2359304 | tf_op jit(solution)/shard_map/ppermute | solution.py:17
  5.7 35.6 %collective-permute-start.10 = (bf16[3072,128]{1,0:T(8,128)(2,1)}, bf16[3072,128]{1,0:T(8,128)(2,1)}, u32[]{:S(2)}, u32[]{:S(2)}) collective-permute-start(bf16[3072,128]{1,0:T(8,128)(2,1)} %get-tuple-element.5), channel_id=1, source_target_pairs={{0,2},{1,3},{2,0},{3,1},{4,6},{5,7},{6,4},{7,5},{8,10},{9,11},{10,... | collective-permute-start | bytes 2359304 | tf_op jit(solution)/shard_map/ppermute | solution.py:17
  5.8 22.4 %collective-permute-start.3 = (s32[48,12]{1,0:T(8,128)S(1)}, s32[48,12]{1,0:T(8,128)S(1)}, u32[]{:S(2)}, u32[]{:S(2)}) collective-permute-start(s32[48,12]{1,0:T(8,128)S(1)} %broadcast_subtract_fusion), channel_id=1, source_target_pairs={{0,1},{1,0},{2,3},{3,2},{4,5},{5,4},{6,7},{7,6},{8,9},{9,8},{10,11... | collective-permute-start | bytes 6920 | tf_op jit(solution)/shard_map/ppermute | solution.py:17
  6.1 37.1 %collective-permute-start.5 = (bf16[3072,128]{1,0:T(8,128)(2,1)}, bf16[3072,128]{1,0:T(8,128)(2,1)}, u32[]{:S(2)}, u32[]{:S(2)}) collective-permute-start(bf16[3072,128]{1,0:T(8,128)(2,1)} %get-tuple-element.6), channel_id=1, source_target_pairs={{0,4},{4,0},{8,12},{12,8},{16,20},{20,16},{24,28},{28,24},{1,5},{5... | collective-permute-start | bytes 2359304 | tf_op jit(solution)/shard_map/ppermute | solution.py:17
  28.3 56.2 %collective-permute-start.1 = (bf16[1536,512]{1,0:T(8,128)(2,1)S(1)}, bf16[1536,512]{1,0:T(8,128)(2,1)S(1)}, u32[]{:S(2)}, u32[]{:S(2)}) collective-permute-start(bf16[1536,512]{1,0:T(8,128)(2,1)S(1)} %copy-done), channel_id=1, source_target_pairs={{0,2},{1,3},{2,0},{3,1},{4,6},{5,7},{6,4},{7,5},{8,10},{9,11},{10,... | collective-permute-start | bytes 4718600 | tf_op jit(solution)/shard_map/ppermute | solution.py:17
  31.1 20.6 %collective-permute-start.11 = (bf16[3072,128]{1,0:T(8,128)(2,1)}, bf16[3072,128]{1,0:T(8,128)(2,1)S(1)}, u32[]{:S(2)}, u32[]{:S(2)}) collective-permute-start(bf16[3072,128]{1,0:T(8,128)(2,1)} %collective-permute-done.9.refs_0_), channel_id=1, source_target_pairs={{0,4},{4,0},{8,12},{12,8},{16,20},{20,16},{24,28},{28,24},{1,5},{5... | collective-permute-start | bytes 2359304 | tf_op jit(solution)/shard_map/ppermute | solution.py:17
  41.3 27.4 %collective-permute-start.12 = (bf16[3072,128]{1,0:T(8,128)(2,1)}, bf16[3072,128]{1,0:T(8,128)(2,1)S(1)}, u32[]{:S(2)}, u32[]{:S(2)}) collective-permute-start(bf16[3072,128]{1,0:T(8,128)(2,1)} %collective-permute-done.10.refs_1_), channel_id=1, source_target_pairs={{0,4},{4,0},{8,12},{12,8},{16,20},{20,16},{24,28},{28,24},{1,5},{5... | collective-permute-start | bytes 2359304 | tf_op jit(solution)/shard_map/ppermute | solution.py:17
  43.2 41.2 %collective-permute-start.6 = (bf16[3072,128]{1,0:T(8,128)(2,1)}, bf16[3072,128]{1,0:T(8,128)(2,1)}, u32[]{:S(2)}, u32[]{:S(2)}) collective-permute-start(bf16[3072,128]{1,0:T(8,128)(2,1)} %get-tuple-element.5), channel_id=1, source_target_pairs={{0,4},{4,0},{8,12},{12,8},{16,20},{20,16},{24,28},{28,24},{1,5},{5... | collective-permute-start | bytes 2359304 | tf_op jit(solution)/shard_map/ppermute | solution.py:17
  51.8 32.7 %copy-start.2 = (bf16[3072,128]{1,0:T(8,128)(2,1)}, bf16[3072,128]{1,0:T(8,128)(2,1)S(1)}, u32[]{:S(2)}) copy-start(bf16[3072,128]{1,0:T(8,128)(2,1)S(1)} %collective-permute-done.11.refs_2_) | copy-start | bytes 2359300
  51.8 33.3 %collective-permute-start.13 = (bf16[3072,128]{1,0:T(8,128)(2,1)S(1)}, bf16[3072,128]{1,0:T(8,128)(2,1)S(1)}, u32[]{:S(2)}, u32[]{:S(2)}) collective-permute-start(bf16[3072,128]{1,0:T(8,128)(2,1)S(1)} %collective-permute-done.11.refs_2_), channel_id=1, source_target_pairs={{0,8},{8,16},{12,4},{16,24},{20,12},{28,20},{1,9},{9,17},{13,5},{1... | collective-permute-start | bytes 2359304 | tf_op jit(solution)/shard_map/ppermute | solution.py:17
  68.6 16.4 %copy-start.3 = (bf16[3072,128]{1,0:T(8,128)(2,1)}, bf16[3072,128]{1,0:T(8,128)(2,1)S(1)}, u32[]{:S(2)}) copy-start(bf16[3072,128]{1,0:T(8,128)(2,1)S(1)} %collective-permute-done.12.refs_3_) | copy-start | bytes 2359300
  68.6 20.8 %collective-permute-start.14 = (bf16[3072,128]{1,0:T(8,128)(2,1)S(1)}, bf16[3072,128]{1,0:T(8,128)(2,1)S(1)}, u32[]{:S(2)}, u32[]{:S(2)}) collective-permute-start(bf16[3072,128]{1,0:T(8,128)(2,1)S(1)} %collective-permute-done.12.refs_3_), channel_id=1, source_target_pairs={{0,8},{8,16},{12,4},{16,24},{20,12},{28,20},{1,9},{9,17},{13,5},{1... | collective-permute-start | bytes 2359304 | tf_op jit(solution)/shard_map/ppermute | solution.py:17
  84.5 60.2 %collective-permute-start = (bf16[1536,512]{1,0:T(8,128)(2,1)S(1)}, bf16[1536,512]{1,0:T(8,128)(2,1)}, u32[]{:S(2)}, u32[]{:S(2)}) collective-permute-start(bf16[1536,512]{1,0:T(8,128)(2,1)S(1)} %copy-done), channel_id=1, source_target_pairs={{0,1},{1,0},{2,3},{3,2},{4,5},{5,4},{6,7},{7,6},{8,9},{9,8},{10,11... | collective-permute-start | bytes 4718600 | tf_op jit(solution)/shard_map/ppermute | solution.py:17
  84.5 33.3 %copy-start.1 = (bf16[1536,512]{1,0:T(8,128)(2,1)}, bf16[1536,512]{1,0:T(8,128)(2,1)S(1)}, u32[]{:S(2)}) copy-start(bf16[1536,512]{1,0:T(8,128)(2,1)S(1)} %collective-permute-done.1.refs_2_) | copy-start | bytes 4718596
  84.5 60.1 %collective-permute-start.2 = (bf16[1536,512]{1,0:T(8,128)(2,1)S(1)}, bf16[1536,512]{1,0:T(8,128)(2,1)}, u32[]{:S(2)}, u32[]{:S(2)}) collective-permute-start(bf16[1536,512]{1,0:T(8,128)(2,1)S(1)} %collective-permute-done.1.refs_2_), channel_id=1, source_target_pairs={{0,1},{1,0},{2,3},{3,2},{4,5},{5,4},{6,7},{7,6},{8,9},{9,8},{10,11... | collective-permute-start | bytes 4718600 | tf_op jit(solution)/shard_map/ppermute | solution.py:17
  85.0 4.4 %copy-start.4 = (bf16[3072,128]{1,0:T(8,128)(2,1)}, bf16[3072,128]{1,0:T(8,128)(2,1)S(1)}, u32[]{:S(2)}) copy-start(bf16[3072,128]{1,0:T(8,128)(2,1)S(1)} %collective-permute-done.13.refs_4_) | copy-start | bytes 2359300
  85.0 32.7 %collective-permute-start.7 = (bf16[3072,128]{1,0:T(8,128)(2,1)}, bf16[3072,128]{1,0:T(8,128)(2,1)}, u32[]{:S(2)}, u32[]{:S(2)}) collective-permute-start(bf16[3072,128]{1,0:T(8,128)(2,1)} %collective-permute-done.5.refs_1_), channel_id=1, source_target_pairs={{0,8},{8,16},{12,4},{16,24},{20,12},{28,20},{1,9},{9,17},{13,5},{1... | collective-permute-start | bytes 2359304 | tf_op jit(solution)/shard_map/ppermute | solution.py:17
  89.4 0.9 copy-start.5
  90.4 32.3 %collective-permute-start.8 = (bf16[3072,128]{1,0:T(8,128)(2,1)}, bf16[3072,128]{1,0:T(8,128)(2,1)}, u32[]{:S(2)}, u32[]{:S(2)}) collective-permute-start(bf16[3072,128]{1,0:T(8,128)(2,1)} %collective-permute-done.6.refs_2_), channel_id=1, source_target_pairs={{0,8},{8,16},{12,4},{16,24},{20,12},{28,20},{1,9},{9,17},{13,5},{1... | collective-permute-start | bytes 2359304 | tf_op jit(solution)/shard_map/ppermute | solution.py:17

commit v2 on v1

v2 whole, which is shorter than its diff:
```python
import functools

import jax
import jax.numpy as jnp
from jax import lax
from jax.experimental import pallas as pl
from jax.experimental.pallas import tpu as pltpu
from jax.sharding import PartitionSpec as P

EVERY = ("region", "col")
VMEM = 60 * 2**20
PAIR = 2
LANES = 8
DEPTH = 3
V_BITS, BLOCK_BITS = 8, 10


def moved(array, axis, target):
    count = lax.axis_size(axis)
    pairs = [(i, target(i)) for i in range(count)]
    return lax.ppermute(array, axis, [(i, j) for i, j in pairs if 0 <= j < count])


def to_core(array):
    return moved(array, "col", lambda c: c ^ 1)


def to_side(array):
    return moved(array, "col", lambda c: c ^ 2)


def to_near(array):
    return moved(array, "region", lambda r: r ^ 1)


def to_far(array):
    return moved(array, "region", lambda r: r + 1 if r % 2 else r - 1)


def onward(array):
    return moved(array, "region", lambda r: r - 2 if r % 2 else r + 2)


def after(array, *others):
    return lax.optimization_barrier((array, *others))[0]


def largest_divisor(length, limit):
    return max(d for d in range(1, limit + 1) if length % d == 0)


def anywhere(count):
    return [pl.BlockSpec(memory_space=pl.ANY)] * count


def image_kernel(group, parts, cols_ref, offs_ref, own_ref, other_ref, *refs):
    pieces = len(parts)
    v_refs, (out_ref, v_all, sems) = refs[:pieces], refs[pieces:]
    step = pl.program_id(0)
    slots, block = own_ref.shape[1], own_ref.shape[2]

    @pl.when(step == 0)
    def _():
        v_all[...] = jnp.zeros_like(v_all)
        copies = []
        for p in range(pieces):
            rows = v_refs[p].shape[0]
            start = pl.multiple_of(offs_ref[p] * block, block)
            target = v_all.at[pl.ds(start, rows), pl.ds(parts[p] * block, block)]
            copies.append(pltpu.make_async_copy(v_refs[p], target, sems.at[p]))
        for copy in copies:
            copy.start()
        for copy in copies:
            copy.wait()

    for g in range(group):
        row = step * group + g
        left, right = [], []
        for a_ref, base in ((own_ref, 0), (other_ref, slots)):
            for s in range(slots):
                start = pl.multiple_of(cols_ref[row, base + s] * block, block)
                left.append(a_ref[g, s])
                right.append(v_all[pl.ds(start, block), :])
        product = jnp.dot(
            jnp.concatenate(left, axis=1),
            jnp.concatenate(right, axis=0),
            preferred_element_type=jnp.float32,
        )
        for part in range(2):
            out_ref[part, g] = product[:, part * block : (part + 1) * block]


def image_of(cols, offs, own, other, v_pieces, parts):
    rows, slots, block = own.shape[:3]
    group = largest_divisor(rows, 8)
    a_spec = pl.BlockSpec((group, slots, block, block), lambda i, c, o: (i, 0, 0, 0))
    return pl.pallas_call(
        functools.partial(image_kernel, group, parts),
        out_shape=jax.ShapeDtypeStruct((2, rows, block, block), jnp.float32),
        grid_spec=pltpu.PrefetchScalarGridSpec(
            num_scalar_prefetch=2,
            grid=(rows // group,),
            in_specs=[a_spec, a_spec] + anywhere(len(v_pieces)),
            out_specs=pl.BlockSpec((2, group, block, block), lambda i, c, o: (0, i, 0, 0)),
            scratch_shapes=[
                pltpu.VMEM((3 * rows * block, 2 * block), jnp.bfloat16),
                pltpu.SemaphoreType.DMA((len(v_pieces),)),
            ],
        ),
        compiler_params=pltpu.CompilerParams(vmem_limit_bytes=VMEM),
        cost_estimate=pl.CostEstimate(
            flops=8 * rows * slots * block**3,
            bytes_accessed=4 * rows * slots * block * block,
            transcendentals=0,
        ),
        name="image",
    )(cols, offs, own, other, *v_pieces)


def class_list(members, places, rows, capacity):
    sources, targets, slots = members.shape
    held = members.astype(jnp.int32)
    tasks = (held.sum(axis=2) + PAIR - 1) // PAIR
    ends = jnp.cumsum(tasks, axis=1)
    rank = jnp.cumsum(held, axis=2) - held
    at = jnp.where(members, (ends - tasks)[:, :, None] * PAIR + rank, -1)
    target = jnp.arange(targets, dtype=jnp.int32)[:, None]
    block_id = (target % rows) * slots + jnp.arange(slots, dtype=jnp.int32)[None, :]
    code = ((target << (BLOCK_BITS + V_BITS)) + (block_id << V_BITS))[None] + places
    at = at.reshape(sources, 1, targets * slots)
    code = code.reshape(sources, 1, targets * slots)
    line = jnp.arange(capacity * PAIR, dtype=jnp.int32)[None, :, None]
    codes = jnp.where(at == line, code, 0).sum(axis=2)
    most = ends[:, -1].max()
    steps = (most + LANES - 1) // LANES
    return codes.reshape(-1), jnp.reshape(steps, (1,)).astype(jnp.int32)


def capacity_of(rows, slots, parts):
    tasks = (rows * slots + rows * parts * (PAIR - 1)) // PAIR
    return -(-tasks // LANES) * LANES


def add_listed(codes_ref, steps_ref, a_refs, v_all, blocks, sems, total, first_row):
    block = blocks.shape[-1]
    per_source = LANES * PAIR
    length = codes_ref.shape[0] // len(a_refs)
    steps = steps_ref[0]

    def fetch(step):
        slot = lax.rem(step, DEPTH)
        for s, a_ref in enumerate(a_refs):
            for n in range(per_source):
                code = codes_ref[s * length + step * per_source + n]
                block_id = (code >> V_BITS) & ((1 << BLOCK_BITS) - 1)
                pltpu.make_async_copy(
                    a_ref.at[block_id], blocks.at[slot, s * per_source + n], sems.at[slot]
                ).start()

    for ahead in range(DEPTH - 1):
        @pl.when(ahead < steps)
        def _():
            fetch(ahead)

    def run():
        def one(step, carry):
            slot = lax.rem(step, DEPTH)

            @pl.when(step + DEPTH - 1 < steps)
            def _():
                fetch(step + DEPTH - 1)

            pltpu.make_async_copy(blocks.at[slot], blocks.at[slot], sems.at[slot]).wait()
            products = []
            for s in range(len(a_refs)):
                for n in range(LANES):
                    left, right = [], []
                    for g in range(PAIR):
                        at = n * PAIR + g
                        code = codes_ref[s * length + step * per_source + at]
                        if g == 0:
                            row = jnp.maximum((code >> (BLOCK_BITS + V_BITS)) - first_row, 0)
                        start = pl.multiple_of((code & ((1 << V_BITS) - 1)) * block, block)
                        left.append(blocks[slot, s * per_source + at])
                        right.append(v_all[pl.ds(start, block), :])
                    product = jnp.dot(
                        jnp.concatenate(left, axis=1),
                        jnp.concatenate(right, axis=0),
                        preferred_element_type=jnp.float32,
                    )
                    products.append((row, product))
            for row, product in products:
                total[row] += product
            return carry

        lax.fori_loop(0, steps, one, 0)

    return run


def v_copies(v_refs, v_all, sems, block):
    copies, at = [], block
    for p, ref in enumerate(v_refs):
        rows = ref.shape[0]
        copies.append(pltpu.make_async_copy(ref, v_all.at[pl.ds(at, rows)], sems.at[p]))
        at += rows
    return copies


def more_kernel(pieces, codes_ref, steps_ref, own_ref, other_ref, image_ref, *refs):
    v_refs, (out_ref, v_all, blocks, a_sems, sems) = refs[:pieces], refs[pieces:]
    block = v_all.shape[1]
    copies = v_copies(v_refs, v_all, sems, block)
    copies.append(pltpu.make_async_copy(image_ref, out_ref, sems.at[pieces]))
    for copy in copies:
        copy.start()
    run = add_listed(codes_ref, steps_ref, (own_ref, other_ref), v_all, blocks, a_sems, out_ref, 0)
    v_all[pl.ds(0, block), :] = jnp.zeros((block, block), v_all.dtype)
    for copy in copies:
        copy.wait()
    run()


def list_scratch(v_pieces, block):
    v_rows = block + sum(v.shape[0] for v in v_pieces)
    return [
        pltpu.VMEM((v_rows, block), jnp.bfloat16),
        pltpu.VMEM((DEPTH, 2 * LANES * PAIR, block, block), jnp.bfloat16),
        pltpu.SemaphoreType.DMA((DEPTH,)),
    ]


def more_image(codes, steps, own, other, image, v_pieces):
    targets, block, _ = image.shape
    return pl.pallas_call(
        functools.partial(more_kernel, len(v_pieces)),
        out_shape=jax.ShapeDtypeStruct(image.shape, jnp.float32),
        grid_spec=pltpu.PrefetchScalarGridSpec(
            num_scalar_prefetch=2,
            grid=(1,),
            in_specs=anywhere(3 + len(v_pieces)),
            out_specs=pl.BlockSpec(image.shape, lambda i, c, s: (0, 0, 0)),
            scratch_shapes=list_scratch(v_pieces, block)
            + [pltpu.SemaphoreType.DMA((len(v_pieces) + 1,))],
        ),
        compiler_params=pltpu.CompilerParams(vmem_limit_bytes=VMEM),
        cost_estimate=pl.CostEstimate(
            flops=targets * 8 * block**3, bytes_accessed=2**25, transcendentals=0
        ),
        name="more_image",
    )(codes, steps, own, other, image, *v_pieces)


def split(image):
    upper = image.astype(jnp.bfloat16)
    return upper, (image - upper.astype(jnp.float32)).astype(jnp.bfloat16)


def project_kernel(pieces, codes_ref, steps_ref, me_ref, own_ref, other_ref, image_ref, *refs):
    v_refs, w_refs, refs = refs[:pieces], refs[pieces : pieces + 4], refs[pieces + 4 :]
    out_ref, v_all, blocks, a_sems, fresh, image, w_all, sems = refs
    block = v_all.shape[1]
    copies = v_copies(v_refs, v_all, sems, block)
    for copy in copies:
        copy.start()
    run = add_listed(codes_ref, steps_ref, (own_ref, other_ref), v_all, blocks, a_sems, fresh, 0)
    later = [
        pltpu.make_async_copy(w_refs[q], w_all.at[q], sems.at[pieces + q]) for q in range(4)
    ]
    later.append(pltpu.make_async_copy(image_ref, image, sems.at[pieces + 4]))
    for copy in later:
        copy.start()
    v_all[pl.ds(0, block), :] = jnp.zeros((block, block), v_all.dtype)
    fresh[...] = jnp.zeros_like(fresh)
    for copy in copies:
        copy.wait()
    run()
    for copy in later:
        copy.wait()
    rows = fresh.shape[0]
    length = rows // 4
    out_ref[...] = jnp.zeros_like(out_ref)
    for q in range(4):
        first = (me_ref[0] ^ q) * length
        parts = [
            image[pl.ds(first, length)],
            image[pl.ds(rows + first, length)] + fresh[pl.ds(first, length)],
        ]
        here = jnp.concatenate([p.reshape(length * block, block) for p in parts], axis=1)
        for term in split(here):
            out_ref[...] += jnp.dot(w_all[q], term, preferred_element_type=jnp.float32)


def projected(codes, steps, me, own, other, image, v_pieces, w_pieces):
    targets, block, _ = image.shape
    basis, length = w_pieces[0].shape
    return pl.pallas_call(
        functools.partial(project_kernel, len(v_pieces)),
        out_shape=jax.ShapeDtypeStruct((basis, 2 * block), jnp.float32),
        grid_spec=pltpu.PrefetchScalarGridSpec(
            num_scalar_prefetch=3,
            grid=(1,),
            in_specs=anywhere(7 + len(v_pieces)),
            out_specs=pl.BlockSpec((basis, 2 * block), lambda i, c, s, m: (0, 0)),
            scratch_shapes=list_scratch(v_pieces, block)
            + [
                pltpu.VMEM((targets // 2, block, block), jnp.float32),
                pltpu.VMEM(image.shape, jnp.float32),
                pltpu.VMEM((4, basis, length), jnp.bfloat16),
                pltpu.SemaphoreType.DMA((len(v_pieces) + 5,)),
            ],
        ),
        compiler_params=pltpu.CompilerParams(vmem_limit_bytes=VMEM),
        cost_estimate=pl.CostEstimate(
            flops=4 * targets * basis * block**2, bytes_accessed=2**25, transcendentals=0
        ),
        name="projected",
    )(codes, steps, me, own, other, image, *v_pieces, *w_pieces)


def last_kernel(pieces, codes_ref, steps_ref, me_ref, own_ref, other_ref, before_ref, *refs):
    v_refs, w_refs, refs = refs[:pieces], refs[pieces : pieces + 4], refs[pieces + 4 :]
    out_ref, v_all, blocks, a_sems, fresh, w_all, sems = refs
    block = v_all.shape[1]
    rows = fresh.shape[0]
    col, side = me_ref[0], me_ref[1]
    copies = v_copies(v_refs, v_all, sems, block)
    for copy in copies:
        copy.start()
    run = add_listed(
        codes_ref, steps_ref, (own_ref, other_ref), v_all, blocks, a_sems, fresh, side * rows
    )
    later = [
        pltpu.make_async_copy(w_refs[q], w_all.at[(col ^ q) & 1], sems.at[pieces + (q & 1)])
        for q in range(4)
    ]
    for q in range(4):
        pl.when((col ^ q) >> 1 == side)(later[q].start)
    v_all[pl.ds(0, block), :] = jnp.zeros((block, block), v_all.dtype)
    fresh[...] = jnp.zeros_like(fresh)
    for copy in copies:
        copy.wait()
    run()
    for q in range(4):
        pl.when((col ^ q) >> 1 == side)(later[q].wait)
    tiles, _, tile, _ = out_ref.shape
    basis, length = w_all.shape[1:]
    total = before_ref[:, block:]
    for q in range(2):
        here = fresh[q * (rows // 2) : (q + 1) * (rows // 2)].reshape(length, block)
        for term in split(here):
            total += jnp.dot(w_all[q], term, preferred_element_type=jnp.float32)
    mine = col >> 1
    out_ref[:, mine] = before_ref[:, :block].reshape(tiles, tile, block)
    out_ref[:, 1 - mine] = total.reshape(tiles, tile, block)


def finished(codes, steps, me, own, other, before, v_pieces, w_pieces, devices):
    block = own.shape[-1]
    basis, length = w_pieces[0].shape
    shape = (devices, 2, basis // devices, block)
    whole = pl.BlockSpec(before.shape, lambda i, c, s, m: (0, 0))
    return pl.pallas_call(
        functools.partial(last_kernel, len(v_pieces)),
        out_shape=jax.ShapeDtypeStruct(shape, jnp.float32),
        grid_spec=pltpu.PrefetchScalarGridSpec(
            num_scalar_prefetch=3,
            grid=(1,),
            in_specs=anywhere(2) + [whole] + anywhere(4 + len(v_pieces)),
            out_specs=pl.BlockSpec(shape, lambda i, c, s, m: (0, 0, 0, 0)),
            scratch_shapes=list_scratch(v_pieces, block)
            + [
                pltpu.VMEM((2 * length // block, block, block), jnp.float32),
                pltpu.VMEM((2, basis, length), jnp.bfloat16),
                pltpu.SemaphoreType.DMA((len(v_pieces) + 2,)),
            ],
        ),
        compiler_params=pltpu.CompilerParams(vmem_limit_bytes=VMEM),
        cost_estimate=pl.CostEstimate(
            flops=8 * basis * length * block, bytes_accessed=2**23, transcendentals=0
        ),
        name="finished",
    )(codes, steps, me, own, other, before, *v_pieces, *w_pieces)


def shards(basis_v, basis_w, couplings, coupling_cols):
    rows, slots, block = couplings.shape[:3]
    regions, columns = lax.axis_size("region"), lax.axis_size("col")
    region, col = lax.axis_index("region"), lax.axis_index("col")
    odd = region % 2
    half = rows // 2
    quarter = half // 2

    def cut(array, which):
        start = jnp.where(odd == 1, 1 - which, which) * (half * block)
        return lax.dynamic_slice_in_dim(array, start, half * block, axis=0)

    here = coupling_cols - (region * rows - rows)
    there = to_core(here)
    own_a, own_b = cut(basis_v, 0), cut(basis_v, 1)
    side_a = to_side(own_a)
    near_a = to_near(own_a)
    side_b = to_side(own_b)
    near_b = to_near(own_b)
    other = to_core(after(couplings, there))
    far_a = onward(near_a)
    near_side_a = to_near(side_a)
    far_b = onward(near_b)
    near_side_b = to_near(side_b)
    w_own = basis_w.T
    w_core = to_core(after(w_own, other))
    w_side = to_side(after(w_own, side_b))
    far_side_a = onward(near_side_a)
    w_cross = to_core(w_side)
    far_side_b = [
        onward(near_side_b[: quarter * block]),
        to_far(after(side_b, near_side_a)[quarter * block :]),
    ]
    w_pieces = [w_own, w_core, w_side, w_cross]

    cols = jnp.concatenate([here, there], axis=1)
    near_base = jnp.where(odd == 1, 0, 2 * rows)
    far_base = 2 * rows - near_base
    near_at = [near_base + (1 - odd) * half, near_base + odd * half]
    own_at = [rows + odd * half, rows + (1 - odd) * half]
    offs = jnp.stack([jnp.int32(rows)] + near_at + own_at).astype(jnp.int32)

    both = jnp.stack([here, there])
    in_near = both // rows == near_base // rows
    in_far = both // rows == far_base // rows
    upper = both % rows >= half
    is_a = upper == (odd == 0)
    within = both % half
    late = jnp.where(is_a, within, half + within)
    second = class_list(
        jnp.concatenate([in_far, in_near & is_a], axis=1),
        jnp.concatenate([1 + late, 1 + rows + within], axis=1),
        rows,
        capacity_of(rows, slots, 2),
    )
    third = class_list(
        (in_near & ~is_a) | (in_far & is_a),
        jnp.where(in_near, 1 + within, 1 + half + within),
        rows,
        capacity_of(rows, slots, 1),
    )
    fourth = class_list(in_far & ~is_a, 1 + within, rows, capacity_of(rows, slots, 1))

    image = image_of(
        cols, offs, couplings, other, [basis_v, near_a, near_b, side_a, side_b], (0, 0, 0, 1, 1)
    )
    image = image.reshape(2 * rows, block, block)
    own_list = couplings.reshape(rows * slots, block, block)
    other_list = other.reshape(rows * slots, block, block)
    image = more_image(*second, own_list, other_list, image, [far_a, far_b, near_side_a])
    me = jnp.stack([col, odd]).astype(jnp.int32)
    before = projected(
        *third, me, own_list, other_list, image, [near_side_b, far_side_a], w_pieces
    )
    devices = regions * columns
    sent = finished(
        *fourth, me, own_list, other_list, before, far_side_b, w_pieces, devices
    )
    received = lax.all_to_all(sent, EVERY, 0, 0, tiled=True)
    tile = sent.shape[2]
    summed = received.reshape(regions, columns // 2, 2, 2, tile, block).sum(axis=(0, 1))
    return summed.transpose(2, 1, 0, 3).reshape(tile, columns * block)


def solution(mesh):
    in_specs = (
        P("region", "col"),
        P(("region", "col"), None),
        P("region", "col", None, None),
        P("region", "col"),
    )
    out_specs = P(("region", "col"), None)
    return jax.shard_map(shards, mesh=mesh, in_specs=in_specs, out_specs=out_specs, check_vma=False)
```

time: 176 us -> 207 us (1.18); the launches traced: 175 us -> 204 us
  blocking collectives: 20.2 us -> 31.3 us
  local copies, waits for them, and re-layouts: 6.84 us -> 16.9 us
  other arithmetic: 0.73 us -> 6.5 us
  Pallas kernels: 52.3 us -> 57.3 us
  starting transfers between devices: 27 us -> 24.3 us
  waiting for transfers between devices: 67.9 us -> 65.3 us
  between operations: 0.12 us -> 2.38 us
    all_to_all x1, blocking collectives: 20.2 us -> 31.3 us  [shards(): received = lax.all_to_all(sent, EVERY, 0, 0, tiled=True)]
    pallas_call x3 -> x4, Pallas kernels: 52.3 us -> 57.3 us  [the longest x1 22.8 us: image_of(): pl.pallas_call(functools.partial(image_kernel, group, parts), out_shape=j...]
    slice x0 -> x2, local copies, waits for them, and re-layouts: none -> 3.54 us  [the longest x1 1.78 us: shards(): after(side_b, near_side_a)[quarter * block:]]
    unnamed x15 -> x12, local copies, waits for them, and re-layouts: 1.04 us -> 4.28 us
    ppermute x15 -> x16, starting transfers between devices: 27 us -> 24.3 us  [moved(): lax.ppermute(array, axis, [(i, j) for i, j in pairs if 0 <= j < count])]
    ppermute x15 -> x16, waiting for transfers between devices: 67.9 us -> 65.3 us  [moved(): lax.ppermute(array, axis, [(i, j) for i, j in pairs if 0 <= j < count])]
    reduce_max x0 -> x3, other arithmetic: none -> 2.18 us  [class_list(): most = ends[:, -1].max()]
  transfers between devices with their start and end apart: 15 -> 16, of which waited for: 6 -> 4; matrix products, arithmetic and copies ran while one was open for 3% -> 10% of each run, Pallas kernels for 25% -> 25%
where the time goes in v2:
time: 207 us; the launch traced here: 204 us
  waiting for transfers between devices  65.3 us (32%)
  Pallas kernels  57.3 us (28%)
  blocking collectives  31.3 us (15%)
  starting transfers between devices  24.3 us (12%)
  local copies, waits for them, and re-layouts  16.9 us (8%)
  other arithmetic  6.5 us (3%)
  between operations  2.38 us (1%)
    ppermute x16, waiting for transfers between devices, moved(): lax.ppermute(array, axis, [(i, j) for i, j in pairs if 0 <= j < count])  65.3 us
    all_to_all x1, blocking collectives, shards(): received = lax.all_to_all(sent, EVERY, 0, 0, tiled=True)  31.3 us
    ppermute x16, starting transfers between devices, moved(): lax.ppermute(array, axis, [(i, j) for i, j in pairs if 0 <= j < count])  24.3 us
    pallas_call x1, Pallas kernels, image_of(): pl.pallas_call(functools.partial(image_kernel, group, parts), out_shape=j...  22.8 us
    pallas_call x1, Pallas kernels, projected(): pl.pallas_call(functools.partial(project_kernel, len(v_pieces)), out_shap...  17.1 us
    pallas_call x1, Pallas kernels, more_image(): pl.pallas_call(functools.partial(more_kernel, len(v_pieces)), out_shape=j...  10.8 us
    pallas_call x1, Pallas kernels, finished(): pl.pallas_call(functools.partial(last_kernel, len(v_pieces)), out_shape=j...  6.57 us
    unnamed x12, local copies, waits for them, and re-layouts  4.28 us
  transfers between devices with their start and end apart: 16, of which 4 were waited for; matrix products, arithmetic and copies ran while one was open for 10% of the time, Pallas kernels for 25%

profile of v2, /device:TPU:0, one launch (start us, length us, event | category | flops | bytes accessed | tf_op | source)
XLA Modules:
  0.0 204.0 jit_solution(847823120217163998)
XLA Ops:
  0.0 0.8 copy.32
  1.3 0.8 collective-permute-done
  2.5 2.6 %constant_dynamic-slice_fusion = (bf16[3072,128]{1,0:T(8,128)(2,1)}, bf16[3072,128]{1,0:T(8,128)(2,1)}) fusion(bf16[6144,128]{1,0:T(8,128)(2,1)} %refs_0_.1, s32[]{:T(128)S(6)} %select_n.203, s32[]{:T(128)S(6)} %select_n.201), kind=kLoop, calls=%fused_computation.70 | loop fusion | bytes 3145736 | tf_op jit(solution)/shard_map/dynamic_slice | solution.py:396
  5.1 2.7 %collective-permute-start.2 = (bf16[3072,128]{1,0:T(8,128)(2,1)}, bf16[3072,128]{1,0:T(8,128)(2,1)}, u32[]{:S(2)}, u32[]{:S(2)}) collective-permute-start(bf16[3072,128]{1,0:T(8,128)(2,1)} %get-tuple-element.24), channel_id=1, source_target_pairs={{0,4},{4,0},{8,12},{12,8},{16,20},{20,16},{24,28},{28,24},{1,5},{5... | collective-permute-start | bytes 2359304 | tf_op jit(solution)/shard_map/ppermute | solution.py:21
  7.8 1.5 collective-permute-start.4
  11.1 1.7 copy.40
  12.8 0.8 stack.52.offs_ref
  16.6 27.8 %collective-permute-done.5.refs_4_ = bf16[3072,128]{1,0:T(8,128)(2,1)S(1)} collective-permute-done((bf16[3072,128]{1,0:T(8,128)(2,1)}, bf16[3072,128]{1,0:T(8,128)(2,1)S(1)}, u32[]{:S(2)}, u32[]{:S(2)}) %collective-permute-start.5) | collective-permute-done | bytes 786464 | tf_op jit(solution)/shard_map/ppermute | solution.py:21
  44.4 0.9 copy-done.2
  45.3 1.5 collective-permute-start.12
  49.6 31.2 %collective-permute-done.12.refs_4_ = bf16[512,1536]{1,0:T(8,128)(2,1)S(1)} collective-permute-done((bf16[512,1536]{1,0:T(8,128)(2,1)S(1)}, bf16[512,1536]{1,0:T(8,128)(2,1)S(1)}, u32[]{:S(2)}, u32[]{:S(2)}) %collective-permute-start.12) | collective-permute-done | bytes 1572896 | tf_op jit(solution)/shard_map/ppermute | solution.py:21
  87.1 0.8 select_reduce_fusion
  89.2 4.3 %collective-permute-start.6 = (bf16[3072,128]{1,0:T(8,128)(2,1)}, bf16[3072,128]{1,0:T(8,128)(2,1)}, u32[]{:S(2)}, u32[]{:S(2)}) collective-permute-start(bf16[3072,128]{1,0:T(8,128)(2,1)} %collective-permute-done.2.refs_1_), channel_id=1, source_target_pairs={{0,8},{8,16},{12,4},{16,24},{20,12},{28,20},{1,9},{9,17},{13,5},{1... | collective-permute-start | bytes 2359304 | tf_op jit(solution)/shard_map/ppermute | solution.py:21
  93.5 5.4 %collective-permute-done.8.refs_2_ = bf16[3072,128]{1,0:T(8,128)(2,1)} collective-permute-done((bf16[3072,128]{1,0:T(8,128)(2,1)}, bf16[3072,128]{1,0:T(8,128)(2,1)}, u32[]{:S(2)}, u32[]{:S(2)}) %collective-permute-start.8) | collective-permute-done | bytes 786464 | tf_op jit(solution)/shard_map/ppermute | solution.py:21
  98.9 4.4 %collective-permute-start.7 = (bf16[3072,128]{1,0:T(8,128)(2,1)}, bf16[3072,128]{1,0:T(8,128)(2,1)}, u32[]{:S(2)}, u32[]{:S(2)}) collective-permute-start(bf16[3072,128]{1,0:T(8,128)(2,1)} %collective-permute-done.3.refs_2_), channel_id=1, source_target_pairs={{0,8},{8,16},{12,4},{16,24},{20,12},{28,20},{1,9},{9,17},{13,5},{1... | collective-permute-start | bytes 2359304 | tf_op jit(solution)/shard_map/ppermute | solution.py:21
  103.3 1.8 slice.19
  105.0 3.5 %collective-permute-start.10 = (bf16[3072,128]{1,0:T(8,128)(2,1)}, bf16[3072,128]{1,0:T(8,128)(2,1)}, u32[]{:S(2)}, u32[]{:S(2)}) collective-permute-start(bf16[3072,128]{1,0:T(8,128)(2,1)} %collective-permute-done.8.refs_2_), channel_id=1, source_target_pairs={{0,8},{8,16},{12,4},{16,24},{20,12},{28,20},{1,9},{9,17},{13,5},{1... | collective-permute-start | bytes 2359304 | tf_op jit(solution)/shard_map/ppermute | solution.py:21
  108.5 1.8 slice.20
  110.3 22.8 %image.1 = f32[2,48,128,128]{3,2,1,0:T(8,128)} custom-call(s32[48,24]{1,0:T(8,128)} %pad_add_fusion.cols_ref, s32[5]{0:T(128)} %stack.52.offs_ref, bf16[48,12,128,128]{3,2,1,0:T(8,128)(2,1)} %own_ref.1, bf16[48,12,128,128]{3,2,1,0:T(8,128)(2,1)} %collective-permute-done.1.other_ref, bf16[6144,128]{1,0:T(8,128)(2,1)} %refs_0_.1, ...), custom_call_target="tpu_custom_call" | custom-call | flops 9663676416 | bytes 37748736 | tf_op jit(solution)/shard_map/image/pallas_call | solution.py:97
  133.1 2.6 %collective-permute-start.14 = (bf16[1536,128]{1,0:T(8,128)(2,1)}, bf16[1536,128]{1,0:T(8,128)(2,1)S(1)}, u32[]{:S(2)}, u32[]{:S(2)}) collective-permute-start(bf16[1536,128]{1,0:T(8,128)(2,1)} %slice.20), channel_id=1, source_target_pairs={{0,8},{8,16},{12,4},{16,24},{20,12},{28,20},{1,9},{9,17},{13,5},{1... | collective-permute-start | bytes 1179656 | tf_op jit(solution)/shard_map/ppermute | solution.py:21
  136.5 10.8 %more_image.1.image_ref = f32[96,128,128]{2,1,0:T(8,128)} custom-call(s32[1344]{0:T(1024)} %reshape.441.codes_ref, s32[1]{0:T(128)} %bitcast.8.steps_ref, bf16[576,128,128]{2,1,0:T(8,128)(2,1)} %bitcast.27, bf16[576,128,128]{2,1,0:T(8,128)(2,1)} %bitcast.6.other_ref, f32[96,128,128]{2,1,0:T(8,128)} %bitcast.30, ...), custom_call_target="tpu_custom_call" | custom-call | flops 1610612736 | bytes 33554432 | tf_op jit(solution)/shard_map/more_image/pallas_call | solution.py:235
  147.3 17.1 %projected.1.before_ref = f32[512,256]{1,0:T(8,128)} custom-call(s32[1248]{0:T(1024)} %reshape.439.codes_ref, s32[1]{0:T(128)} %bitcast.7.steps_ref, s32[2]{0:T(128)} %pad_add_fusion.5.me_ref, bf16[576,128,128]{2,1,0:T(8,128)(2,1)} %bitcast.28, bf16[576,128,128]{2,1,0:T(8,128)(2,1)} %bitcast.6.other_ref, f32[96,128,128]{2,1,0:T(8,128)} %more_image.1.image_ref, ...), custom_call_target="tpu_custom_call" | custom-call | flops 3221225472 | bytes 33554432 | tf_op jit(solution)/shard_map/projected/pallas_call | solution.py:297
  165.4 6.6 %finished.1 = f32[32,2,16,128]{3,2,1,0:T(8,128)} custom-call(s32[1248]{0:T(1024)} %reshape.435.codes_ref, s32[1]{0:T(128)} %bitcast.2.steps_ref, s32[2]{0:T(128)} %pad_add_fusion.5.me_ref, bf16[576,128,128]{2,1,0:T(8,128)(2,1)} %bitcast.29, bf16[576,128,128]{2,1,0:T(8,128)(2,1)} %bitcast.6.other_ref, f32[512,256]{1,0:T(8,128)} %projected.1.before_ref, ...), custom_call_target="tpu_custom_call" | custom-call | flops 805306368 | bytes 8388608 | tf_op jit(solution)/shard_map/finished/pallas_call | solution.py:363
  172.0 31.3 %all_to_all.5 = f32[32,2,16,128]{3,2,1,0:T(8,128)S(1)} all-to-all(f32[32,2,16,128]{3,2,1,0:T(8,128)} %finished.1), channel_id=1, replica_groups=mesh['region'=8,'col'=4] {'region','col'}, dimensions={0} | all-to-all | bytes 1048576 | tf_op jit(solution)/shard_map/all_to_all | solution.py:464
  (103 shorter events, 16.1 us)
Async XLA Ops:
  0.8 1.4 collective-permute-start
  2.2 83.3 %collective-permute-start.1 = (bf16[48,12,128,128]{3,2,1,0:T(8,128)(2,1)}, bf16[48,12,128,128]{3,2,1,0:T(8,128)(2,1)}, u32[]{:S(2)}, u32[]{:S(2)}) collective-permute-start(bf16[48,12,128,128]{3,2,1,0:T(8,128)(2,1)} %own_ref.1), channel_id=1, source_target_pairs={{0,1},{1,0},{2,3},{3,2},{4,5},{5,4},{6,7},{7,6},{8,9},{9,8},{10,11... | collective-permute-start | bytes 56623112 | tf_op jit(solution)/shard_map/ppermute | solution.py:21
  5.1 80.3 %collective-permute-start.2 = (bf16[3072,128]{1,0:T(8,128)(2,1)}, bf16[3072,128]{1,0:T(8,128)(2,1)}, u32[]{:S(2)}, u32[]{:S(2)}) collective-permute-start(bf16[3072,128]{1,0:T(8,128)(2,1)} %get-tuple-element.24), channel_id=1, source_target_pairs={{0,4},{4,0},{8,12},{12,8},{16,20},{20,16},{24,28},{28,24},{1,5},{5... | collective-permute-start | bytes 2359304 | tf_op jit(solution)/shard_map/ppermute | solution.py:21
  7.8 41.2 %collective-permute-start.4 = (bf16[3072,128]{1,0:T(8,128)(2,1)}, bf16[3072,128]{1,0:T(8,128)(2,1)}, u32[]{:S(2)}, u32[]{:S(2)}) collective-permute-start(bf16[3072,128]{1,0:T(8,128)(2,1)} %get-tuple-element.24), channel_id=1, source_target_pairs={{0,2},{1,3},{2,0},{3,1},{4,6},{5,7},{6,4},{7,5},{8,10},{9,11},{10,... | collective-permute-start | bytes 2359304 | tf_op jit(solution)/shard_map/ppermute | solution.py:21
  9.3 79.9 %collective-permute-start.3 = (bf16[3072,128]{1,0:T(8,128)(2,1)}, bf16[3072,128]{1,0:T(8,128)(2,1)}, u32[]{:S(2)}, u32[]{:S(2)}) collective-permute-start(bf16[3072,128]{1,0:T(8,128)(2,1)} %get-tuple-element.23), channel_id=1, source_target_pairs={{0,4},{4,0},{8,12},{12,8},{16,20},{20,16},{24,28},{28,24},{1,5},{5... | collective-permute-start | bytes 2359304 | tf_op jit(solution)/shard_map/ppermute | solution.py:21
  9.8 34.6 %collective-permute-start.5 = (bf16[3072,128]{1,0:T(8,128)(2,1)}, bf16[3072,128]{1,0:T(8,128)(2,1)S(1)}, u32[]{:S(2)}, u32[]{:S(2)}) collective-permute-start(bf16[3072,128]{1,0:T(8,128)(2,1)} %get-tuple-element.23), channel_id=1, source_target_pairs={{0,2},{1,3},{2,0},{3,1},{4,6},{5,7},{6,4},{7,5},{8,10},{9,11},{10,... | collective-permute-start | bytes 2359304 | tf_op jit(solution)/shard_map/ppermute | solution.py:21
  12.8 120.3 %copy-start = (bf16[1536,512]{0,1:T(8,128)(2,1)}, bf16[1536,512]{0,1:T(8,128)(2,1)S(1)}, u32[]{:S(2)}) copy-start(bf16[1536,512]{0,1:T(8,128)(2,1)S(1)} %copy.40) | copy-start | bytes 4718596
  44.4 0.9 copy-start.2
  45.3 35.5 %collective-permute-start.12 = (bf16[512,1536]{1,0:T(8,128)(2,1)S(1)}, bf16[512,1536]{1,0:T(8,128)(2,1)S(1)}, u32[]{:S(2)}, u32[]{:S(2)}) collective-permute-start(bf16[512,1536]{1,0:T(8,128)(2,1)S(1)} %bitcast.31), channel_id=1, source_target_pairs={{0,2},{1,3},{2,0},{3,1},{4,6},{5,7},{6,4},{7,5},{8,10},{9,11},{10,... | collective-permute-start | bytes 4718600 | tf_op jit(solution)/shard_map/ppermute | solution.py:21
  49.0 56.0 %collective-permute-start.9 = (bf16[3072,128]{1,0:T(8,128)(2,1)}, bf16[3072,128]{1,0:T(8,128)(2,1)}, u32[]{:S(2)}, u32[]{:S(2)}) collective-permute-start(bf16[3072,128]{1,0:T(8,128)(2,1)} %copy-done.2), channel_id=1, source_target_pairs={{0,4},{4,0},{8,12},{12,8},{16,20},{20,16},{24,28},{28,24},{1,5},{5... | collective-permute-start | bytes 2359304 | tf_op jit(solution)/shard_map/ppermute | solution.py:21
  80.8 52.3 %copy-start.1 = (bf16[512,1536]{1,0:T(8,128)(2,1)}, bf16[512,1536]{1,0:T(8,128)(2,1)S(1)}, u32[]{:S(2)}) copy-start(bf16[512,1536]{1,0:T(8,128)(2,1)S(1)} %collective-permute-done.12.refs_4_) | copy-start | bytes 4718596
  80.8 18.1 %collective-permute-start.8 = (bf16[3072,128]{1,0:T(8,128)(2,1)}, bf16[3072,128]{1,0:T(8,128)(2,1)}, u32[]{:S(2)}, u32[]{:S(2)}) collective-permute-start(bf16[3072,128]{1,0:T(8,128)(2,1)} %collective-permute-done.4.refs_3_), channel_id=1, source_target_pairs={{0,4},{4,0},{8,12},{12,8},{16,20},{20,16},{24,28},{28,24},{1,5},{5... | collective-permute-start | bytes 2359304 | tf_op jit(solution)/shard_map/ppermute | solution.py:21
  85.4 61.9 %collective-permute-start.13 = (bf16[512,1536]{1,0:T(8,128)(2,1)S(1)}, bf16[512,1536]{1,0:T(8,128)(2,1)}, u32[]{:S(2)}, u32[]{:S(2)}) collective-permute-start(bf16[512,1536]{1,0:T(8,128)(2,1)S(1)} %collective-permute-done.12.refs_4_), channel_id=1, source_target_pairs={{0,1},{1,0},{2,3},{3,2},{4,5},{5,4},{6,7},{7,6},{8,9},{9,8},{10,11... | collective-permute-start | bytes 4718600 | tf_op jit(solution)/shard_map/ppermute | solution.py:21
  85.4 61.9 %collective-permute-start.11 = (bf16[512,1536]{1,0:T(8,128)(2,1)S(1)}, bf16[512,1536]{1,0:T(8,128)(2,1)}, u32[]{:S(2)}, u32[]{:S(2)}) collective-permute-start(bf16[512,1536]{1,0:T(8,128)(2,1)S(1)} %bitcast.32), channel_id=1, source_target_pairs={{0,1},{1,0},{2,3},{3,2},{4,5},{5,4},{6,7},{7,6},{8,9},{9,8},{10,11... | collective-permute-start | bytes 4718600 | tf_op jit(solution)/shard_map/ppermute | solution.py:21
  89.2 43.9 %collective-permute-start.6 = (bf16[3072,128]{1,0:T(8,128)(2,1)}, bf16[3072,128]{1,0:T(8,128)(2,1)}, u32[]{:S(2)}, u32[]{:S(2)}) collective-permute-start(bf16[3072,128]{1,0:T(8,128)(2,1)} %collective-permute-done.2.refs_1_), channel_id=1, source_target_pairs={{0,8},{8,16},{12,4},{16,24},{20,12},{28,20},{1,9},{9,17},{13,5},{1... | collective-permute-start | bytes 2359304 | tf_op jit(solution)/shard_map/ppermute | solution.py:21
  98.9 36.9 %collective-permute-start.7 = (bf16[3072,128]{1,0:T(8,128)(2,1)}, bf16[3072,128]{1,0:T(8,128)(2,1)}, u32[]{:S(2)}, u32[]{:S(2)}) collective-permute-start(bf16[3072,128]{1,0:T(8,128)(2,1)} %collective-permute-done.3.refs_2_), channel_id=1, source_target_pairs={{0,8},{8,16},{12,4},{16,24},{20,12},{28,20},{1,9},{9,17},{13,5},{1... | collective-permute-start | bytes 2359304 | tf_op jit(solution)/shard_map/ppermute | solution.py:21
  105.0 42.3 %collective-permute-start.10 = (bf16[3072,128]{1,0:T(8,128)(2,1)}, bf16[3072,128]{1,0:T(8,128)(2,1)}, u32[]{:S(2)}, u32[]{:S(2)}) collective-permute-start(bf16[3072,128]{1,0:T(8,128)(2,1)} %collective-permute-done.8.refs_2_), channel_id=1, source_target_pairs={{0,8},{8,16},{12,4},{16,24},{20,12},{28,20},{1,9},{9,17},{13,5},{1... | collective-permute-start | bytes 2359304 | tf_op jit(solution)/shard_map/ppermute | solution.py:21
  133.1 31.4 %collective-permute-start.14 = (bf16[1536,128]{1,0:T(8,128)(2,1)}, bf16[1536,128]{1,0:T(8,128)(2,1)S(1)}, u32[]{:S(2)}, u32[]{:S(2)}) collective-permute-start(bf16[1536,128]{1,0:T(8,128)(2,1)} %slice.20), channel_id=1, source_target_pairs={{0,8},{8,16},{12,4},{16,24},{20,12},{28,20},{1,9},{9,17},{13,5},{1... | collective-permute-start | bytes 1179656 | tf_op jit(solution)/shard_map/ppermute | solution.py:21
  135.8 28.7 %collective-permute-start.15 = (bf16[1536,128]{1,0:T(8,128)(2,1)}, bf16[1536,128]{1,0:T(8,128)(2,1)S(1)}, u32[]{:S(2)}, u32[]{:S(2)}) collective-permute-start(bf16[1536,128]{1,0:T(8,128)(2,1)} %slice.19), channel_id=1, source_target_pairs={{4,8},{8,4},{12,16},{16,12},{20,24},{24,20},{5,9},{9,5},{13,17},{1... | collective-permute-start | bytes 1179656 | tf_op jit(solution)/shard_map/ppermute | solution.py:21
  164.5 0.8 copy-start.3
  164.5 0.9 copy-start.4

commit v3 on v0

v3 whole, which is shorter than its diff:
```python
import functools

import jax
import jax.numpy as jnp
from jax import lax
from jax.experimental import pallas as pl
from jax.experimental.pallas import tpu as pltpu
from jax.sharding import PartitionSpec as P

EVERY = ("region", "col")
VMEM = 60 * 2**20
PAIR = 2
LANES = 8
DEPTH = 3
V_BITS, BLOCK_BITS = 8, 10
SMALL = pl.CostEstimate(flops=1, bytes_accessed=1, transcendentals=0)
LARGE = pl.CostEstimate(flops=10**12, bytes_accessed=10**9, transcendentals=0)


def moved(array, axis, target):
    count = lax.axis_size(axis)
    pairs = [(i, target(i)) for i in range(count)]
    return lax.ppermute(array, axis, [(i, j) for i, j in pairs if 0 <= j < count])


def to_core(array):
    return moved(array, "col", lambda c: c ^ 1)


def to_side(array):
    return moved(array, "col", lambda c: c ^ 2)


def to_near(array):
    return moved(array, "region", lambda r: r ^ 1)


def to_far(array):
    return moved(array, "region", lambda r: r + 1 if r % 2 else r - 1)


def onward(array):
    return moved(array, "region", lambda r: r - 2 if r % 2 else r + 2)


def together(*arrays):
    return lax.optimization_barrier(arrays)


def after(array, *others):
    return together(array, *others)[0]


def largest_divisor(length, limit):
    return max(d for d in range(1, limit + 1) if length % d == 0)


def anywhere(count):
    return [pl.BlockSpec(memory_space=pl.ANY)] * count


def image_kernel(group, parts, fills, cols_ref, offs_ref, own_ref, other_ref, *refs):
    pieces = len(parts)
    v_refs, refs = refs[:pieces], refs[pieces:]
    out_ref, v_all, blocks, sums, v_sems, a_sems, out_sems = refs
    depth, _, _, slots, block, _ = blocks.shape
    count = out_ref.shape[1]
    groups = count // group
    first = offs_ref[pieces + len(fills)]

    def place(n, rows, part):
        start = pl.multiple_of(offs_ref[n] * block, block)
        return pl.ds(start, rows), pl.ds(part * block, block)

    def read(g):
        slot = lax.rem(g, depth)
        here = pl.ds(first + g * group, group)
        return [
            pltpu.make_async_copy(ref.at[here], blocks.at[slot, n], a_sems.at[slot, n])
            for n, ref in enumerate((own_ref, other_ref))
        ]

    def write(g):
        slot = lax.rem(g, 2)
        return pltpu.make_async_copy(
            sums.at[slot], out_ref.at[:, pl.ds(g * group, group)], out_sems.at[slot]
        )

    copies = []
    for p, ref in enumerate(v_refs):
        rows = ref.shape[0]
        target = v_all.at[place(p, rows, parts[p])]
        copies.append(pltpu.make_async_copy(ref, target, v_sems.at[p]))
    for copy in copies:
        copy.start()
    for g in range(depth - 1):
        for copy in read(g):
            copy.start()
    for n, (rows, part) in enumerate(fills):
        at = place(pieces + n, rows, part)
        v_all[at] = jnp.zeros((rows, block), v_all.dtype)
    for copy in copies:
        copy.wait()

    def one(g, carry):
        slot, out_slot = lax.rem(g, depth), lax.rem(g, 2)

        @pl.when(g + depth - 1 < groups)
        def _():
            for copy in read(g + depth - 1):
                copy.start()

        for copy in read(g):
            copy.wait()

        @pl.when(g >= 2)
        def _():
            write(g - 2).wait()

        for r in range(group):
            left, right = [], []
            for n in range(2):
                for s in range(slots):
                    code = cols_ref[first + g * group + r, n * slots + s]
                    left.append(blocks[slot, n, r, s])
                    right.append(v_all[pl.ds(pl.multiple_of(code * block, block), block), :])
            product = jnp.dot(
                jnp.concatenate(left, axis=1),
                jnp.concatenate(right, axis=0),
                preferred_element_type=jnp.float32,
            )
            for part in range(2):
                sums[out_slot, part, r] = product[:, part * block : (part + 1) * block]
        write(g).start()
        return carry

    lax.fori_loop(0, groups, one, 0)
    for g in range(max(groups - 2, 0), groups):
        write(g).wait()


def image_of(cols, own, other, v_pieces, places, parts, fills, start, count):
    rows, slots, block = own.shape[:3]
    group = largest_divisor(count, 4)
    depth = min(3, count // group + 1)
    pieces = len(v_pieces)
    offs = jnp.stack([*places, *[f[0] for f in fills], start]).astype(jnp.int32)
    fill_shapes = tuple((f[1] * block, f[2]) for f in fills)
    return pl.pallas_call(
        functools.partial(image_kernel, group, parts, fill_shapes),
        out_shape=jax.ShapeDtypeStruct((2, count, block, block), jnp.float32),
        grid_spec=pltpu.PrefetchScalarGridSpec(
            num_scalar_prefetch=2,
            grid=(1,),
            in_specs=anywhere(2 + pieces),
            out_specs=pl.BlockSpec(memory_space=pl.ANY),
            scratch_shapes=[
                pltpu.VMEM((3 * rows * block, 2 * block), jnp.bfloat16),
                pltpu.VMEM((depth, 2, group, slots, block, block), jnp.bfloat16),
                pltpu.VMEM((2, 2, group, block, block), jnp.float32),
                pltpu.SemaphoreType.DMA((pieces,)),
                pltpu.SemaphoreType.DMA((depth, 2)),
                pltpu.SemaphoreType.DMA((2,)),
            ],
        ),
        compiler_params=pltpu.CompilerParams(vmem_limit_bytes=VMEM),
        cost_estimate=SMALL,
        name="image",
    )(cols, offs, own, other, *v_pieces)


def cut_kernel(start_ref, v_ref, out_ref, stage, sems):
    start = pl.multiple_of(start_ref[0] * 128, 128)
    read = pltpu.make_async_copy(v_ref.at[pl.ds(start, stage.shape[0])], stage, sems.at[0])
    write = pltpu.make_async_copy(stage, out_ref, sems.at[1])
    read.start()
    read.wait()
    write.start()
    write.wait()


def cut(array, start, length):
    part = jax.ShapeDtypeStruct((length, array.shape[1]), array.dtype)
    return pl.pallas_call(
        cut_kernel,
        out_shape=part,
        grid_spec=pltpu.PrefetchScalarGridSpec(
            num_scalar_prefetch=1,
            grid=(1,),
            in_specs=anywhere(1),
            out_specs=pl.BlockSpec(memory_space=pl.ANY),
            scratch_shapes=[pltpu.VMEM(part.shape, part.dtype), pltpu.SemaphoreType.DMA((2,))],
        ),
        cost_estimate=SMALL,
        name="cut",
    )(jnp.reshape(start, (1,)).astype(jnp.int32), array)


def lists_kernel(rows, slots, plan, codes_ref, *refs):
    outs, steps_ref = refs[:-1], refs[-1]
    per_source = LANES * PAIR
    size = 2 * rows * slots
    lengths = [out.shape[0] // 2 for out in outs]
    turns = max(len(classes) for classes in plan)

    def one_row(row, ends):
        ends = list(ends)
        for turn in range(turns):
            active = [
                (2 * k + source, out, classes[turn] * size + (source * rows + row) * slots)
                for k, (out, classes) in enumerate(zip(outs, plan))
                if turn < len(classes)
                for source in range(2)
            ]
            for s in range(slots):
                for n, out, base in active:
                    code = codes_ref[base + s]
                    out[ends[n]] = code
                    ends[n] = ends[n] + jnp.minimum(code, 1)
            for n, out, _ in active:
                out[ends[n]] = 0
                ends[n] = ends[n] + (ends[n] & (PAIR - 1))
        return tuple(ends)

    first = tuple(jnp.int32(source * length) for length in lengths for source in range(2))
    ends = lax.fori_loop(0, rows, one_row, first)
    for k, out in enumerate(outs):
        pair = ends[2 * k], ends[2 * k + 1]
        most = jnp.maximum(pair[0], pair[1] - lengths[k])
        steps = lax.div(most + per_source - 1, per_source)
        steps_ref[k] = steps
        for source in range(2):
            def clear(at, carry, out=out):
                out[at] = 0
                return carry

            lax.fori_loop(pair[source], source * lengths[k] + steps * per_source, clear, 0)


def lists_of(codes, rows, slots, plan):
    lengths = [2 * capacity_of(rows, slots, len(c)) * PAIR for c in plan]
    smem = pl.BlockSpec(memory_space=pltpu.SMEM)
    *lists, steps = pl.pallas_call(
        functools.partial(lists_kernel, rows, slots, plan),
        out_shape=[jax.ShapeDtypeStruct((n,), jnp.int32) for n in lengths + [len(plan)]],
        in_specs=[smem],
        out_specs=[smem] * (len(plan) + 1),
        cost_estimate=SMALL,
        name="lists",
    )(codes)
    return lists, steps


def capacity_of(rows, slots, parts):
    tasks = (rows * slots + rows * parts * (PAIR - 1)) // PAIR
    return (-(-tasks // LANES) + 1) * LANES


def add_listed(codes_ref, steps, a_refs, v_all, blocks, sems, total):
    block = blocks.shape[-1]
    per_source = LANES * PAIR
    length = codes_ref.shape[0] // len(a_refs)

    def fetch(step):
        slot = lax.rem(step, DEPTH)
        for s, a_ref in enumerate(a_refs):
            for n in range(per_source):
                code = codes_ref[s * length + step * per_source + n]
                block_id = (code >> V_BITS) & ((1 << BLOCK_BITS) - 1)
                pltpu.make_async_copy(
                    a_ref.at[block_id], blocks.at[slot, s * per_source + n], sems.at[slot]
                ).start()

    for ahead in range(DEPTH - 1):
        @pl.when(ahead < steps)
        def _():
            fetch(ahead)

    def run():
        def one(step, carry):
            slot = lax.rem(step, DEPTH)

            @pl.when(step + DEPTH - 1 < steps)
            def _():
                fetch(step + DEPTH - 1)

            pltpu.make_async_copy(blocks.at[slot], blocks.at[slot], sems.at[slot]).wait()
            products = []
            for s in range(len(a_refs)):
                for n in range(LANES):
                    left, right = [], []
                    for g in range(PAIR):
                        at = n * PAIR + g
                        code = codes_ref[s * length + step * per_source + at]
                        if g == 0:
                            row = code >> (BLOCK_BITS + V_BITS)
                        start = pl.multiple_of((code & ((1 << V_BITS) - 1)) * block, block)
                        left.append(blocks[slot, s * per_source + at])
                        right.append(v_all[pl.ds(start, block), :])
                    product = jnp.dot(
                        jnp.concatenate(left, axis=1),
                        jnp.concatenate(right, axis=0),
                        preferred_element_type=jnp.float32,
                    )
                    products.append((row, product))
            for row, product in products:
                total[row] += product
            return carry

        lax.fori_loop(0, steps, one, 0)

    return run


def list_scratch(v_pieces, block):
    v_rows = block + sum(v.shape[0] for v in v_pieces)
    return [
        pltpu.VMEM((v_rows, block), jnp.bfloat16),
        pltpu.VMEM((DEPTH, 2 * LANES * PAIR, block, block), jnp.bfloat16),
        pltpu.SemaphoreType.DMA((DEPTH,)),
    ]


def copies_of(pairs, sems):
    copies = [pltpu.make_async_copy(a, b, sems.at[n]) for n, (a, b) in enumerate(pairs)]
    for copy in copies:
        copy.start()
    return copies


def v_places(v_refs, v_all, block):
    places, at = [], block
    for ref in v_refs:
        places.append((ref, v_all.at[pl.ds(at, ref.shape[0])]))
        at += ref.shape[0]
    return places


def later_kernel(pieces, codes_ref, steps_ref, me_ref, own_ref, other_ref, *refs):
    images, v_refs, refs = refs[:2], refs[2 : 2 + pieces], refs[2 + pieces :]
    out_ref, v_all, blocks, a_sems, sems = refs
    block = out_ref.shape[1]
    pairs = v_places(v_refs, v_all, block)
    for n, ref in enumerate(images):
        pairs.append((ref.at[1], out_ref.at[pl.ds(me_ref[1 + n], ref.shape[1])]))
    copies = copies_of(pairs, sems)
    run = add_listed(
        codes_ref, steps_ref[0], (own_ref, other_ref), v_all, blocks, a_sems, out_ref
    )
    v_all[pl.ds(0, block), :] = jnp.zeros((block, block), v_all.dtype)
    for copy in copies:
        copy.wait()
    run()


def later_image(codes, steps, me, own, other, images, v_pieces):
    block = own.shape[-1]
    shape = (sum(image.shape[1] for image in images), block, block)
    return pl.pallas_call(
        functools.partial(later_kernel, len(v_pieces)),
        out_shape=jax.ShapeDtypeStruct(shape, jnp.float32),
        grid_spec=pltpu.PrefetchScalarGridSpec(
            num_scalar_prefetch=3,
            grid=(1,),
            in_specs=anywhere(4 + len(v_pieces)),
            out_specs=pl.BlockSpec(shape, lambda i, *_: (0, 0, 0)),
            scratch_shapes=list_scratch(v_pieces, block)
            + [pltpu.SemaphoreType.DMA((len(v_pieces) + 2,))],
        ),
        compiler_params=pltpu.CompilerParams(vmem_limit_bytes=VMEM),
        cost_estimate=LARGE,
        name="later",
    )(codes, steps, me, own, other, *images, *v_pieces)


def last_kernel(pieces, codes_ref, steps_ref, me_ref, own_ref, other_ref, *refs):
    images, late_ref, refs = refs[:2], refs[2], refs[3:]
    v_refs, w_refs = refs[:pieces], refs[pieces : 4 + pieces]
    out_ref, v_all, blocks, a_sems, image, w_all, sems = refs[4 + pieces :]
    _, rows, block, _ = image.shape
    early = copies_of(v_places(v_refs, v_all, block) + [(late_ref, image.at[1])], sems)
    run = add_listed(
        codes_ref, steps_ref[1], (own_ref, other_ref), v_all, blocks, a_sems, image.at[1]
    )
    w_places = [(w_refs[q], w_all.at[q]) for q in range(4)]
    for n, ref in enumerate(images):
        w_places.append((ref.at[0], image.at[0, pl.ds(me_ref[1 + n], ref.shape[1])]))
    later = copies_of(w_places, sems.at[pl.ds(pieces + 1, 6)])
    v_all[pl.ds(0, block), :] = jnp.zeros((block, block), v_all.dtype)
    for copy in early:
        copy.wait()
    run()
    for copy in later:
        copy.wait()
    length = rows // 4
    total = None
    for q in range(4):
        terms = []
        for part in range(2):
            here = image[part, pl.ds((me_ref[0] ^ q) * length, length)]
            here = here.reshape(length * block, block)
            upper = here.astype(jnp.bfloat16)
            terms += [upper, (here - upper.astype(jnp.float32)).astype(jnp.bfloat16)]
        term = jnp.dot(
            w_all[q], jnp.concatenate(terms, axis=1), preferred_element_type=jnp.float32
        )
        total = term if total is None else total + term
    mine = me_ref[0] >> 1
    count, _, tile, _ = out_ref.shape
    for part, place in ((0, mine), (1, 1 - mine)):
        first = 2 * part * block
        both = total[:, first : first + block] + total[:, first + block : first + 2 * block]
        out_ref[:, place] = both.reshape(count, tile, block)


def last_projected(codes, steps, me, own, other, images, late, v_pieces, w_pieces, devices):
    rows, block, _ = late.shape
    basis, length = w_pieces[0].shape
    shape = (devices, 2, basis // devices, block)
    return pl.pallas_call(
        functools.partial(last_kernel, len(v_pieces)),
        out_shape=jax.ShapeDtypeStruct(shape, jnp.float32),
        grid_spec=pltpu.PrefetchScalarGridSpec(
            num_scalar_prefetch=3,
            grid=(1,),
            in_specs=anywhere(9 + len(v_pieces)),
            out_specs=pl.BlockSpec(shape, lambda i, *_: (0, 0, 0, 0)),
            scratch_shapes=list_scratch(v_pieces, block)
            + [
                pltpu.VMEM((2, rows, block, block), jnp.float32),
                pltpu.VMEM((4, basis, length), jnp.bfloat16),
                pltpu.SemaphoreType.DMA((len(v_pieces) + 7,)),
            ],
        ),
        compiler_params=pltpu.CompilerParams(vmem_limit_bytes=VMEM),
        cost_estimate=SMALL,
        name="last_projected",
    )(codes, steps, me, own, other, *images, late, *v_pieces, *w_pieces)


def shards(basis_v, basis_w, couplings, coupling_cols):
    rows, slots, block = couplings.shape[:3]
    regions, columns = lax.axis_size("region"), lax.axis_size("col")
    region, col = lax.axis_index("region"), lax.axis_index("col")
    odd = region % 2
    half = rows // 2

    own_a = cut(basis_v, odd * half, half * block)
    near_a, side_a = to_near(own_a), to_side(own_a)
    here = after(coupling_cols, own_a) - (region * rows - rows)
    there = to_core(here)
    w_own = basis_w.T
    w_core = to_core(after(w_own, there))
    other = to_core(after(couplings, w_core))
    own_b = cut(after(basis_v, w_core), (1 - odd) * half, half * block)
    near_b, side_b = to_near(own_b), to_side(own_b)

    cols = jnp.concatenate([here, there], axis=1)
    near_base = jnp.where(odd == 1, 0, 2 * rows)
    far_base = 2 * rows - near_base
    first, second = (1 - odd) * half, odd * half
    near_at = [near_base + first, near_base + second]
    far_at = [far_base + first, far_base + second]
    own_at = [rows + second, rows + first]
    me = jnp.stack([col, first, second]).astype(jnp.int32)

    both = jnp.stack([here, there])[None]
    in_near = both // rows == near_base // rows
    in_far = both // rows == far_base // rows
    is_a = (both % rows >= half) == (odd == 0)
    kind = jnp.arange(2, dtype=jnp.int32)[:, None, None, None]
    row = jnp.arange(rows, dtype=jnp.int32)[:, None]
    summed_early = (row >= half) == (odd == 0)
    taken = jnp.where(
        kind == 0, (in_near & (~is_a | summed_early)) | (in_far & is_a), in_far & ~is_a
    )
    piece = jnp.where(kind == 0, jnp.where(in_far, 2, jnp.where(is_a, 0, 1)), 0)
    block_id = row * slots + jnp.arange(slots, dtype=jnp.int32)[None, :]
    codes = (row << (BLOCK_BITS + V_BITS)) + (block_id << V_BITS)
    codes = jnp.where(taken, codes + 1 + piece * half + both % half, 0).reshape(-1)
    (later, last), steps = lists_of(codes, rows, slots, ((0,), (1,)))

    near_a, side_a, steps, cols, me, w_own = together(near_a, side_a, steps, cols, me, w_own)
    far_a, near_side_a = onward(near_a), to_near(side_a)

    near_b, side_b, other = together(near_b, side_b, other)
    far_b, near_side_b = onward(after(near_b, far_a)), to_near(side_b)
    w_side = to_side(after(w_own, near_b))
    pieces = [basis_v, near_a, near_b, far_a, side_a, side_b]
    at = [jnp.int32(rows), *near_at, far_at[0], *own_at]
    fills = [(far_at[1], half, 0), (near_base, rows, 1), (far_base, rows, 1)]
    early = image_of(
        cols, couplings, other, pieces, at, (0, 0, 0, 0, 1, 1), fills, first, half
    )

    early, near_side_a = together(early, near_side_a)
    far_side_a = onward(near_side_a)
    pieces = [basis_v, near_a, near_b, far_a, far_b, side_a, side_b, near_side_a]
    at = [jnp.int32(rows), *near_at, *far_at, *own_at, near_at[0]]
    fills = [(near_at[1], half, 1), (far_base, rows, 1)]
    rest = image_of(
        cols, couplings, other, pieces, at, (0, 0, 0, 0, 0, 1, 1, 1), fills, second, half
    )
    images = [early, rest]
    rest, side_b, w_side = together(rest, side_b, w_side)
    far_side_b = to_far(side_b)
    w_pieces = [w_own, w_core, w_side, to_core(w_side)]
    images = [early, rest]
    own_list = couplings.reshape(rows * slots, block, block)
    other_list = other.reshape(rows * slots, block, block)
    pieces = [near_side_a, near_side_b, far_side_a]
    image = later_image(later, steps, me, own_list, other_list, images, pieces)

    sent = last_projected(
        last, steps, me, own_list, other_list, images, image, [far_side_b], w_pieces,
        regions * columns,
    )
    received = lax.all_to_all(sent, EVERY, 0, 0, tiled=True)
    tile = sent.shape[2]
    summed = received.reshape(regions, columns // 2, 2, 2, tile, block).sum(axis=(0, 1))
    return summed.transpose(2, 1, 0, 3).reshape(tile, columns * block)


def solution(mesh):
    in_specs = (
        P("region", "col"),
        P(("region", "col"), None),
        P("region", "col", None, None),
        P("region", "col"),
    )
    out_specs = P(("region", "col"), None)
    return jax.shard_map(shards, mesh=mesh, in_specs=in_specs, out_specs=out_specs, check_vma=False)
```

time: 603 us -> 144 us (0.24)
  waiting for transfers between devices: 424 us -> 23.4 us
  local copies, waits for them, and re-layouts: 82.6 us -> 5.73 us
  Pallas kernels: 0 us -> 63 us
  matrix products: 54.1 us -> 0 us
  blocking collectives: 0 us -> 25.8 us
  other arithmetic: 21.8 us -> 1.76 us
  starting transfers between devices: 6.47 us -> 23 us
  between operations: 13.2 us -> 0.2 us
    reduce_scatter x2 -> x0, waiting for transfers between devices: 234 us -> none  [the longest x1 135 us: shards(): lax.psum_scatter(partial_tile, ('region', 'col'), scatter_dimension=0, ti...]
    all_gather x1 -> x0, waiting for transfers between devices: 124 us -> none  [shards(): widened = lax.all_gather(with_rims, 'col', axis=1, tiled=True)]
    gather x6 -> x0, local copies, waits for them, and re-layouts: 79.6 us -> none  [one_group(): picked = widened_blocks[columns]]
    pallas_call x0 -> x7, Pallas kernels: none -> 63 us  [the longest x2 24.4 us: image_of(): pl.pallas_call(functools.partial(image_kernel, group, parts, fill_shapes)...]
    dot_general x8 -> x0, matrix products: 54.1 us -> none  [the longest x6 52.1 us: one_group(): jnp.einsum('gkrs,gksc->grc', blocks, picked, preferred_element_type=jnp.f...]
    ppermute x2 -> x15, waiting for transfers between devices: 66.3 us -> 23.4 us  [moved(): lax.ppermute(array, axis, [(i, j) for i, j in pairs if 0 <= j < count])]
    all_to_all x0 -> x1, blocking collectives: none -> 25.8 us  [shards(): received = lax.all_to_all(sent, EVERY, 0, 0, tiled=True)]
    concatenate x1, other arithmetic: 19.5 us -> 0.69 us  [shards(): cols = jnp.concatenate([here, there], axis=1)]
  transfers between devices with their start and end apart: 5 -> 15, of which waited for: 4 -> 7; matrix products, arithmetic and copies ran while one was open for 0% -> 3% of each run, Pallas kernels for 0% -> 36%
where the time goes in v3:
time: 144 us; the launch traced here: 143 us
  Pallas kernels  63 us (44%)
  blocking collectives  25.8 us (18%)
  waiting for transfers between devices  23.4 us (16%)
  starting transfers between devices  23 us (16%)
  local copies, waits for them, and re-layouts  5.73 us (4%)
  other arithmetic  1.76 us (1%)
    all_to_all x1, blocking collectives, shards(): received = lax.all_to_all(sent, EVERY, 0, 0, tiled=True)  25.8 us
    pallas_call x2, Pallas kernels, image_of(): pl.pallas_call(functools.partial(image_kernel, group, parts, fill_shapes)...  24.4 us
    ppermute x15, waiting for transfers between devices, moved(): lax.ppermute(array, axis, [(i, j) for i, j in pairs if 0 <= j < count])  23.4 us
    ppermute x15, starting transfers between devices, moved(): lax.ppermute(array, axis, [(i, j) for i, j in pairs if 0 <= j < count])  23 us
    pallas_call x1, Pallas kernels, later_image(): pl.pallas_call(functools.partial(later_kernel, len(v_pieces)), out_shape=...  17.6 us
    pallas_call x1, Pallas kernels, last_projected(): pl.pallas_call(functools.partial(last_kernel, len(v_pieces)), out_shape=j...  9.95 us
    pallas_call x1, Pallas kernels, lists_of(): pl.pallas_call(functools.partial(lists_kernel, rows, slots, plan), out_sh...  6.75 us
    pallas_call x2, Pallas kernels, cut(): pl.pallas_call(cut_kernel, out_shape=part, grid_spec=pltpu.PrefetchScalar...  4.23 us
  transfers between devices with their start and end apart: 15, of which 7 were waited for; matrix products, arithmetic and copies ran while one was open for 3% of the time, Pallas kernels for 36%

profile of v3, /device:TPU:0, one launch (start us, length us, event | category | flops | bytes accessed | tf_op | source)
XLA Modules:
  0.0 142.9 jit_solution(12976553783048859480)
XLA Ops:
  0.0 2.2 %cut.2 = bf16[3072,128]{1,0:T(8,128)(2,1)} custom-call(s32[1]{0:T(128)} %bitcast.start_ref, bf16[6144,128]{1,0:T(8,128)(2,1)} %refs_0_.3), custom_call_target="tpu_custom_call" | custom-call | flops 1 | bytes 1 | tf_op jit(solution)/shard_map/cut/pallas_call | solution.py:184
  4.0 3.1 %collective-permute-done.3.refs_5_ = bf16[512,1536]{1,0:T(8,128)(2,1)S(1)} collective-permute-done((bf16[512,1536]{1,0:T(8,128)(2,1)S(1)}, bf16[512,1536]{1,0:T(8,128)(2,1)S(1)}, u32[]{:S(2)}, u32[]{:S(2)}) %collective-permute-start.3) | collective-permute-done | bytes 1572896 | tf_op jit(solution)/shard_map/ppermute | solution.py:23
  7.4 0.8 copy-done.3
  8.2 2.9 %collective-permute-start.1 = (bf16[3072,128]{1,0:T(8,128)(2,1)}, bf16[3072,128]{1,0:T(8,128)(2,1)S(1)}, u32[]{:S(2)}, u32[]{:S(2)}) collective-permute-start(bf16[3072,128]{1,0:T(8,128)(2,1)} %cut.2), channel_id=1, source_target_pairs={{0,4},{4,0},{8,12},{12,8},{16,20},{20,16},{24,28},{28,24},{1,5},{5... | collective-permute-start | bytes 2359304 | tf_op jit(solution)/shard_map/ppermute | solution.py:23
  11.1 1.5 %collective-permute-start.2 = (bf16[3072,128]{1,0:T(8,128)(2,1)}, bf16[3072,128]{1,0:T(8,128)(2,1)S(1)}, u32[]{:S(2)}, u32[]{:S(2)}) collective-permute-start(bf16[3072,128]{1,0:T(8,128)(2,1)} %cut.2), channel_id=1, source_target_pairs={{0,2},{1,3},{2,0},{3,1},{4,6},{5,7},{6,4},{7,5},{8,10},{9,11},{10,... | collective-permute-start | bytes 2359304 | tf_op jit(solution)/shard_map/ppermute | solution.py:23
  13.0 2.1 %cut.3 = bf16[3072,128]{1,0:T(8,128)(2,1)} custom-call(s32[1]{0:T(128)} %bitcast.4.start_ref, bf16[6144,128]{1,0:T(8,128)(2,1)} %refs_0_.3), custom_call_target="tpu_custom_call" | custom-call | flops 1 | bytes 1 | tf_op jit(solution)/shard_map/cut/pallas_call | solution.py:184
  16.3 0.7 reshape.270.codes_ref
  17.7 6.8 %lists.1 = (s32[1280]{0:T(1024)}, s32[1280]{0:T(1024)}, s32[2]{0:T(128)}) custom-call(s32[2304]{0:T(1024)} %reshape.270.codes_ref), custom_call_target="tpu_custom_call" | custom-call | flops 1 | bytes 1 | tf_op jit(solution)/shard_map/lists/pallas_call | solution.py:243
  25.1 4.5 %collective-permute-done.1.refs_1_ = bf16[3072,128]{1,0:T(8,128)(2,1)S(1)} collective-permute-done((bf16[3072,128]{1,0:T(8,128)(2,1)}, bf16[3072,128]{1,0:T(8,128)(2,1)S(1)}, u32[]{:S(2)}, u32[]{:S(2)}) %collective-permute-start.1) | collective-permute-done | bytes 786464 | tf_op jit(solution)/shard_map/ppermute | solution.py:23
  29.6 2.1 %collective-permute-done.2.refs_4_.refs_5_ = bf16[3072,128]{1,0:T(8,128)(2,1)S(1)} collective-permute-done((bf16[3072,128]{1,0:T(8,128)(2,1)}, bf16[3072,128]{1,0:T(8,128)(2,1)S(1)}, u32[]{:S(2)}, u32[]{:S(2)}) %collective-permute-start.2) | collective-permute-done | bytes 786464 | tf_op jit(solution)/shard_map/ppermute | solution.py:23
  31.7 4.4 %collective-permute-start.7 = (bf16[3072,128]{1,0:T(8,128)(2,1)S(1)}, bf16[3072,128]{1,0:T(8,128)(2,1)}, u32[]{:S(2)}, u32[]{:S(2)}) collective-permute-start(bf16[3072,128]{1,0:T(8,128)(2,1)S(1)} %collective-permute-done.1.refs_1_), channel_id=1, source_target_pairs={{0,8},{8,16},{12,4},{16,24},{20,12},{28,20},{1,9},{9,17},{13,5},{1... | collective-permute-start | bytes 2359304 | tf_op jit(solution)/shard_map/ppermute | solution.py:23
  36.1 10.0 %collective-permute-done.4.refs_2_ = bf16[3072,128]{1,0:T(8,128)(2,1)} collective-permute-done((bf16[3072,128]{1,0:T(8,128)(2,1)}, bf16[3072,128]{1,0:T(8,128)(2,1)}, u32[]{:S(2)}, u32[]{:S(2)}) %collective-permute-start.4) | collective-permute-done | bytes 786464 | tf_op jit(solution)/shard_map/ppermute | solution.py:23
  46.1 1.5 %collective-permute-done.5.refs_5_.refs_6_ = bf16[3072,128]{1,0:T(8,128)(2,1)} collective-permute-done((bf16[3072,128]{1,0:T(8,128)(2,1)}, bf16[3072,128]{1,0:T(8,128)(2,1)}, u32[]{:S(2)}, u32[]{:S(2)}) %collective-permute-start.5) | collective-permute-done | bytes 786464 | tf_op jit(solution)/shard_map/ppermute | solution.py:23
  47.6 1.5 %collective-permute-start.10 = (bf16[512,1536]{1,0:T(8,128)(2,1)S(1)}, bf16[512,1536]{1,0:T(8,128)(2,1)}, u32[]{:S(2)}, u32[]{:S(2)}) collective-permute-start(bf16[512,1536]{1,0:T(8,128)(2,1)S(1)} %bitcast.24), channel_id=1, source_target_pairs={{0,2},{1,3},{2,0},{3,1},{4,6},{5,7},{6,4},{7,5},{8,10},{9,11},{10,... | collective-permute-start | bytes 4718600 | tf_op jit(solution)/shard_map/ppermute | solution.py:23
  50.2 5.2 %collective-permute-start.9 = (bf16[3072,128]{1,0:T(8,128)(2,1)}, bf16[3072,128]{1,0:T(8,128)(2,1)}, u32[]{:S(2)}, u32[]{:S(2)}) collective-permute-start(bf16[3072,128]{1,0:T(8,128)(2,1)} %collective-permute-done.4.refs_2_), channel_id=1, source_target_pairs={{0,8},{8,16},{12,4},{16,24},{20,12},{28,20},{1,9},{9,17},{13,5},{1... | collective-permute-start | bytes 2359304 | tf_op jit(solution)/shard_map/ppermute | solution.py:23
  55.5 12.0 %image.2.refs_0_ = f32[2,24,128,128]{3,2,1,0:T(8,128)} custom-call(s32[48,24]{1,0:T(8,128)} %pad_add_fusion.cols_ref, s32[10]{0:T(128)} %stack.74.offs_ref, bf16[48,12,128,128]{3,2,1,0:T(8,128)(2,1)} %own_ref.3, bf16[48,12,128,128]{3,2,1,0:T(8,128)(2,1)} %collective-permute-done.6.other_ref, bf16[6144,128]{1,0:T(8,128)(2,1)} %refs_0_.3, ...), custom_call_target="tpu_custom_call" | custom-call | flops 1 | bytes 1 | tf_op jit(solution)/shard_map/image/pallas_call | solution.py:149
  67.5 2.2 %collective-permute-done.8.refs_7_.refs_2_ = bf16[3072,128]{1,0:T(8,128)(2,1)} collective-permute-done((bf16[3072,128]{1,0:T(8,128)(2,1)S(1)}, bf16[3072,128]{1,0:T(8,128)(2,1)}, u32[]{:S(2)}, u32[]{:S(2)}) %collective-permute-start.8) | collective-permute-done | bytes 786464 | tf_op jit(solution)/shard_map/ppermute | solution.py:23
  69.7 3.5 %collective-permute-start.12 = (bf16[3072,128]{1,0:T(8,128)(2,1)}, bf16[3072,128]{1,0:T(8,128)(2,1)S(1)}, u32[]{:S(2)}, u32[]{:S(2)}) collective-permute-start(bf16[3072,128]{1,0:T(8,128)(2,1)} %collective-permute-done.8.refs_7_.refs_2_), channel_id=1, source_target_pairs={{0,8},{8,16},{12,4},{16,24},{20,12},{28,20},{1,9},{9,17},{13,5},{1... | collective-permute-start | bytes 2359304 | tf_op jit(solution)/shard_map/ppermute | solution.py:23
  73.8 12.4 %image.3.refs_1_ = f32[2,24,128,128]{3,2,1,0:T(8,128)} custom-call(s32[48,24]{1,0:T(8,128)} %pad_add_fusion.cols_ref, s32[11]{0:T(128)} %stack.75.offs_ref, bf16[48,12,128,128]{3,2,1,0:T(8,128)(2,1)} %own_ref.3, bf16[48,12,128,128]{3,2,1,0:T(8,128)(2,1)} %collective-permute-done.6.other_ref, bf16[6144,128]{1,0:T(8,128)(2,1)} %refs_0_.3, ...), custom_call_target="tpu_custom_call" | custom-call | flops 1 | bytes 1 | tf_op jit(solution)/shard_map/image/pallas_call | solution.py:149
  86.3 1.6 %collective-permute-start.13 = (bf16[3072,128]{1,0:T(8,128)(2,1)}, bf16[3072,128]{1,0:T(8,128)(2,1)}, u32[]{:S(2)}, u32[]{:S(2)}) collective-permute-start(bf16[3072,128]{1,0:T(8,128)(2,1)} %collective-permute-done.5.refs_5_.refs_6_), channel_id=1, source_target_pairs={{4,8},{8,4},{12,16},{16,12},{20,24},{24,20},{5,9},{9,5},{13,17},{1... | collective-permute-start | bytes 2359304 | tf_op jit(solution)/shard_map/ppermute | solution.py:23
  87.9 0.9 copy-done.6
  88.8 17.6 %later.1.refs_2_ = f32[48,128,128]{2,1,0:T(8,128)} custom-call(s32[1280]{0:T(1024)} %get-tuple-element.48.codes_ref, s32[2]{0:T(128)} %get-tuple-element.31.steps_ref, s32[3]{0:T(128)} %pad_add_fusion.2.me_ref, bf16[576,128,128]{2,1,0:T(8,128)(2,1)} %bitcast.21, bf16[576,128,128]{2,1,0:T(8,128)(2,1)} %bitcast.7.other_ref, f32[2,24,128,128]{3,2,1,0:T(8,128)} %image.2.refs_0_, ...), custom_call_target="tpu_custom_call" | custom-call | flops 999999995904 | bytes 1000000000 | tf_op jit(solution)/shard_map/later/pallas_call | solution.py:359
  106.4 9.9 %last_projected.1 = f32[32,2,16,128]{3,2,1,0:T(8,128)} custom-call(s32[1280]{0:T(1024)} %get-tuple-element.29.codes_ref, s32[2]{0:T(128)} %get-tuple-element.31.steps_ref, s32[3]{0:T(128)} %pad_add_fusion.2.me_ref, bf16[576,128,128]{2,1,0:T(8,128)(2,1)} %bitcast.22, bf16[576,128,128]{2,1,0:T(8,128)(2,1)} %bitcast.7.other_ref, ...), custom_call_target="tpu_custom_call" | custom-call | flops 1 | bytes 1 | tf_op jit(solution)/shard_map/last_projected/pallas_call | solution.py:420
  116.4 25.8 %all_to_all.5 = f32[32,2,16,128]{3,2,1,0:T(8,128)S(1)} all-to-all(f32[32,2,16,128]{3,2,1,0:T(8,128)} %last_projected.1), channel_id=1, replica_groups=mesh['region'=8,'col'=4] {'region','col'}, dimensions={0} | all-to-all | bytes 1048576 | tf_op jit(solution)/shard_map/all_to_all | solution.py:518
  (55 shorter events, 7.6 us)
Async XLA Ops:
  0.0 2.2 %copy-start.5 = (s32[48,12]{0,1:T(8,128)S(1)}, s32[48,12]{0,1:T(8,128)}, u32[]{:S(2)}) copy-start(s32[48,12]{0,1:T(8,128)} %param.7) | copy-start | bytes 6916
  0.0 2.8 %copy-start.4 = (bf16[1536,512]{1,0:T(8,128)(2,1)S(1)}, bf16[1536,512]{1,0:T(8,128)(2,1)}, u32[]{:S(2)}) copy-start(bf16[1536,512]{1,0:T(8,128)(2,1)} %param.5) | copy-start | bytes 4718596
  2.3 1.4 collective-permute-start
  3.5 44.1 %copy-start = (bf16[1536,512]{0,1:T(8,128)(2,1)}, bf16[1536,512]{0,1:T(8,128)(2,1)S(1)}, u32[]{:S(2)}) copy-start(bf16[1536,512]{0,1:T(8,128)(2,1)S(1)} %copy.24) | copy-start | bytes 4718596
  3.7 3.4 %collective-permute-start.3 = (bf16[512,1536]{1,0:T(8,128)(2,1)S(1)}, bf16[512,1536]{1,0:T(8,128)(2,1)S(1)}, u32[]{:S(2)}, u32[]{:S(2)}) collective-permute-start(bf16[512,1536]{1,0:T(8,128)(2,1)S(1)} %bitcast.23), channel_id=1, source_target_pairs={{0,1},{1,0},{2,3},{3,2},{4,5},{5,4},{6,7},{7,6},{8,9},{9,8},{10,11... | collective-permute-start | bytes 4718600 | tf_op jit(solution)/shard_map/ppermute | solution.py:23
  7.1 1.1 copy-start.3
  7.1 40.5 %collective-permute-start.6 = (bf16[48,12,128,128]{3,2,1,0:T(8,128)(2,1)}, bf16[48,12,128,128]{3,2,1,0:T(8,128)(2,1)}, u32[]{:S(2)}, u32[]{:S(2)}) collective-permute-start(bf16[48,12,128,128]{3,2,1,0:T(8,128)(2,1)} %own_ref.3), channel_id=1, source_target_pairs={{0,1},{1,0},{2,3},{3,2},{4,5},{5,4},{6,7},{7,6},{8,9},{9,8},{10,11... | collective-permute-start | bytes 56623112 | tf_op jit(solution)/shard_map/ppermute | solution.py:23
  8.2 21.4 %collective-permute-start.1 = (bf16[3072,128]{1,0:T(8,128)(2,1)}, bf16[3072,128]{1,0:T(8,128)(2,1)S(1)}, u32[]{:S(2)}, u32[]{:S(2)}) collective-permute-start(bf16[3072,128]{1,0:T(8,128)(2,1)} %cut.2), channel_id=1, source_target_pairs={{0,4},{4,0},{8,12},{12,8},{16,20},{20,16},{24,28},{28,24},{1,5},{5... | collective-permute-start | bytes 2359304 | tf_op jit(solution)/shard_map/ppermute | solution.py:23
  11.1 20.6 %collective-permute-start.2 = (bf16[3072,128]{1,0:T(8,128)(2,1)}, bf16[3072,128]{1,0:T(8,128)(2,1)S(1)}, u32[]{:S(2)}, u32[]{:S(2)}) collective-permute-start(bf16[3072,128]{1,0:T(8,128)(2,1)} %cut.2), channel_id=1, source_target_pairs={{0,2},{1,3},{2,0},{3,1},{4,6},{5,7},{6,4},{7,5},{8,10},{9,11},{10,... | collective-permute-start | bytes 2359304 | tf_op jit(solution)/shard_map/ppermute | solution.py:23
  15.0 31.1 %collective-permute-start.4 = (bf16[3072,128]{1,0:T(8,128)(2,1)}, bf16[3072,128]{1,0:T(8,128)(2,1)}, u32[]{:S(2)}, u32[]{:S(2)}) collective-permute-start(bf16[3072,128]{1,0:T(8,128)(2,1)} %cut.3), channel_id=1, source_target_pairs={{0,4},{4,0},{8,12},{12,8},{16,20},{20,16},{24,28},{28,24},{1,5},{5... | collective-permute-start | bytes 2359304 | tf_op jit(solution)/shard_map/ppermute | solution.py:23
  15.6 32.0 %collective-permute-start.5 = (bf16[3072,128]{1,0:T(8,128)(2,1)}, bf16[3072,128]{1,0:T(8,128)(2,1)}, u32[]{:S(2)}, u32[]{:S(2)}) collective-permute-start(bf16[3072,128]{1,0:T(8,128)(2,1)} %cut.3), channel_id=1, source_target_pairs={{0,2},{1,3},{2,0},{3,1},{4,6},{5,7},{6,4},{7,5},{8,10},{9,11},{10,... | collective-permute-start | bytes 2359304 | tf_op jit(solution)/shard_map/ppermute | solution.py:23
  29.6 25.9 %copy-start.1 = (bf16[3072,128]{1,0:T(8,128)(2,1)}, bf16[3072,128]{1,0:T(8,128)(2,1)S(1)}, u32[]{:S(2)}) copy-start(bf16[3072,128]{1,0:T(8,128)(2,1)S(1)} %collective-permute-done.1.refs_1_) | copy-start | bytes 2359300
  31.7 23.8 %copy-start.2 = (bf16[3072,128]{1,0:T(8,128)(2,1)}, bf16[3072,128]{1,0:T(8,128)(2,1)S(1)}, u32[]{:S(2)}) copy-start(bf16[3072,128]{1,0:T(8,128)(2,1)S(1)} %collective-permute-done.2.refs_4_.refs_5_) | copy-start | bytes 2359300
  31.7 18.5 %collective-permute-start.7 = (bf16[3072,128]{1,0:T(8,128)(2,1)S(1)}, bf16[3072,128]{1,0:T(8,128)(2,1)}, u32[]{:S(2)}, u32[]{:S(2)}) collective-permute-start(bf16[3072,128]{1,0:T(8,128)(2,1)S(1)} %collective-permute-done.1.refs_1_), channel_id=1, source_target_pairs={{0,8},{8,16},{12,4},{16,24},{20,12},{28,20},{1,9},{9,17},{13,5},{1... | collective-permute-start | bytes 2359304 | tf_op jit(solution)/shard_map/ppermute | solution.py:23
  47.6 38.7 %collective-permute-start.10 = (bf16[512,1536]{1,0:T(8,128)(2,1)S(1)}, bf16[512,1536]{1,0:T(8,128)(2,1)}, u32[]{:S(2)}, u32[]{:S(2)}) collective-permute-start(bf16[512,1536]{1,0:T(8,128)(2,1)S(1)} %bitcast.24), channel_id=1, source_target_pairs={{0,2},{1,3},{2,0},{3,1},{4,6},{5,7},{6,4},{7,5},{8,10},{9,11},{10,... | collective-permute-start | bytes 4718600 | tf_op jit(solution)/shard_map/ppermute | solution.py:23
  49.1 20.6 %collective-permute-start.8 = (bf16[3072,128]{1,0:T(8,128)(2,1)S(1)}, bf16[3072,128]{1,0:T(8,128)(2,1)}, u32[]{:S(2)}, u32[]{:S(2)}) collective-permute-start(bf16[3072,128]{1,0:T(8,128)(2,1)S(1)} %collective-permute-done.2.refs_4_.refs_5_), channel_id=1, source_target_pairs={{0,4},{4,0},{8,12},{12,8},{16,20},{20,16},{24,28},{28,24},{1,5},{5... | collective-permute-start | bytes 2359304 | tf_op jit(solution)/shard_map/ppermute | solution.py:23
  50.2 23.6 %collective-permute-start.9 = (bf16[3072,128]{1,0:T(8,128)(2,1)}, bf16[3072,128]{1,0:T(8,128)(2,1)}, u32[]{:S(2)}, u32[]{:S(2)}) collective-permute-start(bf16[3072,128]{1,0:T(8,128)(2,1)} %collective-permute-done.4.refs_2_), channel_id=1, source_target_pairs={{0,8},{8,16},{12,4},{16,24},{20,12},{28,20},{1,9},{9,17},{13,5},{1... | collective-permute-start | bytes 2359304 | tf_op jit(solution)/shard_map/ppermute | solution.py:23
  55.5 32.4 %collective-permute-start.11 = (bf16[3072,128]{1,0:T(8,128)(2,1)}, bf16[3072,128]{1,0:T(8,128)(2,1)}, u32[]{:S(2)}, u32[]{:S(2)}) collective-permute-start(bf16[3072,128]{1,0:T(8,128)(2,1)} %collective-permute-done.5.refs_5_.refs_6_), channel_id=1, source_target_pairs={{0,4},{4,0},{8,12},{12,8},{16,20},{20,16},{24,28},{28,24},{1,5},{5... | collective-permute-start | bytes 2359304 | tf_op jit(solution)/shard_map/ppermute | solution.py:23
  69.7 18.2 %collective-permute-start.12 = (bf16[3072,128]{1,0:T(8,128)(2,1)}, bf16[3072,128]{1,0:T(8,128)(2,1)S(1)}, u32[]{:S(2)}, u32[]{:S(2)}) collective-permute-start(bf16[3072,128]{1,0:T(8,128)(2,1)} %collective-permute-done.8.refs_7_.refs_2_), channel_id=1, source_target_pairs={{0,8},{8,16},{12,4},{16,24},{20,12},{28,20},{1,9},{9,17},{13,5},{1... | collective-permute-start | bytes 2359304 | tf_op jit(solution)/shard_map/ppermute | solution.py:23
  86.3 20.1 %collective-permute-start.13 = (bf16[3072,128]{1,0:T(8,128)(2,1)}, bf16[3072,128]{1,0:T(8,128)(2,1)}, u32[]{:S(2)}, u32[]{:S(2)}) collective-permute-start(bf16[3072,128]{1,0:T(8,128)(2,1)} %collective-permute-done.5.refs_5_.refs_6_), channel_id=1, source_target_pairs={{4,8},{8,4},{12,16},{16,12},{20,24},{24,20},{5,9},{9,5},{13,17},{1... | collective-permute-start | bytes 2359304 | tf_op jit(solution)/shard_map/ppermute | solution.py:23
  87.9 18.6 %collective-permute-start.14 = (bf16[512,1536]{1,0:T(8,128)(2,1)}, bf16[512,1536]{1,0:T(8,128)(2,1)}, u32[]{:S(2)}, u32[]{:S(2)}) collective-permute-start(bf16[512,1536]{1,0:T(8,128)(2,1)} %collective-permute-done.10.refs_6_), channel_id=1, source_target_pairs={{0,1},{1,0},{2,3},{3,2},{4,5},{5,4},{6,7},{7,6},{8,9},{9,8},{10,11... | collective-permute-start | bytes 4718600 | tf_op jit(solution)/shard_map/ppermute | solution.py:23
  87.9 0.9 copy-start.6

commit v4 on v3

--- a/solution.py
+++ b/solution.py
@@ -11,7 +11,7 @@
 VMEM = 60 * 2**20
 PAIR = 2
 LANES = 8
-DEPTH = 3
+DEPTH = 5
 V_BITS, BLOCK_BITS = 8, 10
 SMALL = pl.CostEstimate(flops=1, bytes_accessed=1, transcendentals=0)
 LARGE = pl.CostEstimate(flops=10**12, bytes_accessed=10**9, transcendentals=0)
@@ -449,11 +449,10 @@
     near_a, side_a = to_near(own_a), to_side(own_a)
     here = after(coupling_cols, own_a) - (region * rows - rows)
     there = to_core(here)
+    other = to_core(after(couplings, there))
+    own_b = cut(after(basis_v, there), (1 - odd) * half, half * block)
+    near_b, side_b = to_near(own_b), to_side(own_b)
     w_own = basis_w.T
-    w_core = to_core(after(w_own, there))
-    other = to_core(after(couplings, w_core))
-    own_b = cut(after(basis_v, w_core), (1 - odd) * half, half * block)
-    near_b, side_b = to_near(own_b), to_side(own_b)
 
     cols = jnp.concatenate([here, there], axis=1)
     near_base = jnp.where(odd == 1, 0, 2 * rows)
@@ -502,9 +501,9 @@
         cols, couplings, other, pieces, at, (0, 0, 0, 0, 0, 1, 1, 1), fills, second, half
     )
     images = [early, rest]
-    rest, side_b, w_side = together(rest, side_b, w_side)
+    rest, side_b, w_own, w_side = together(rest, side_b, w_own, w_side)
     far_side_b = to_far(side_b)
-    w_pieces = [w_own, w_core, w_side, to_core(w_side)]
+    w_pieces = [w_own, to_core(w_own), w_side, to_core(w_side)]
     images = [early, rest]
     own_list = couplings.reshape(rows * slots, block, block)
     other_list = other.reshape(rows * slots, block, block)

time: 144 us -> 138 us (0.958)
  waiting for transfers between devices: 23.4 us -> 18.2 us
    ppermute x15, waiting for transfers between devices: 23.4 us -> 18.2 us  [moved(): lax.ppermute(array, axis, [(i, j) for i, j in pairs if 0 <= j < count])]
    unnamed x15 -> x13, local copies, waits for them, and re-layouts: 2.4 us -> 3.56 us
  transfers between devices with their start and end apart: 15 -> 15, of which waited for: 7 -> 7; matrix products, arithmetic and copies ran while one was open for 3% -> 5% of each run, Pallas kernels for 36% -> 37%
where the time goes in v4:
time: 138 us; the launch traced here: 136 us
  Pallas kernels  62.4 us (45%)
  blocking collectives  24.7 us (18%)
  starting transfers between devices  22.2 us (16%)
  waiting for transfers between devices  18.2 us (13%)
  local copies, waits for them, and re-layouts  6.96 us (5%)
  other arithmetic  1.75 us (1%)
    all_to_all x1, blocking collectives, shards(): received = lax.all_to_all(sent, EVERY, 0, 0, tiled=True)  24.7 us
    pallas_call x2, Pallas kernels, image_of(): pl.pallas_call(functools.partial(image_kernel, group, parts, fill_shapes)...  24.4 us
    ppermute x15, starting transfers between devices, moved(): lax.ppermute(array, axis, [(i, j) for i, j in pairs if 0 <= j < count])  22.2 us
    ppermute x15, waiting for transfers between devices, moved(): lax.ppermute(array, axis, [(i, j) for i, j in pairs if 0 <= j < count])  18.2 us
    pallas_call x1, Pallas kernels, later_image(): pl.pallas_call(functools.partial(later_kernel, len(v_pieces)), out_shape=...  17.2 us
    pallas_call x1, Pallas kernels, last_projected(): pl.pallas_call(functools.partial(last_kernel, len(v_pieces)), out_shape=j...  9.96 us
    pallas_call x1, Pallas kernels, lists_of(): pl.pallas_call(functools.partial(lists_kernel, rows, slots, plan), out_sh...  6.74 us
    pallas_call x2, Pallas kernels, cut(): pl.pallas_call(cut_kernel, out_shape=part, grid_spec=pltpu.PrefetchScalar...  4.09 us
  transfers between devices with their start and end apart: 15, of which 7 were waited for; matrix products, arithmetic and copies ran while one was open for 5% of the time, Pallas kernels for 37%

profile of v4, /device:TPU:0, one launch (start us, length us, event | category | flops | bytes accessed | tf_op | source)
XLA Modules:
  0.0 136.5 jit_solution(16952736121111851624)
XLA Ops:
  0.0 2.0 %cut.2 = bf16[3072,128]{1,0:T(8,128)(2,1)} custom-call(s32[1]{0:T(128)} %bitcast.start_ref, bf16[6144,128]{1,0:T(8,128)(2,1)} %refs_0_.3), custom_call_target="tpu_custom_call" | custom-call | flops 1 | bytes 1 | tf_op jit(solution)/shard_map/cut/pallas_call | solution.py:184
  2.7 0.8 collective-permute-done
  3.9 2.6 %collective-permute-start.2 = (bf16[3072,128]{1,0:T(8,128)(2,1)}, bf16[3072,128]{1,0:T(8,128)(2,1)S(1)}, u32[]{:S(2)}, u32[]{:S(2)}) collective-permute-start(bf16[3072,128]{1,0:T(8,128)(2,1)} %cut.2), channel_id=1, source_target_pairs={{0,2},{1,3},{2,0},{3,1},{4,6},{5,7},{6,4},{7,5},{8,10},{9,11},{10,... | collective-permute-start | bytes 2359304 | tf_op jit(solution)/shard_map/ppermute | solution.py:23
  6.5 1.5 %collective-permute-start.1 = (bf16[3072,128]{1,0:T(8,128)(2,1)}, bf16[3072,128]{1,0:T(8,128)(2,1)S(1)}, u32[]{:S(2)}, u32[]{:S(2)}) collective-permute-start(bf16[3072,128]{1,0:T(8,128)(2,1)} %cut.2), channel_id=1, source_target_pairs={{0,4},{4,0},{8,12},{12,8},{16,20},{20,16},{24,28},{28,24},{1,5},{5... | collective-permute-start | bytes 2359304 | tf_op jit(solution)/shard_map/ppermute | solution.py:23
  8.9 2.1 %cut.3 = bf16[3072,128]{1,0:T(8,128)(2,1)} custom-call(s32[1]{0:T(128)} %bitcast.4.start_ref, bf16[6144,128]{1,0:T(8,128)(2,1)} %refs_0_.3), custom_call_target="tpu_custom_call" | custom-call | flops 1 | bytes 1 | tf_op jit(solution)/shard_map/cut/pallas_call | solution.py:184
  12.4 0.7 reshape.270.codes_ref
  13.1 2.7 %copy.24 = bf16[1536,512]{0,1:T(8,128)(2,1)} copy(bf16[1536,512]{1,0:T(8,128)(2,1)} %param.5) | data formatting | bytes 3145728 | tf_op args[1]
  15.8 6.7 %lists.1 = (s32[1280]{0:T(1024)}, s32[1280]{0:T(1024)}, s32[2]{0:T(128)}) custom-call(s32[2304]{0:T(1024)} %reshape.270.codes_ref), custom_call_target="tpu_custom_call" | custom-call | flops 1 | bytes 1 | tf_op jit(solution)/shard_map/lists/pallas_call | solution.py:243
  23.2 1.9 %collective-permute-done.2.refs_4_.refs_5_ = bf16[3072,128]{1,0:T(8,128)(2,1)S(1)} collective-permute-done((bf16[3072,128]{1,0:T(8,128)(2,1)}, bf16[3072,128]{1,0:T(8,128)(2,1)S(1)}, u32[]{:S(2)}, u32[]{:S(2)}) %collective-permute-start.2) | collective-permute-done | bytes 786464 | tf_op jit(solution)/shard_map/ppermute | solution.py:23
  25.1 2.0 %collective-permute-done.1.refs_1_ = bf16[3072,128]{1,0:T(8,128)(2,1)S(1)} collective-permute-done((bf16[3072,128]{1,0:T(8,128)(2,1)}, bf16[3072,128]{1,0:T(8,128)(2,1)S(1)}, u32[]{:S(2)}, u32[]{:S(2)}) %collective-permute-start.1) | collective-permute-done | bytes 786464 | tf_op jit(solution)/shard_map/ppermute | solution.py:23
  27.1 3.5 %collective-permute-start.6 = (bf16[3072,128]{1,0:T(8,128)(2,1)S(1)}, bf16[3072,128]{1,0:T(8,128)(2,1)S(1)}, u32[]{:S(2)}, u32[]{:S(2)}) collective-permute-start(bf16[3072,128]{1,0:T(8,128)(2,1)S(1)} %collective-permute-done.1.refs_1_), channel_id=1, source_target_pairs={{0,8},{8,16},{12,4},{16,24},{20,12},{28,20},{1,9},{9,17},{13,5},{1... | collective-permute-start | bytes 2359304 | tf_op jit(solution)/shard_map/ppermute | solution.py:23
  30.6 11.1 %collective-permute-done.4.refs_5_.refs_6_ = bf16[3072,128]{1,0:T(8,128)(2,1)} collective-permute-done((bf16[3072,128]{1,0:T(8,128)(2,1)}, bf16[3072,128]{1,0:T(8,128)(2,1)}, u32[]{:S(2)}, u32[]{:S(2)}) %collective-permute-start.4) | collective-permute-done | bytes 786464 | tf_op jit(solution)/shard_map/ppermute | solution.py:23
  41.7 1.4 collective-permute-done.3.refs_2_
  43.5 1.6 %collective-permute-start.7 = (bf16[3072,128]{1,0:T(8,128)(2,1)S(1)}, bf16[3072,128]{1,0:T(8,128)(2,1)}, u32[]{:S(2)}, u32[]{:S(2)}) collective-permute-start(bf16[3072,128]{1,0:T(8,128)(2,1)S(1)} %collective-permute-done.2.refs_4_.refs_5_), channel_id=1, source_target_pairs={{0,4},{4,0},{8,12},{12,8},{16,20},{20,16},{24,28},{28,24},{1,5},{5... | collective-permute-start | bytes 2359304 | tf_op jit(solution)/shard_map/ppermute | solution.py:23
  45.1 0.7 collective-permute-done.6.refs_3_
  45.9 5.3 %collective-permute-start.8 = (bf16[3072,128]{1,0:T(8,128)(2,1)S(1)}, bf16[3072,128]{1,0:T(8,128)(2,1)}, u32[]{:S(2)}, u32[]{:S(2)}) collective-permute-start(bf16[3072,128]{1,0:T(8,128)(2,1)S(1)} %collective-permute-done.3.refs_2_), channel_id=1, source_target_pairs={{0,8},{8,16},{12,4},{16,24},{20,12},{28,20},{1,9},{9,17},{13,5},{1... | collective-permute-start | bytes 2359304 | tf_op jit(solution)/shard_map/ppermute | solution.py:23
  51.9 12.0 %image.2.refs_0_ = f32[2,24,128,128]{3,2,1,0:T(8,128)} custom-call(s32[48,24]{1,0:T(8,128)} %pad_add_fusion.cols_ref, s32[10]{0:T(128)} %stack.74.offs_ref, bf16[48,12,128,128]{3,2,1,0:T(8,128)(2,1)} %own_ref.3, bf16[48,12,128,128]{3,2,1,0:T(8,128)(2,1)} %collective-permute-done.5.other_ref, bf16[6144,128]{1,0:T(8,128)(2,1)} %refs_0_.3, ...), custom_call_target="tpu_custom_call" | custom-call | flops 1 | bytes 1 | tf_op jit(solution)/shard_map/image/pallas_call | solution.py:149
  64.1 3.6 %collective-permute-start.11 = (bf16[3072,128]{1,0:T(8,128)(2,1)}, bf16[3072,128]{1,0:T(8,128)(2,1)S(1)}, u32[]{:S(2)}, u32[]{:S(2)}) collective-permute-start(bf16[3072,128]{1,0:T(8,128)(2,1)} %collective-permute-done.7.refs_7_.refs_2_), channel_id=1, source_target_pairs={{0,8},{8,16},{12,4},{16,24},{20,12},{28,20},{1,9},{9,17},{13,5},{1... | collective-permute-start | bytes 2359304 | tf_op jit(solution)/shard_map/ppermute | solution.py:23
  68.4 12.4 %image.3.refs_1_ = f32[2,24,128,128]{3,2,1,0:T(8,128)} custom-call(s32[48,24]{1,0:T(8,128)} %pad_add_fusion.cols_ref, s32[11]{0:T(128)} %stack.75.offs_ref, bf16[48,12,128,128]{3,2,1,0:T(8,128)(2,1)} %own_ref.3, bf16[48,12,128,128]{3,2,1,0:T(8,128)(2,1)} %collective-permute-done.5.other_ref, bf16[6144,128]{1,0:T(8,128)(2,1)} %refs_0_.3, ...), custom_call_target="tpu_custom_call" | custom-call | flops 1 | bytes 1 | tf_op jit(solution)/shard_map/image/pallas_call | solution.py:149
  80.9 1.6 %collective-permute-start.12 = (bf16[3072,128]{1,0:T(8,128)(2,1)}, bf16[3072,128]{1,0:T(8,128)(2,1)}, u32[]{:S(2)}, u32[]{:S(2)}) collective-permute-start(bf16[3072,128]{1,0:T(8,128)(2,1)} %collective-permute-done.4.refs_5_.refs_6_), channel_id=1, source_target_pairs={{4,8},{8,4},{12,16},{16,12},{20,24},{24,20},{5,9},{9,5},{13,17},{1... | collective-permute-start | bytes 2359304 | tf_op jit(solution)/shard_map/ppermute | solution.py:23
  83.0 0.9 copy-done.5
  83.9 17.2 %later.1.refs_2_ = f32[48,128,128]{2,1,0:T(8,128)} custom-call(s32[1280]{0:T(1024)} %get-tuple-element.47.codes_ref, s32[2]{0:T(128)} %get-tuple-element.31.steps_ref, s32[3]{0:T(128)} %pad_add_fusion.2.me_ref, bf16[576,128,128]{2,1,0:T(8,128)(2,1)} %bitcast.21, bf16[576,128,128]{2,1,0:T(8,128)(2,1)} %bitcast.7.other_ref, f32[2,24,128,128]{3,2,1,0:T(8,128)} %image.2.refs_0_, ...), custom_call_target="tpu_custom_call" | custom-call | flops 999999995904 | bytes 1000000000 | tf_op jit(solution)/shard_map/later/pallas_call | solution.py:359
  101.1 10.0 %last_projected.1 = f32[32,2,16,128]{3,2,1,0:T(8,128)} custom-call(s32[1280]{0:T(1024)} %get-tuple-element.29.codes_ref, s32[2]{0:T(128)} %get-tuple-element.31.steps_ref, s32[3]{0:T(128)} %pad_add_fusion.2.me_ref, bf16[576,128,128]{2,1,0:T(8,128)(2,1)} %bitcast.22, bf16[576,128,128]{2,1,0:T(8,128)(2,1)} %bitcast.7.other_ref, ...), custom_call_target="tpu_custom_call" | custom-call | flops 1 | bytes 1 | tf_op jit(solution)/shard_map/last_projected/pallas_call | solution.py:420
  111.1 24.7 %all_to_all.5 = f32[32,2,16,128]{3,2,1,0:T(8,128)S(1)} all-to-all(f32[32,2,16,128]{3,2,1,0:T(8,128)} %last_projected.1), channel_id=1, replica_groups=mesh['region'=8,'col'=4] {'region','col'}, dimensions={0} | all-to-all | bytes 1048576 | tf_op jit(solution)/shard_map/all_to_all | solution.py:517
  (53 shorter events, 7.2 us)
Async XLA Ops:
  0.0 2.0 %copy-start.4 = (s32[48,12]{0,1:T(8,128)S(1)}, s32[48,12]{0,1:T(8,128)}, u32[]{:S(2)}) copy-start(s32[48,12]{0,1:T(8,128)} %param.7) | copy-start | bytes 6916
  2.1 1.4 collective-permute-start
  3.5 39.6 %collective-permute-start.5 = (bf16[48,12,128,128]{3,2,1,0:T(8,128)(2,1)}, bf16[48,12,128,128]{3,2,1,0:T(8,128)(2,1)}, u32[]{:S(2)}, u32[]{:S(2)}) collective-permute-start(bf16[48,12,128,128]{3,2,1,0:T(8,128)(2,1)} %own_ref.3), channel_id=1, source_target_pairs={{0,1},{1,0},{2,3},{3,2},{4,5},{5,4},{6,7},{7,6},{8,9},{9,8},{10,11... | collective-permute-start | bytes 56623112 | tf_op jit(solution)/shard_map/ppermute | solution.py:23
  3.9 21.2 %collective-permute-start.2 = (bf16[3072,128]{1,0:T(8,128)(2,1)}, bf16[3072,128]{1,0:T(8,128)(2,1)S(1)}, u32[]{:S(2)}, u32[]{:S(2)}) collective-permute-start(bf16[3072,128]{1,0:T(8,128)(2,1)} %cut.2), channel_id=1, source_target_pairs={{0,2},{1,3},{2,0},{3,1},{4,6},{5,7},{6,4},{7,5},{8,10},{9,11},{10,... | collective-permute-start | bytes 2359304 | tf_op jit(solution)/shard_map/ppermute | solution.py:23
  6.5 20.6 %collective-permute-start.1 = (bf16[3072,128]{1,0:T(8,128)(2,1)}, bf16[3072,128]{1,0:T(8,128)(2,1)S(1)}, u32[]{:S(2)}, u32[]{:S(2)}) collective-permute-start(bf16[3072,128]{1,0:T(8,128)(2,1)} %cut.2), channel_id=1, source_target_pairs={{0,4},{4,0},{8,12},{12,8},{16,20},{20,16},{24,28},{28,24},{1,5},{5... | collective-permute-start | bytes 2359304 | tf_op jit(solution)/shard_map/ppermute | solution.py:23
  10.9 30.8 %collective-permute-start.4 = (bf16[3072,128]{1,0:T(8,128)(2,1)}, bf16[3072,128]{1,0:T(8,128)(2,1)}, u32[]{:S(2)}, u32[]{:S(2)}) collective-permute-start(bf16[3072,128]{1,0:T(8,128)(2,1)} %cut.3), channel_id=1, source_target_pairs={{0,2},{1,3},{2,0},{3,1},{4,6},{5,7},{6,4},{7,5},{8,10},{9,11},{10,... | collective-permute-start | bytes 2359304 | tf_op jit(solution)/shard_map/ppermute | solution.py:23
  11.5 31.5 %collective-permute-start.3 = (bf16[3072,128]{1,0:T(8,128)(2,1)}, bf16[3072,128]{1,0:T(8,128)(2,1)S(1)}, u32[]{:S(2)}, u32[]{:S(2)}) collective-permute-start(bf16[3072,128]{1,0:T(8,128)(2,1)} %cut.3), channel_id=1, source_target_pairs={{0,4},{4,0},{8,12},{12,8},{16,20},{20,16},{24,28},{28,24},{1,5},{5... | collective-permute-start | bytes 2359304 | tf_op jit(solution)/shard_map/ppermute | solution.py:23
  25.1 26.8 %copy-start = (bf16[3072,128]{1,0:T(8,128)(2,1)}, bf16[3072,128]{1,0:T(8,128)(2,1)S(1)}, u32[]{:S(2)}) copy-start(bf16[3072,128]{1,0:T(8,128)(2,1)S(1)} %collective-permute-done.2.refs_4_.refs_5_) | copy-start | bytes 2359300
  27.1 24.8 %copy-start.1 = (bf16[3072,128]{1,0:T(8,128)(2,1)}, bf16[3072,128]{1,0:T(8,128)(2,1)S(1)}, u32[]{:S(2)}) copy-start(bf16[3072,128]{1,0:T(8,128)(2,1)S(1)} %collective-permute-done.1.refs_1_) | copy-start | bytes 2359300
  27.1 18.8 %collective-permute-start.6 = (bf16[3072,128]{1,0:T(8,128)(2,1)S(1)}, bf16[3072,128]{1,0:T(8,128)(2,1)S(1)}, u32[]{:S(2)}, u32[]{:S(2)}) collective-permute-start(bf16[3072,128]{1,0:T(8,128)(2,1)S(1)} %collective-permute-done.1.refs_1_), channel_id=1, source_target_pairs={{0,8},{8,16},{12,4},{16,24},{20,12},{28,20},{1,9},{9,17},{13,5},{1... | collective-permute-start | bytes 2359304 | tf_op jit(solution)/shard_map/ppermute | solution.py:23
  43.1 8.8 %copy-start.2 = (bf16[3072,128]{1,0:T(8,128)(2,1)}, bf16[3072,128]{1,0:T(8,128)(2,1)S(1)}, u32[]{:S(2)}) copy-start(bf16[3072,128]{1,0:T(8,128)(2,1)S(1)} %collective-permute-done.3.refs_2_) | copy-start | bytes 2359300
  43.1 37.8 %collective-permute-start.9 = (bf16[512,1536]{1,0:T(8,128)(2,1)}, bf16[512,1536]{1,0:T(8,128)(2,1)}, u32[]{:S(2)}, u32[]{:S(2)}) collective-permute-start(bf16[512,1536]{1,0:T(8,128)(2,1)} %bitcast.5.refs_4_), channel_id=1, source_target_pairs={{0,2},{1,3},{2,0},{3,1},{4,6},{5,7},{6,4},{7,5},{8,10},{9,11},{10,... | collective-permute-start | bytes 4718600 | tf_op jit(solution)/shard_map/ppermute | solution.py:23
  43.5 20.6 %collective-permute-start.7 = (bf16[3072,128]{1,0:T(8,128)(2,1)S(1)}, bf16[3072,128]{1,0:T(8,128)(2,1)}, u32[]{:S(2)}, u32[]{:S(2)}) collective-permute-start(bf16[3072,128]{1,0:T(8,128)(2,1)S(1)} %collective-permute-done.2.refs_4_.refs_5_), channel_id=1, source_target_pairs={{0,4},{4,0},{8,12},{12,8},{16,20},{20,16},{24,28},{28,24},{1,5},{5... | collective-permute-start | bytes 2359304 | tf_op jit(solution)/shard_map/ppermute | solution.py:23
  45.9 6.0 %copy-start.3 = (bf16[3072,128]{1,0:T(8,128)(2,1)}, bf16[3072,128]{1,0:T(8,128)(2,1)S(1)}, u32[]{:S(2)}) copy-start(bf16[3072,128]{1,0:T(8,128)(2,1)S(1)} %collective-permute-done.6.refs_3_) | copy-start | bytes 2359300
  45.9 22.5 %collective-permute-start.8 = (bf16[3072,128]{1,0:T(8,128)(2,1)S(1)}, bf16[3072,128]{1,0:T(8,128)(2,1)}, u32[]{:S(2)}, u32[]{:S(2)}) collective-permute-start(bf16[3072,128]{1,0:T(8,128)(2,1)S(1)} %collective-permute-done.3.refs_2_), channel_id=1, source_target_pairs={{0,8},{8,16},{12,4},{16,24},{20,12},{28,20},{1,9},{9,17},{13,5},{1... | collective-permute-start | bytes 2359304 | tf_op jit(solution)/shard_map/ppermute | solution.py:23
  51.9 31.1 %collective-permute-start.10 = (bf16[3072,128]{1,0:T(8,128)(2,1)}, bf16[3072,128]{1,0:T(8,128)(2,1)}, u32[]{:S(2)}, u32[]{:S(2)}) collective-permute-start(bf16[3072,128]{1,0:T(8,128)(2,1)} %collective-permute-done.4.refs_5_.refs_6_), channel_id=1, source_target_pairs={{0,4},{4,0},{8,12},{12,8},{16,20},{20,16},{24,28},{28,24},{1,5},{5... | collective-permute-start | bytes 2359304 | tf_op jit(solution)/shard_map/ppermute | solution.py:23
  64.1 18.8 %collective-permute-start.11 = (bf16[3072,128]{1,0:T(8,128)(2,1)}, bf16[3072,128]{1,0:T(8,128)(2,1)S(1)}, u32[]{:S(2)}, u32[]{:S(2)}) collective-permute-start(bf16[3072,128]{1,0:T(8,128)(2,1)} %collective-permute-done.7.refs_7_.refs_2_), channel_id=1, source_target_pairs={{0,8},{8,16},{12,4},{16,24},{20,12},{28,20},{1,9},{9,17},{13,5},{1... | collective-permute-start | bytes 2359304 | tf_op jit(solution)/shard_map/ppermute | solution.py:23
  80.9 20.2 %collective-permute-start.12 = (bf16[3072,128]{1,0:T(8,128)(2,1)}, bf16[3072,128]{1,0:T(8,128)(2,1)}, u32[]{:S(2)}, u32[]{:S(2)}) collective-permute-start(bf16[3072,128]{1,0:T(8,128)(2,1)} %collective-permute-done.4.refs_5_.refs_6_), channel_id=1, source_target_pairs={{4,8},{8,4},{12,16},{16,12},{20,24},{24,20},{5,9},{9,5},{13,17},{1... | collective-permute-start | bytes 2359304 | tf_op jit(solution)/shard_map/ppermute | solution.py:23
  82.5 18.6 %collective-permute-start.13 = (bf16[512,1536]{1,0:T(8,128)(2,1)}, bf16[512,1536]{1,0:T(8,128)(2,1)}, u32[]{:S(2)}, u32[]{:S(2)}) collective-permute-start(bf16[512,1536]{1,0:T(8,128)(2,1)} %bitcast.5.refs_4_), channel_id=1, source_target_pairs={{0,1},{1,0},{2,3},{3,2},{4,5},{5,4},{6,7},{7,6},{8,9},{9,8},{10,11... | collective-permute-start | bytes 4718600 | tf_op jit(solution)/shard_map/ppermute | solution.py:23
  82.5 18.6 %collective-permute-start.14 = (bf16[512,1536]{1,0:T(8,128)(2,1)}, bf16[512,1536]{1,0:T(8,128)(2,1)}, u32[]{:S(2)}, u32[]{:S(2)}) collective-permute-start(bf16[512,1536]{1,0:T(8,128)(2,1)} %collective-permute-done.9.refs_6_), channel_id=1, source_target_pairs={{0,1},{1,0},{2,3},{3,2},{4,5},{5,4},{6,7},{7,6},{8,9},{9,8},{10,11... | collective-permute-start | bytes 4718600 | tf_op jit(solution)/shard_map/ppermute | solution.py:23
  83.0 0.9 copy-start.5

commit v5 on v4

--- a/solution.py
+++ b/solution.py
@@ -8,7 +8,7 @@
 from jax.sharding import PartitionSpec as P
 
 EVERY = ("region", "col")
-VMEM = 60 * 2**20
+VMEM = 34 * 2**20
 PAIR = 2
 LANES = 8
 DEPTH = 5
@@ -483,7 +483,7 @@
     far_a, near_side_a = onward(near_a), to_near(side_a)
 
     near_b, side_b, other = together(near_b, side_b, other)
-    far_b, near_side_b = onward(after(near_b, far_a)), to_near(side_b)
+    far_b, near_side_b = onward(near_b), to_near(after(side_b, far_a))
     w_side = to_side(after(w_own, near_b))
     pieces = [basis_v, near_a, near_b, far_a, side_a, side_b]
     at = [jnp.int32(rows), *near_at, far_at[0], *own_at]

time: 138 us -> 132 us (0.957)
  Pallas kernels: 62.4 us -> 50.7 us
  blocking collectives: 24.7 us -> 29.7 us
  waiting for transfers between devices: 18.2 us -> 20.1 us
    pallas_call x1, Pallas kernels: 17.2 us -> 11.1 us  [later_image(): pl.pallas_call(functools.partial(later_kernel, len(v_pieces)), out_shape=...]
    all_to_all x1, blocking collectives: 24.7 us -> 29.7 us  [shards(): received = lax.all_to_all(sent, EVERY, 0, 0, tiled=True)]
    pallas_call x2, Pallas kernels: 24.4 us -> 21.7 us  [image_of(): pl.pallas_call(functools.partial(image_kernel, group, parts, fill_shapes)...]
    pallas_call x1, Pallas kernels: 9.96 us -> 7.29 us  [last_projected(): pl.pallas_call(functools.partial(last_kernel, len(v_pieces)), out_shape=j...]
    ppermute x15, waiting for transfers between devices: 18.2 us -> 20.1 us  [moved(): lax.ppermute(array, axis, [(i, j) for i, j in pairs if 0 <= j < count])]
    unnamed x13 -> x15, local copies, waits for them, and re-layouts: 3.56 us -> 4.42 us
  transfers between devices with their start and end apart: 15 -> 15, of which waited for: 7 -> 6; matrix products, arithmetic and copies ran while one was open for 5% -> 4% of each run, Pallas kernels for 37% -> 32%
where the time goes in v5:
time: 132 us; the launch traced here: 131 us
  Pallas kernels  50.7 us (38%)
  blocking collectives  29.7 us (22%)
  starting transfers between devices  23.1 us (18%)
  waiting for transfers between devices  20.1 us (15%)
  local copies, waits for them, and re-layouts  6.63 us (5%)
    all_to_all x1, blocking collectives, shards(): received = lax.all_to_all(sent, EVERY, 0, 0, tiled=True)  29.7 us
    ppermute x15, starting transfers between devices, moved(): lax.ppermute(array, axis, [(i, j) for i, j in pairs if 0 <= j < count])  23.1 us
    pallas_call x2, Pallas kernels, image_of(): pl.pallas_call(functools.partial(image_kernel, group, parts, fill_shapes)...  21.7 us
    ppermute x15, waiting for transfers between devices, moved(): lax.ppermute(array, axis, [(i, j) for i, j in pairs if 0 <= j < count])  20.1 us
    pallas_call x1, Pallas kernels, later_image(): pl.pallas_call(functools.partial(later_kernel, len(v_pieces)), out_shape=...  11.1 us
    pallas_call x1, Pallas kernels, last_projected(): pl.pallas_call(functools.partial(last_kernel, len(v_pieces)), out_shape=j...  7.29 us
    pallas_call x1, Pallas kernels, lists_of(): pl.pallas_call(functools.partial(lists_kernel, rows, slots, plan), out_sh...  6.48 us
    unnamed x15, local copies, waits for them, and re-layouts  4.42 us
  transfers between devices with their start and end apart: 15, of which 6 were waited for; matrix products, arithmetic and copies ran while one was open for 4% of the time, Pallas kernels for 32%

profile of v5, /device:TPU:0, one launch (start us, length us, event | category | flops | bytes accessed | tf_op | source)
XLA Modules:
  0.0 131.1 jit_solution(13224109095713792876)
XLA Ops:
  0.0 2.0 %cut.2 = bf16[3072,128]{1,0:T(8,128)(2,1)} custom-call(s32[1]{0:T(128)} %bitcast.start_ref, bf16[6144,128]{1,0:T(8,128)(2,1)} %refs_0_.3), custom_call_target="tpu_custom_call" | custom-call | flops 1 | bytes 1 | tf_op jit(solution)/shard_map/cut/pallas_call | solution.py:184
  2.7 0.8 collective-permute-done
  3.9 2.6 %collective-permute-start.2 = (bf16[3072,128]{1,0:T(8,128)(2,1)}, bf16[3072,128]{1,0:T(8,128)(2,1)S(1)}, u32[]{:S(2)}, u32[]{:S(2)}) collective-permute-start(bf16[3072,128]{1,0:T(8,128)(2,1)} %cut.2), channel_id=1, source_target_pairs={{0,2},{1,3},{2,0},{3,1},{4,6},{5,7},{6,4},{7,5},{8,10},{9,11},{10,... | collective-permute-start | bytes 2359304 | tf_op jit(solution)/shard_map/ppermute | solution.py:23
  6.5 1.5 %collective-permute-start.1 = (bf16[3072,128]{1,0:T(8,128)(2,1)}, bf16[3072,128]{1,0:T(8,128)(2,1)S(1)}, u32[]{:S(2)}, u32[]{:S(2)}) collective-permute-start(bf16[3072,128]{1,0:T(8,128)(2,1)} %cut.2), channel_id=1, source_target_pairs={{0,4},{4,0},{8,12},{12,8},{16,20},{20,16},{24,28},{28,24},{1,5},{5... | collective-permute-start | bytes 2359304 | tf_op jit(solution)/shard_map/ppermute | solution.py:23
  8.3 2.1 %cut.3 = bf16[3072,128]{1,0:T(8,128)(2,1)} custom-call(s32[1]{0:T(128)} %bitcast.4.start_ref, bf16[6144,128]{1,0:T(8,128)(2,1)} %refs_0_.3), custom_call_target="tpu_custom_call" | custom-call | flops 1 | bytes 1 | tf_op jit(solution)/shard_map/cut/pallas_call | solution.py:184
  11.9 0.7 reshape.270.codes_ref
  12.6 2.7 %copy.24 = bf16[1536,512]{0,1:T(8,128)(2,1)} copy(bf16[1536,512]{1,0:T(8,128)(2,1)} %param.5) | data formatting | bytes 3145728 | tf_op args[1]
  15.3 6.5 %lists.1 = (s32[1280]{0:T(1024)}, s32[1280]{0:T(1024)}, s32[2]{0:T(128)}) custom-call(s32[2304]{0:T(1024)} %reshape.270.codes_ref), custom_call_target="tpu_custom_call" | custom-call | flops 1 | bytes 1 | tf_op jit(solution)/shard_map/lists/pallas_call | solution.py:243
  21.9 3.3 %collective-permute-done.2.refs_4_.refs_5_ = bf16[3072,128]{1,0:T(8,128)(2,1)S(1)} collective-permute-done((bf16[3072,128]{1,0:T(8,128)(2,1)}, bf16[3072,128]{1,0:T(8,128)(2,1)S(1)}, u32[]{:S(2)}, u32[]{:S(2)}) %collective-permute-start.2) | collective-permute-done | bytes 786464 | tf_op jit(solution)/shard_map/ppermute | solution.py:23
  25.1 2.0 %collective-permute-done.1.refs_1_ = bf16[3072,128]{1,0:T(8,128)(2,1)S(1)} collective-permute-done((bf16[3072,128]{1,0:T(8,128)(2,1)}, bf16[3072,128]{1,0:T(8,128)(2,1)S(1)}, u32[]{:S(2)}, u32[]{:S(2)}) %collective-permute-start.1) | collective-permute-done | bytes 786464 | tf_op jit(solution)/shard_map/ppermute | solution.py:23
  27.1 4.4 %collective-permute-start.6 = (bf16[3072,128]{1,0:T(8,128)(2,1)S(1)}, bf16[3072,128]{1,0:T(8,128)(2,1)}, u32[]{:S(2)}, u32[]{:S(2)}) collective-permute-start(bf16[3072,128]{1,0:T(8,128)(2,1)S(1)} %collective-permute-done.1.refs_1_), channel_id=1, source_target_pairs={{0,8},{8,16},{12,4},{16,24},{20,12},{28,20},{1,9},{9,17},{13,5},{1... | collective-permute-start | bytes 2359304 | tf_op jit(solution)/shard_map/ppermute | solution.py:23
  31.5 10.3 %collective-permute-done.4.refs_5_.refs_6_ = bf16[3072,128]{1,0:T(8,128)(2,1)} collective-permute-done((bf16[3072,128]{1,0:T(8,128)(2,1)}, bf16[3072,128]{1,0:T(8,128)(2,1)}, u32[]{:S(2)}, u32[]{:S(2)}) %collective-permute-start.4) | collective-permute-done | bytes 786464 | tf_op jit(solution)/shard_map/ppermute | solution.py:23
  41.7 1.5 %collective-permute-done.3.refs_2_ = bf16[3072,128]{1,0:T(8,128)(2,1)} collective-permute-done((bf16[3072,128]{1,0:T(8,128)(2,1)}, bf16[3072,128]{1,0:T(8,128)(2,1)}, u32[]{:S(2)}, u32[]{:S(2)}) %collective-permute-start.3) | collective-permute-done | bytes 786464 | tf_op jit(solution)/shard_map/ppermute | solution.py:23
  43.6 1.7 %collective-permute-start.7 = (bf16[3072,128]{1,0:T(8,128)(2,1)S(1)}, bf16[3072,128]{1,0:T(8,128)(2,1)}, u32[]{:S(2)}, u32[]{:S(2)}) collective-permute-start(bf16[3072,128]{1,0:T(8,128)(2,1)S(1)} %collective-permute-done.2.refs_4_.refs_5_), channel_id=1, source_target_pairs={{0,4},{4,0},{8,12},{12,8},{16,20},{20,16},{24,28},{28,24},{1,5},{5... | collective-permute-start | bytes 2359304 | tf_op jit(solution)/shard_map/ppermute | solution.py:23
  45.4 4.4 %collective-permute-start.8 = (bf16[3072,128]{1,0:T(8,128)(2,1)}, bf16[3072,128]{1,0:T(8,128)(2,1)}, u32[]{:S(2)}, u32[]{:S(2)}) collective-permute-start(bf16[3072,128]{1,0:T(8,128)(2,1)} %collective-permute-done.3.refs_2_), channel_id=1, source_target_pairs={{0,8},{8,16},{12,4},{16,24},{20,12},{28,20},{1,9},{9,17},{13,5},{1... | collective-permute-start | bytes 2359304 | tf_op jit(solution)/shard_map/ppermute | solution.py:23
  49.8 10.4 %image.2.refs_0_ = f32[2,24,128,128]{3,2,1,0:T(8,128)S(1)} custom-call(s32[48,24]{1,0:T(8,128)S(1)} %pad_add_fusion.cols_ref, s32[10]{0:T(128)S(1)} %stack.74.offs_ref, bf16[48,12,128,128]{3,2,1,0:T(8,128)(2,1)} %own_ref.3, bf16[48,12,128,128]{3,2,1,0:T(8,128)(2,1)} %collective-permute-done.5.other_ref, bf16[6144,128]{1,0:T(8,128)(2,1)S(1)} %copy-done, ...), custom_call_target="tpu_custom_call" | custom-call | flops 1 | bytes 1 | tf_op jit(solution)/shard_map/image/pallas_call | solution.py:149
  60.2 1.7 %copy-done.1 = f32[2,24,128,128]{3,2,1,0:T(8,128)} copy-done((f32[2,24,128,128]{3,2,1,0:T(8,128)}, f32[2,24,128,128]{3,2,1,0:T(8,128)S(1)}, u32[]{:S(2)}) %copy-start.1) | copy-done | bytes 3145752
  61.9 2.3 %collective-permute-done.7.refs_7_.refs_2_ = bf16[3072,128]{1,0:T(8,128)(2,1)} collective-permute-done((bf16[3072,128]{1,0:T(8,128)(2,1)S(1)}, bf16[3072,128]{1,0:T(8,128)(2,1)}, u32[]{:S(2)}, u32[]{:S(2)}) %collective-permute-start.7) | collective-permute-done | bytes 786464 | tf_op jit(solution)/shard_map/ppermute | solution.py:23
  64.1 4.6 %collective-permute-start.11 = (bf16[3072,128]{1,0:T(8,128)(2,1)}, bf16[3072,128]{1,0:T(8,128)(2,1)}, u32[]{:S(2)}, u32[]{:S(2)}) collective-permute-start(bf16[3072,128]{1,0:T(8,128)(2,1)} %collective-permute-done.7.refs_7_.refs_2_), channel_id=1, source_target_pairs={{0,8},{8,16},{12,4},{16,24},{20,12},{28,20},{1,9},{9,17},{13,5},{1... | collective-permute-start | bytes 2359304 | tf_op jit(solution)/shard_map/ppermute | solution.py:23
  68.8 11.3 %image.3.refs_1_ = f32[2,24,128,128]{3,2,1,0:T(8,128)S(1)} custom-call(s32[48,24]{1,0:T(8,128)S(1)} %pad_add_fusion.cols_ref, s32[11]{0:T(128)S(1)} %stack.75.offs_ref, bf16[48,12,128,128]{3,2,1,0:T(8,128)(2,1)} %own_ref.3, bf16[48,12,128,128]{3,2,1,0:T(8,128)(2,1)} %collective-permute-done.5.other_ref, bf16[6144,128]{1,0:T(8,128)(2,1)S(1)} %copy-done, ...), custom_call_target="tpu_custom_call" | custom-call | flops 1 | bytes 1 | tf_op jit(solution)/shard_map/image/pallas_call | solution.py:149
  80.1 1.6 %collective-permute-start.12 = (bf16[3072,128]{1,0:T(8,128)(2,1)}, bf16[3072,128]{1,0:T(8,128)(2,1)}, u32[]{:S(2)}, u32[]{:S(2)}) collective-permute-start(bf16[3072,128]{1,0:T(8,128)(2,1)} %collective-permute-done.4.refs_5_.refs_6_), channel_id=1, source_target_pairs={{4,8},{8,4},{12,16},{16,12},{20,24},{24,20},{5,9},{9,5},{13,17},{1... | collective-permute-start | bytes 2359304 | tf_op jit(solution)/shard_map/ppermute | solution.py:23
  82.3 11.1 %later.1.refs_2_ = f32[48,128,128]{2,1,0:T(8,128)S(1)} custom-call(s32[1280]{0:T(1024)S(1)} %copy-done.5, s32[2]{0:T(128)S(1)} %copy-done.4, s32[3]{0:T(128)S(1)} %pad_add_fusion.2.me_ref, bf16[576,128,128]{2,1,0:T(8,128)(2,1)} %bitcast.21, bf16[576,128,128]{2,1,0:T(8,128)(2,1)} %bitcast.7.other_ref, f32[2,24,128,128]{3,2,1,0:T(8,128)S(1)} %copy-done.2, ...), custom_call_target="tpu_custom_call" | custom-call | flops 999999995904 | bytes 1000000000 | tf_op jit(solution)/shard_map/later/pallas_call | solution.py:359
  93.4 7.3 %last_projected.1 = f32[32,2,16,128]{3,2,1,0:T(8,128)S(1)} custom-call(s32[1280]{0:T(1024)S(1)} %copy-done.3, s32[2]{0:T(128)S(1)} %copy-done.4, s32[3]{0:T(128)S(1)} %pad_add_fusion.2.me_ref, bf16[576,128,128]{2,1,0:T(8,128)(2,1)} %bitcast.22, bf16[576,128,128]{2,1,0:T(8,128)(2,1)} %bitcast.7.other_ref, f32[2,24,128,128]{3,2,1,0:T(8,128)S(1)} %copy-done.2, ...), custom_call_target="tpu_custom_call" | custom-call | flops 1 | bytes 1 | tf_op jit(solution)/shard_map/last_projected/pallas_call | solution.py:420
  100.7 29.7 %all_to_all.5 = f32[32,2,16,128]{3,2,1,0:T(8,128)S(1)} all-to-all(f32[32,2,16,128]{3,2,1,0:T(8,128)S(1)} %last_projected.1), channel_id=1, replica_groups=mesh['region'=8,'col'=4] {'region','col'}, dimensions={0} | all-to-all | bytes 1048576 | tf_op jit(solution)/shard_map/all_to_all | solution.py:517
  (55 shorter events, 4.5 us)
Async XLA Ops:
  0.0 2.1 %copy-start.6 = (s32[48,12]{0,1:T(8,128)S(1)}, s32[48,12]{0,1:T(8,128)}, u32[]{:S(2)}) copy-start(s32[48,12]{0,1:T(8,128)} %param.7) | copy-start | bytes 6916
  2.2 1.4 %collective-permute-start = (s32[48,12]{1,0:T(8,128)S(1)}, s32[48,12]{1,0:T(8,128)S(1)}, u32[]{:S(2)}, u32[]{:S(2)}) collective-permute-start(s32[48,12]{1,0:T(8,128)S(1)} %broadcast_subtract_fusion), channel_id=1, source_target_pairs={{0,1},{1,0},{2,3},{3,2},{4,5},{5,4},{6,7},{7,6},{8,9},{9,8},{10,11... | collective-permute-start | bytes 6920 | tf_op jit(solution)/shard_map/ppermute | solution.py:23
  3.5 39.7 %collective-permute-start.5 = (bf16[48,12,128,128]{3,2,1,0:T(8,128)(2,1)}, bf16[48,12,128,128]{3,2,1,0:T(8,128)(2,1)}, u32[]{:S(2)}, u32[]{:S(2)}) collective-permute-start(bf16[48,12,128,128]{3,2,1,0:T(8,128)(2,1)} %own_ref.3), channel_id=1, source_target_pairs={{0,1},{1,0},{2,3},{3,2},{4,5},{5,4},{6,7},{7,6},{8,9},{9,8},{10,11... | collective-permute-start | bytes 56623112 | tf_op jit(solution)/shard_map/ppermute | solution.py:23
  3.9 21.2 %collective-permute-start.2 = (bf16[3072,128]{1,0:T(8,128)(2,1)}, bf16[3072,128]{1,0:T(8,128)(2,1)S(1)}, u32[]{:S(2)}, u32[]{:S(2)}) collective-permute-start(bf16[3072,128]{1,0:T(8,128)(2,1)} %cut.2), channel_id=1, source_target_pairs={{0,2},{1,3},{2,0},{3,1},{4,6},{5,7},{6,4},{7,5},{8,10},{9,11},{10,... | collective-permute-start | bytes 2359304 | tf_op jit(solution)/shard_map/ppermute | solution.py:23
  6.5 20.6 %collective-permute-start.1 = (bf16[3072,128]{1,0:T(8,128)(2,1)}, bf16[3072,128]{1,0:T(8,128)(2,1)S(1)}, u32[]{:S(2)}, u32[]{:S(2)}) collective-permute-start(bf16[3072,128]{1,0:T(8,128)(2,1)} %cut.2), channel_id=1, source_target_pairs={{0,4},{4,0},{8,12},{12,8},{16,20},{20,16},{24,28},{28,24},{1,5},{5... | collective-permute-start | bytes 2359304 | tf_op jit(solution)/shard_map/ppermute | solution.py:23
  10.4 31.3 %collective-permute-start.4 = (bf16[3072,128]{1,0:T(8,128)(2,1)}, bf16[3072,128]{1,0:T(8,128)(2,1)}, u32[]{:S(2)}, u32[]{:S(2)}) collective-permute-start(bf16[3072,128]{1,0:T(8,128)(2,1)} %cut.3), channel_id=1, source_target_pairs={{0,2},{1,3},{2,0},{3,1},{4,6},{5,7},{6,4},{7,5},{8,10},{9,11},{10,... | collective-permute-start | bytes 2359304 | tf_op jit(solution)/shard_map/ppermute | solution.py:23
  11.0 32.2 %collective-permute-start.3 = (bf16[3072,128]{1,0:T(8,128)(2,1)}, bf16[3072,128]{1,0:T(8,128)(2,1)}, u32[]{:S(2)}, u32[]{:S(2)}) collective-permute-start(bf16[3072,128]{1,0:T(8,128)(2,1)} %cut.3), channel_id=1, source_target_pairs={{0,4},{4,0},{8,12},{12,8},{16,20},{20,16},{24,28},{28,24},{1,5},{5... | collective-permute-start | bytes 2359304 | tf_op jit(solution)/shard_map/ppermute | solution.py:23
  12.6 37.2 %copy-start = (bf16[6144,128]{1,0:T(8,128)(2,1)S(1)}, bf16[6144,128]{1,0:T(8,128)(2,1)}, u32[]{:S(2)}) copy-start(bf16[6144,128]{1,0:T(8,128)(2,1)} %refs_0_.3) | copy-start | bytes 4718596
  27.1 22.6 %collective-permute-start.6 = (bf16[3072,128]{1,0:T(8,128)(2,1)S(1)}, bf16[3072,128]{1,0:T(8,128)(2,1)}, u32[]{:S(2)}, u32[]{:S(2)}) collective-permute-start(bf16[3072,128]{1,0:T(8,128)(2,1)S(1)} %collective-permute-done.1.refs_1_), channel_id=1, source_target_pairs={{0,8},{8,16},{12,4},{16,24},{20,12},{28,20},{1,9},{9,17},{13,5},{1... | collective-permute-start | bytes 2359304 | tf_op jit(solution)/shard_map/ppermute | solution.py:23
  43.2 36.9 %collective-permute-start.9 = (bf16[512,1536]{1,0:T(8,128)(2,1)}, bf16[512,1536]{1,0:T(8,128)(2,1)}, u32[]{:S(2)}, u32[]{:S(2)}) collective-permute-start(bf16[512,1536]{1,0:T(8,128)(2,1)} %bitcast.5.refs_4_), channel_id=1, source_target_pairs={{0,2},{1,3},{2,0},{3,1},{4,6},{5,7},{6,4},{7,5},{8,10},{9,11},{10,... | collective-permute-start | bytes 4718600 | tf_op jit(solution)/shard_map/ppermute | solution.py:23
  43.6 20.6 %collective-permute-start.7 = (bf16[3072,128]{1,0:T(8,128)(2,1)S(1)}, bf16[3072,128]{1,0:T(8,128)(2,1)}, u32[]{:S(2)}, u32[]{:S(2)}) collective-permute-start(bf16[3072,128]{1,0:T(8,128)(2,1)S(1)} %collective-permute-done.2.refs_4_.refs_5_), channel_id=1, source_target_pairs={{0,4},{4,0},{8,12},{12,8},{16,20},{20,16},{24,28},{28,24},{1,5},{5... | collective-permute-start | bytes 2359304 | tf_op jit(solution)/shard_map/ppermute | solution.py:23
  45.4 23.5 %collective-permute-start.8 = (bf16[3072,128]{1,0:T(8,128)(2,1)}, bf16[3072,128]{1,0:T(8,128)(2,1)}, u32[]{:S(2)}, u32[]{:S(2)}) collective-permute-start(bf16[3072,128]{1,0:T(8,128)(2,1)} %collective-permute-done.3.refs_2_), channel_id=1, source_target_pairs={{0,8},{8,16},{12,4},{16,24},{20,12},{28,20},{1,9},{9,17},{13,5},{1... | collective-permute-start | bytes 2359304 | tf_op jit(solution)/shard_map/ppermute | solution.py:23
  49.8 32.5 %collective-permute-start.10 = (bf16[3072,128]{1,0:T(8,128)(2,1)}, bf16[3072,128]{1,0:T(8,128)(2,1)}, u32[]{:S(2)}, u32[]{:S(2)}) collective-permute-start(bf16[3072,128]{1,0:T(8,128)(2,1)} %collective-permute-done.4.refs_5_.refs_6_), channel_id=1, source_target_pairs={{0,4},{4,0},{8,12},{12,8},{16,20},{20,16},{24,28},{28,24},{1,5},{5... | collective-permute-start | bytes 2359304 | tf_op jit(solution)/shard_map/ppermute | solution.py:23
  60.2 1.7 %copy-start.1 = (f32[2,24,128,128]{3,2,1,0:T(8,128)}, f32[2,24,128,128]{3,2,1,0:T(8,128)S(1)}, u32[]{:S(2)}) copy-start(f32[2,24,128,128]{3,2,1,0:T(8,128)S(1)} %image.2.refs_0_) | copy-start | bytes 9437188
  64.1 18.1 %collective-permute-start.11 = (bf16[3072,128]{1,0:T(8,128)(2,1)}, bf16[3072,128]{1,0:T(8,128)(2,1)}, u32[]{:S(2)}, u32[]{:S(2)}) collective-permute-start(bf16[3072,128]{1,0:T(8,128)(2,1)} %collective-permute-done.7.refs_7_.refs_2_), channel_id=1, source_target_pairs={{0,8},{8,16},{12,4},{16,24},{20,12},{28,20},{1,9},{9,17},{13,5},{1... | collective-permute-start | bytes 2359304 | tf_op jit(solution)/shard_map/ppermute | solution.py:23
  68.8 13.4 %copy-start.2 = (f32[2,24,128,128]{3,2,1,0:T(8,128)S(1)}, f32[2,24,128,128]{3,2,1,0:T(8,128)}, u32[]{:S(2)}) copy-start(f32[2,24,128,128]{3,2,1,0:T(8,128)} %copy-done.1) | copy-start | bytes 9437188
  68.8 13.4 %copy-start.4 = (s32[2]{0:T(128)S(1)}, s32[2]{0:T(128)}, u32[]{:S(2)}) copy-start(s32[2]{0:T(128)} %get-tuple-element.31.steps_ref) | copy-start | bytes 28
  68.8 13.4 %copy-start.5 = (s32[1280]{0:T(1024)S(1)}, s32[1280]{0:T(1024)}, u32[]{:S(2)}) copy-start(s32[1280]{0:T(1024)} %get-tuple-element.46.codes_ref) | copy-start | bytes 15364
  80.1 13.2 %collective-permute-start.12 = (bf16[3072,128]{1,0:T(8,128)(2,1)}, bf16[3072,128]{1,0:T(8,128)(2,1)}, u32[]{:S(2)}, u32[]{:S(2)}) collective-permute-start(bf16[3072,128]{1,0:T(8,128)(2,1)} %collective-permute-done.4.refs_5_.refs_6_), channel_id=1, source_target_pairs={{4,8},{8,4},{12,16},{16,12},{20,24},{24,20},{5,9},{9,5},{13,17},{1... | collective-permute-start | bytes 2359304 | tf_op jit(solution)/shard_map/ppermute | solution.py:23
  81.7 11.7 %collective-permute-start.13 = (bf16[512,1536]{1,0:T(8,128)(2,1)}, bf16[512,1536]{1,0:T(8,128)(2,1)}, u32[]{:S(2)}, u32[]{:S(2)}) collective-permute-start(bf16[512,1536]{1,0:T(8,128)(2,1)} %bitcast.5.refs_4_), channel_id=1, source_target_pairs={{0,1},{1,0},{2,3},{3,2},{4,5},{5,4},{6,7},{7,6},{8,9},{9,8},{10,11... | collective-permute-start | bytes 4718600 | tf_op jit(solution)/shard_map/ppermute | solution.py:23
  81.7 11.7 %collective-permute-start.14 = (bf16[512,1536]{1,0:T(8,128)(2,1)}, bf16[512,1536]{1,0:T(8,128)(2,1)}, u32[]{:S(2)}, u32[]{:S(2)}) collective-permute-start(bf16[512,1536]{1,0:T(8,128)(2,1)} %collective-permute-done.9.refs_6_), channel_id=1, source_target_pairs={{0,1},{1,0},{2,3},{3,2},{4,5},{5,4},{6,7},{7,6},{8,9},{9,8},{10,11... | collective-permute-start | bytes 4718600 | tf_op jit(solution)/shard_map/ppermute | solution.py:23
  82.3 11.1 %copy-start.3 = (s32[1280]{0:T(1024)S(1)}, s32[1280]{0:T(1024)}, u32[]{:S(2)}) copy-start(s32[1280]{0:T(1024)} %get-tuple-element.29.codes_ref) | copy-start | bytes 15364

commit v6 on v5

--- a/solution.py
+++ b/solution.py
@@ -35,8 +35,8 @@
     return moved(array, "region", lambda r: r ^ 1)
 
 
-def to_far(array):
-    return moved(array, "region", lambda r: r + 1 if r % 2 else r - 1)
+def beyond(array):
+    return moved(array, "region", lambda r: r + 2 if r % 2 else r - 2)
 
 
 def onward(array):
@@ -169,8 +169,8 @@
     )(cols, offs, own, other, *v_pieces)
 
 
-def cut_kernel(start_ref, v_ref, out_ref, stage, sems):
-    start = pl.multiple_of(start_ref[0] * 128, 128)
+def cut_kernel(block, start_ref, v_ref, out_ref, stage, sems):
+    start = pl.multiple_of(start_ref[0] * block, block)
     read = pltpu.make_async_copy(v_ref.at[pl.ds(start, stage.shape[0])], stage, sems.at[0])
     write = pltpu.make_async_copy(stage, out_ref, sems.at[1])
     read.start()
@@ -179,10 +179,10 @@
     write.wait()
 
 
-def cut(array, start, length):
+def cut(array, start, length, block):
     part = jax.ShapeDtypeStruct((length, array.shape[1]), array.dtype)
     return pl.pallas_call(
-        cut_kernel,
+        functools.partial(cut_kernel, block),
         out_shape=part,
         grid_spec=pltpu.PrefetchScalarGridSpec(
             num_scalar_prefetch=1,
@@ -441,16 +441,17 @@
 def shards(basis_v, basis_w, couplings, coupling_cols):
     rows, slots, block = couplings.shape[:3]
     regions, columns = lax.axis_size("region"), lax.axis_size("col")
+    assert columns == 4 and regions % 2 == 0 and rows * slots <= 1 << BLOCK_BITS
     region, col = lax.axis_index("region"), lax.axis_index("col")
     odd = region % 2
     half = rows // 2
 
-    own_a = cut(basis_v, odd * half, half * block)
+    own_a = cut(basis_v, odd * half, half * block, block)
     near_a, side_a = to_near(own_a), to_side(own_a)
     here = after(coupling_cols, own_a) - (region * rows - rows)
     there = to_core(here)
     other = to_core(after(couplings, there))
-    own_b = cut(after(basis_v, there), (1 - odd) * half, half * block)
+    own_b = cut(after(basis_v, there), (1 - odd) * half, half * block, block)
     near_b, side_b = to_near(own_b), to_side(own_b)
     w_own = basis_w.T
 
@@ -479,11 +480,11 @@
     codes = jnp.where(taken, codes + 1 + piece * half + both % half, 0).reshape(-1)
     (later, last), steps = lists_of(codes, rows, slots, ((0,), (1,)))
 
-    near_a, side_a, steps, cols, me, w_own = together(near_a, side_a, steps, cols, me, w_own)
+    near_a, steps, cols, me, w_own = together(near_a, steps, cols, me, w_own)
     far_a, near_side_a = onward(near_a), to_near(side_a)
 
     near_b, side_b, other = together(near_b, side_b, other)
-    far_b, near_side_b = onward(near_b), to_near(after(side_b, far_a))
+    far_b, passing = onward(near_b), beyond(side_b)
     w_side = to_side(after(w_own, near_b))
     pieces = [basis_v, near_a, near_b, far_a, side_a, side_b]
     at = [jnp.int32(rows), *near_at, far_at[0], *own_at]
@@ -492,8 +493,9 @@
         cols, couplings, other, pieces, at, (0, 0, 0, 0, 1, 1), fills, first, half
     )
 
-    early, near_side_a = together(early, near_side_a)
-    far_side_a = onward(near_side_a)
+    early, near_side_a, passing = together(early, near_side_a, passing)
+    far_side_b = to_near(passing)
+    far_side_a, near_side_b = onward(near_side_a), to_near(after(side_b, passing))
     pieces = [basis_v, near_a, near_b, far_a, far_b, side_a, side_b, near_side_a]
     at = [jnp.int32(rows), *near_at, *far_at, *own_at, near_at[0]]
     fills = [(near_at[1], half, 1), (far_base, rows, 1)]
@@ -501,8 +503,7 @@
         cols, couplings, other, pieces, at, (0, 0, 0, 0, 0, 1, 1, 1), fills, second, half
     )
     images = [early, rest]
-    rest, side_b, w_own, w_side = together(rest, side_b, w_own, w_side)
-    far_side_b = to_far(side_b)
+    rest, w_own, w_side = together(rest, w_own, w_side)
     w_pieces = [w_own, to_core(w_own), w_side, to_core(w_side)]
     images = [early, rest]
     own_list = couplings.reshape(rows * slots, block, block)

time: 132 us -> 129 us (0.977)
  blocking collectives: 29.7 us -> 23 us
  waiting for transfers between devices: 20.1 us -> 24.4 us
    all_to_all x1, blocking collectives: 29.7 us -> 23 us  [shards(): received = lax.all_to_all(sent, EVERY, 0, 0, tiled=True)]
    ppermute x15 -> x16, waiting for transfers between devices: 20.1 us -> 24.4 us  [moved(): lax.ppermute(array, axis, [(i, j) for i, j in pairs if 0 <= j < count])]
    ppermute x15 -> x16, starting transfers between devices: 23.1 us -> 23.5 us  [moved(): lax.ppermute(array, axis, [(i, j) for i, j in pairs if 0 <= j < count])]
  transfers between devices with their start and end apart: 15 -> 16, of which waited for: 6 -> 7; matrix products, arithmetic and copies ran while one was open for 4% -> 4% of each run, Pallas kernels for 32% -> 32%
where the time goes in v6:
time: 129 us
  Pallas kernels  50.9 us (39%)
  waiting for transfers between devices  24.4 us (19%)
  starting transfers between devices  23.5 us (18%)
  blocking collectives  23 us (18%)
  local copies, waits for them, and re-layouts  6.63 us (5%)
    ppermute x16, waiting for transfers between devices, moved(): lax.ppermute(array, axis, [(i, j) for i, j in pairs if 0 <= j < count])  24.4 us
    ppermute x16, starting transfers between devices, moved(): lax.ppermute(array, axis, [(i, j) for i, j in pairs if 0 <= j < count])  23.5 us
    all_to_all x1, blocking collectives, shards(): received = lax.all_to_all(sent, EVERY, 0, 0, tiled=True)  23 us
    pallas_call x2, Pallas kernels, image_of(): pl.pallas_call(functools.partial(image_kernel, group, parts, fill_shapes)...  21.7 us
    pallas_call x1, Pallas kernels, later_image(): pl.pallas_call(functools.partial(later_kernel, len(v_pieces)), out_shape=...  11.1 us
    pallas_call x1, Pallas kernels, last_projected(): pl.pallas_call(functools.partial(last_kernel, len(v_pieces)), out_shape=j...  7.29 us
    pallas_call x1, Pallas kernels, lists_of(): pl.pallas_call(functools.partial(lists_kernel, rows, slots, plan), out_sh...  6.62 us
    unnamed x15, local copies, waits for them, and re-layouts  4.42 us
  transfers between devices with their start and end apart: 16, of which 7 were waited for; matrix products, arithmetic and copies ran while one was open for 4% of the time, Pallas kernels for 32%

profile of v6, /device:TPU:0, one launch (start us, length us, event | category | flops | bytes accessed | tf_op | source)
XLA Modules:
  0.0 129.1 jit_solution(1443367291396629220)
XLA Ops:
  0.0 2.0 %cut.2 = bf16[3072,128]{1,0:T(8,128)(2,1)} custom-call(s32[1]{0:T(128)} %bitcast.start_ref, bf16[6144,128]{1,0:T(8,128)(2,1)} %refs_0_.3), custom_call_target="tpu_custom_call" | custom-call | flops 1 | bytes 1 | tf_op jit(solution)/shard_map/cut/pallas_call | solution.py:184
  2.7 0.8 collective-permute-done
  3.9 2.6 %collective-permute-start.6 = (bf16[3072,128]{1,0:T(8,128)(2,1)}, bf16[3072,128]{1,0:T(8,128)(2,1)S(1)}, u32[]{:S(2)}, u32[]{:S(2)}) collective-permute-start(bf16[3072,128]{1,0:T(8,128)(2,1)} %cut.2), channel_id=1, source_target_pairs={{0,2},{1,3},{2,0},{3,1},{4,6},{5,7},{6,4},{7,5},{8,10},{9,11},{10,... | collective-permute-start | bytes 2359304 | tf_op jit(solution)/shard_map/ppermute | solution.py:23
  6.5 1.5 %collective-permute-start.1 = (bf16[3072,128]{1,0:T(8,128)(2,1)}, bf16[3072,128]{1,0:T(8,128)(2,1)S(1)}, u32[]{:S(2)}, u32[]{:S(2)}) collective-permute-start(bf16[3072,128]{1,0:T(8,128)(2,1)} %cut.2), channel_id=1, source_target_pairs={{0,4},{4,0},{8,12},{12,8},{16,20},{20,16},{24,28},{28,24},{1,5},{5... | collective-permute-start | bytes 2359304 | tf_op jit(solution)/shard_map/ppermute | solution.py:23
  8.3 2.1 %cut.3 = bf16[3072,128]{1,0:T(8,128)(2,1)} custom-call(s32[1]{0:T(128)} %bitcast.4.start_ref, bf16[6144,128]{1,0:T(8,128)(2,1)} %refs_0_.3), custom_call_target="tpu_custom_call" | custom-call | flops 1 | bytes 1 | tf_op jit(solution)/shard_map/cut/pallas_call | solution.py:184
  11.9 0.7 reshape.270.codes_ref
  12.6 2.7 %copy.24 = bf16[1536,512]{0,1:T(8,128)(2,1)} copy(bf16[1536,512]{1,0:T(8,128)(2,1)} %param.5) | data formatting | bytes 3145728 | tf_op args[1]
  15.3 6.6 %lists.1 = (s32[1280]{0:T(1024)}, s32[1280]{0:T(1024)}, s32[2]{0:T(128)}) custom-call(s32[2304]{0:T(1024)} %reshape.270.codes_ref), custom_call_target="tpu_custom_call" | custom-call | flops 1 | bytes 1 | tf_op jit(solution)/shard_map/lists/pallas_call | solution.py:243
  22.0 5.1 %collective-permute-done.1.refs_1_ = bf16[3072,128]{1,0:T(8,128)(2,1)S(1)} collective-permute-done((bf16[3072,128]{1,0:T(8,128)(2,1)}, bf16[3072,128]{1,0:T(8,128)(2,1)S(1)}, u32[]{:S(2)}, u32[]{:S(2)}) %collective-permute-start.1) | collective-permute-done | bytes 786464 | tf_op jit(solution)/shard_map/ppermute | solution.py:23
  27.1 4.4 %collective-permute-start.5 = (bf16[3072,128]{1,0:T(8,128)(2,1)S(1)}, bf16[3072,128]{1,0:T(8,128)(2,1)}, u32[]{:S(2)}, u32[]{:S(2)}) collective-permute-start(bf16[3072,128]{1,0:T(8,128)(2,1)S(1)} %collective-permute-done.1.refs_1_), channel_id=1, source_target_pairs={{0,8},{8,16},{12,4},{16,24},{20,12},{28,20},{1,9},{9,17},{13,5},{1... | collective-permute-start | bytes 2359304 | tf_op jit(solution)/shard_map/ppermute | solution.py:23
  31.5 10.3 %collective-permute-done.3.refs_5_.refs_6_ = bf16[3072,128]{1,0:T(8,128)(2,1)} collective-permute-done((bf16[3072,128]{1,0:T(8,128)(2,1)}, bf16[3072,128]{1,0:T(8,128)(2,1)}, u32[]{:S(2)}, u32[]{:S(2)}) %collective-permute-start.3) | collective-permute-done | bytes 786464 | tf_op jit(solution)/shard_map/ppermute | solution.py:23
  41.7 2.3 %collective-permute-done.2.refs_2_ = bf16[3072,128]{1,0:T(8,128)(2,1)} collective-permute-done((bf16[3072,128]{1,0:T(8,128)(2,1)}, bf16[3072,128]{1,0:T(8,128)(2,1)}, u32[]{:S(2)}, u32[]{:S(2)}) %collective-permute-start.2) | collective-permute-done | bytes 786464 | tf_op jit(solution)/shard_map/ppermute | solution.py:23
  44.1 1.3 collective-permute-start.8
  45.6 5.5 %collective-permute-start.9 = (bf16[3072,128]{1,0:T(8,128)(2,1)}, bf16[3072,128]{1,0:T(8,128)(2,1)}, u32[]{:S(2)}, u32[]{:S(2)}) collective-permute-start(bf16[3072,128]{1,0:T(8,128)(2,1)} %collective-permute-done.2.refs_2_), channel_id=1, source_target_pairs={{0,8},{8,16},{12,4},{16,24},{20,12},{28,20},{1,9},{9,17},{13,5},{1... | collective-permute-start | bytes 2359304 | tf_op jit(solution)/shard_map/ppermute | solution.py:23
  51.1 10.4 %image.2.refs_0_ = f32[2,24,128,128]{3,2,1,0:T(8,128)S(1)} custom-call(s32[48,24]{1,0:T(8,128)S(1)} %pad_add_fusion.cols_ref, s32[10]{0:T(128)S(1)} %stack.74.offs_ref, bf16[48,12,128,128]{3,2,1,0:T(8,128)(2,1)} %own_ref.3, bf16[48,12,128,128]{3,2,1,0:T(8,128)(2,1)} %collective-permute-done.4.other_ref, bf16[6144,128]{1,0:T(8,128)(2,1)S(1)} %copy-done, ...), custom_call_target="tpu_custom_call" | custom-call | flops 1 | bytes 1 | tf_op jit(solution)/shard_map/image/pallas_call | solution.py:149
  61.5 1.7 %copy-done.1 = f32[2,24,128,128]{3,2,1,0:T(8,128)} copy-done((f32[2,24,128,128]{3,2,1,0:T(8,128)}, f32[2,24,128,128]{3,2,1,0:T(8,128)S(1)}, u32[]{:S(2)}) %copy-start.1) | copy-done | bytes 3145752
  63.2 0.9 collective-permute-done.8
  64.7 5.3 %collective-permute-start.12 = (bf16[3072,128]{1,0:T(8,128)(2,1)}, bf16[3072,128]{1,0:T(8,128)(2,1)}, u32[]{:S(2)}, u32[]{:S(2)}) collective-permute-start(bf16[3072,128]{1,0:T(8,128)(2,1)} %collective-permute-done.7.refs_7_.refs_2_), channel_id=1, source_target_pairs={{0,8},{8,16},{12,4},{16,24},{20,12},{28,20},{1,9},{9,17},{13,5},{1... | collective-permute-start | bytes 2359304 | tf_op jit(solution)/shard_map/ppermute | solution.py:23
  70.2 11.3 %image.3.refs_1_ = f32[2,24,128,128]{3,2,1,0:T(8,128)S(1)} custom-call(s32[48,24]{1,0:T(8,128)S(1)} %pad_add_fusion.cols_ref, s32[11]{0:T(128)S(1)} %stack.75.offs_ref, bf16[48,12,128,128]{3,2,1,0:T(8,128)(2,1)} %own_ref.3, bf16[48,12,128,128]{3,2,1,0:T(8,128)(2,1)} %collective-permute-done.4.other_ref, bf16[6144,128]{1,0:T(8,128)(2,1)S(1)} %copy-done, ...), custom_call_target="tpu_custom_call" | custom-call | flops 1 | bytes 1 | tf_op jit(solution)/shard_map/image/pallas_call | solution.py:149
  82.1 2.8 %collective-permute-done.11.refs_3_ = bf16[3072,128]{1,0:T(8,128)(2,1)} collective-permute-done((bf16[3072,128]{1,0:T(8,128)(2,1)}, bf16[3072,128]{1,0:T(8,128)(2,1)}, u32[]{:S(2)}, u32[]{:S(2)}) %collective-permute-start.11) | collective-permute-done | bytes 786464 | tf_op jit(solution)/shard_map/ppermute | solution.py:23
  84.9 11.1 %later.1.refs_2_ = f32[48,128,128]{2,1,0:T(8,128)S(1)} custom-call(s32[1280]{0:T(1024)S(1)} %copy-done.5, s32[2]{0:T(128)S(1)} %copy-done.4, s32[3]{0:T(128)S(1)} %pad_add_fusion.2.me_ref, bf16[576,128,128]{2,1,0:T(8,128)(2,1)} %bitcast.21, bf16[576,128,128]{2,1,0:T(8,128)(2,1)} %bitcast.7.other_ref, f32[2,24,128,128]{3,2,1,0:T(8,128)S(1)} %copy-done.2, ...), custom_call_target="tpu_custom_call" | custom-call | flops 999999995904 | bytes 1000000000 | tf_op jit(solution)/shard_map/later/pallas_call | solution.py:359
  96.0 2.1 %collective-permute-done.13.refs_3_ = bf16[3072,128]{1,0:T(8,128)(2,1)} collective-permute-done((bf16[3072,128]{1,0:T(8,128)(2,1)}, bf16[3072,128]{1,0:T(8,128)(2,1)}, u32[]{:S(2)}, u32[]{:S(2)}) %collective-permute-start.13) | collective-permute-done | bytes 786464 | tf_op jit(solution)/shard_map/ppermute | solution.py:23
  98.1 7.3 %last_projected.1 = f32[32,2,16,128]{3,2,1,0:T(8,128)S(1)} custom-call(s32[1280]{0:T(1024)S(1)} %copy-done.3, s32[2]{0:T(128)S(1)} %copy-done.4, s32[3]{0:T(128)S(1)} %pad_add_fusion.2.me_ref, bf16[576,128,128]{2,1,0:T(8,128)(2,1)} %bitcast.22, bf16[576,128,128]{2,1,0:T(8,128)(2,1)} %bitcast.7.other_ref, f32[2,24,128,128]{3,2,1,0:T(8,128)S(1)} %copy-done.2, ...), custom_call_target="tpu_custom_call" | custom-call | flops 1 | bytes 1 | tf_op jit(solution)/shard_map/last_projected/pallas_call | solution.py:420
  105.4 23.0 %all_to_all.5 = f32[32,2,16,128]{3,2,1,0:T(8,128)S(1)} all-to-all(f32[32,2,16,128]{3,2,1,0:T(8,128)S(1)} %last_projected.1), channel_id=1, replica_groups=mesh['region'=8,'col'=4] {'region','col'}, dimensions={0} | all-to-all | bytes 1048576 | tf_op jit(solution)/shard_map/all_to_all | solution.py:518
  (57 shorter events, 5.0 us)
Async XLA Ops:
  0.0 2.1 %copy-start.6 = (s32[48,12]{0,1:T(8,128)S(1)}, s32[48,12]{0,1:T(8,128)}, u32[]{:S(2)}) copy-start(s32[48,12]{0,1:T(8,128)} %param.7) | copy-start | bytes 6916
  2.2 1.4 %collective-permute-start = (s32[48,12]{1,0:T(8,128)S(1)}, s32[48,12]{1,0:T(8,128)S(1)}, u32[]{:S(2)}, u32[]{:S(2)}) collective-permute-start(s32[48,12]{1,0:T(8,128)S(1)} %broadcast_subtract_fusion), channel_id=1, source_target_pairs={{0,1},{1,0},{2,3},{3,2},{4,5},{5,4},{6,7},{7,6},{8,9},{9,8},{10,11... | collective-permute-start | bytes 6920 | tf_op jit(solution)/shard_map/ppermute | solution.py:23
  3.5 40.6 %collective-permute-start.4 = (bf16[48,12,128,128]{3,2,1,0:T(8,128)(2,1)}, bf16[48,12,128,128]{3,2,1,0:T(8,128)(2,1)}, u32[]{:S(2)}, u32[]{:S(2)}) collective-permute-start(bf16[48,12,128,128]{3,2,1,0:T(8,128)(2,1)} %own_ref.3), channel_id=1, source_target_pairs={{0,1},{1,0},{2,3},{3,2},{4,5},{5,4},{6,7},{7,6},{8,9},{9,8},{10,11... | collective-permute-start | bytes 56623112 | tf_op jit(solution)/shard_map/ppermute | solution.py:23
  3.9 27.6 %collective-permute-start.6 = (bf16[3072,128]{1,0:T(8,128)(2,1)}, bf16[3072,128]{1,0:T(8,128)(2,1)S(1)}, u32[]{:S(2)}, u32[]{:S(2)}) collective-permute-start(bf16[3072,128]{1,0:T(8,128)(2,1)} %cut.2), channel_id=1, source_target_pairs={{0,2},{1,3},{2,0},{3,1},{4,6},{5,7},{6,4},{7,5},{8,10},{9,11},{10,... | collective-permute-start | bytes 2359304 | tf_op jit(solution)/shard_map/ppermute | solution.py:23
  6.5 20.6 %collective-permute-start.1 = (bf16[3072,128]{1,0:T(8,128)(2,1)}, bf16[3072,128]{1,0:T(8,128)(2,1)S(1)}, u32[]{:S(2)}, u32[]{:S(2)}) collective-permute-start(bf16[3072,128]{1,0:T(8,128)(2,1)} %cut.2), channel_id=1, source_target_pairs={{0,4},{4,0},{8,12},{12,8},{16,20},{20,16},{24,28},{28,24},{1,5},{5... | collective-permute-start | bytes 2359304 | tf_op jit(solution)/shard_map/ppermute | solution.py:23
  10.5 31.3 %collective-permute-start.3 = (bf16[3072,128]{1,0:T(8,128)(2,1)}, bf16[3072,128]{1,0:T(8,128)(2,1)}, u32[]{:S(2)}, u32[]{:S(2)}) collective-permute-start(bf16[3072,128]{1,0:T(8,128)(2,1)} %cut.3), channel_id=1, source_target_pairs={{0,2},{1,3},{2,0},{3,1},{4,6},{5,7},{6,4},{7,5},{8,10},{9,11},{10,... | collective-permute-start | bytes 2359304 | tf_op jit(solution)/shard_map/ppermute | solution.py:23
  11.1 33.0 %collective-permute-start.2 = (bf16[3072,128]{1,0:T(8,128)(2,1)}, bf16[3072,128]{1,0:T(8,128)(2,1)}, u32[]{:S(2)}, u32[]{:S(2)}) collective-permute-start(bf16[3072,128]{1,0:T(8,128)(2,1)} %cut.3), channel_id=1, source_target_pairs={{0,4},{4,0},{8,12},{12,8},{16,20},{20,16},{24,28},{28,24},{1,5},{5... | collective-permute-start | bytes 2359304 | tf_op jit(solution)/shard_map/ppermute | solution.py:23
  12.6 38.5 %copy-start = (bf16[6144,128]{1,0:T(8,128)(2,1)S(1)}, bf16[6144,128]{1,0:T(8,128)(2,1)}, u32[]{:S(2)}) copy-start(bf16[6144,128]{1,0:T(8,128)(2,1)} %refs_0_.3) | copy-start | bytes 4718596
  27.1 24.0 %collective-permute-start.5 = (bf16[3072,128]{1,0:T(8,128)(2,1)S(1)}, bf16[3072,128]{1,0:T(8,128)(2,1)}, u32[]{:S(2)}, u32[]{:S(2)}) collective-permute-start(bf16[3072,128]{1,0:T(8,128)(2,1)S(1)} %collective-permute-done.1.refs_1_), channel_id=1, source_target_pairs={{0,8},{8,16},{12,4},{16,24},{20,12},{28,20},{1,9},{9,17},{13,5},{1... | collective-permute-start | bytes 2359304 | tf_op jit(solution)/shard_map/ppermute | solution.py:23
  31.5 31.7 %collective-permute-start.7 = (bf16[3072,128]{1,0:T(8,128)(2,1)S(1)}, bf16[3072,128]{1,0:T(8,128)(2,1)}, u32[]{:S(2)}, u32[]{:S(2)}) collective-permute-start(bf16[3072,128]{1,0:T(8,128)(2,1)S(1)} %collective-permute-done.6.refs_4_.refs_5_), channel_id=1, source_target_pairs={{0,4},{4,0},{8,12},{12,8},{16,20},{20,16},{24,28},{28,24},{1,5},{5... | collective-permute-start | bytes 2359304 | tf_op jit(solution)/shard_map/ppermute | solution.py:23
  44.1 20.0 %collective-permute-start.8 = (bf16[3072,128]{1,0:T(8,128)(2,1)}, bf16[3072,128]{1,0:T(8,128)(2,1)}, u32[]{:S(2)}, u32[]{:S(2)}) collective-permute-start(bf16[3072,128]{1,0:T(8,128)(2,1)} %collective-permute-done.3.refs_5_.refs_6_), channel_id=1, source_target_pairs={{4,12},{8,0},{12,20},{16,8},{20,28},{24,16},{5,13},{9,1},{13,21},{... | collective-permute-start | bytes 2359304 | tf_op jit(solution)/shard_map/ppermute | solution.py:23
  45.4 36.1 %collective-permute-start.10 = (bf16[512,1536]{1,0:T(8,128)(2,1)}, bf16[512,1536]{1,0:T(8,128)(2,1)}, u32[]{:S(2)}, u32[]{:S(2)}) collective-permute-start(bf16[512,1536]{1,0:T(8,128)(2,1)} %bitcast.5.refs_4_), channel_id=1, source_target_pairs={{0,2},{1,3},{2,0},{3,1},{4,6},{5,7},{6,4},{7,5},{8,10},{9,11},{10,... | collective-permute-start | bytes 4718600 | tf_op jit(solution)/shard_map/ppermute | solution.py:23
  45.6 24.6 %collective-permute-start.9 = (bf16[3072,128]{1,0:T(8,128)(2,1)}, bf16[3072,128]{1,0:T(8,128)(2,1)}, u32[]{:S(2)}, u32[]{:S(2)}) collective-permute-start(bf16[3072,128]{1,0:T(8,128)(2,1)} %collective-permute-done.2.refs_2_), channel_id=1, source_target_pairs={{0,8},{8,16},{12,4},{16,24},{20,12},{28,20},{1,9},{9,17},{13,5},{1... | collective-permute-start | bytes 2359304 | tf_op jit(solution)/shard_map/ppermute | solution.py:23
  61.5 1.7 %copy-start.1 = (f32[2,24,128,128]{3,2,1,0:T(8,128)}, f32[2,24,128,128]{3,2,1,0:T(8,128)S(1)}, u32[]{:S(2)}) copy-start(f32[2,24,128,128]{3,2,1,0:T(8,128)S(1)} %image.2.refs_0_) | copy-start | bytes 9437188
  64.1 20.8 %collective-permute-start.11 = (bf16[3072,128]{1,0:T(8,128)(2,1)}, bf16[3072,128]{1,0:T(8,128)(2,1)}, u32[]{:S(2)}, u32[]{:S(2)}) collective-permute-start(bf16[3072,128]{1,0:T(8,128)(2,1)} %collective-permute-done.3.refs_5_.refs_6_), channel_id=1, source_target_pairs={{0,4},{4,0},{8,12},{12,8},{16,20},{20,16},{24,28},{28,24},{1,5},{5... | collective-permute-start | bytes 2359304 | tf_op jit(solution)/shard_map/ppermute | solution.py:23
  64.7 20.2 %collective-permute-start.12 = (bf16[3072,128]{1,0:T(8,128)(2,1)}, bf16[3072,128]{1,0:T(8,128)(2,1)}, u32[]{:S(2)}, u32[]{:S(2)}) collective-permute-start(bf16[3072,128]{1,0:T(8,128)(2,1)} %collective-permute-done.7.refs_7_.refs_2_), channel_id=1, source_target_pairs={{0,8},{8,16},{12,4},{16,24},{20,12},{28,20},{1,9},{9,17},{13,5},{1... | collective-permute-start | bytes 2359304 | tf_op jit(solution)/shard_map/ppermute | solution.py:23
  70.1 14.8 %copy-start.2 = (f32[2,24,128,128]{3,2,1,0:T(8,128)S(1)}, f32[2,24,128,128]{3,2,1,0:T(8,128)}, u32[]{:S(2)}) copy-start(f32[2,24,128,128]{3,2,1,0:T(8,128)} %copy-done.1) | copy-start | bytes 9437188
  70.1 14.8 %copy-start.4 = (s32[2]{0:T(128)S(1)}, s32[2]{0:T(128)}, u32[]{:S(2)}) copy-start(s32[2]{0:T(128)} %get-tuple-element.30.steps_ref) | copy-start | bytes 28
  70.1 14.8 %copy-start.5 = (s32[1280]{0:T(1024)S(1)}, s32[1280]{0:T(1024)}, u32[]{:S(2)}) copy-start(s32[1280]{0:T(1024)} %get-tuple-element.44.codes_ref) | copy-start | bytes 15364
  70.1 28.0 %collective-permute-start.13 = (bf16[3072,128]{1,0:T(8,128)(2,1)}, bf16[3072,128]{1,0:T(8,128)(2,1)}, u32[]{:S(2)}, u32[]{:S(2)}) collective-permute-start(bf16[3072,128]{1,0:T(8,128)(2,1)} %collective-permute-done.8), channel_id=1, source_target_pairs={{0,4},{4,0},{8,12},{12,8},{16,20},{20,16},{24,28},{28,24},{1,5},{5... | collective-permute-start | bytes 2359304 | tf_op jit(solution)/shard_map/ppermute | solution.py:23
  81.5 16.6 %collective-permute-start.14 = (bf16[512,1536]{1,0:T(8,128)(2,1)}, bf16[512,1536]{1,0:T(8,128)(2,1)}, u32[]{:S(2)}, u32[]{:S(2)}) collective-permute-start(bf16[512,1536]{1,0:T(8,128)(2,1)} %bitcast.5.refs_4_), channel_id=1, source_target_pairs={{0,1},{1,0},{2,3},{3,2},{4,5},{5,4},{6,7},{7,6},{8,9},{9,8},{10,11... | collective-permute-start | bytes 4718600 | tf_op jit(solution)/shard_map/ppermute | solution.py:23
  81.6 16.6 %collective-permute-start.15 = (bf16[512,1536]{1,0:T(8,128)(2,1)}, bf16[512,1536]{1,0:T(8,128)(2,1)}, u32[]{:S(2)}, u32[]{:S(2)}) collective-permute-start(bf16[512,1536]{1,0:T(8,128)(2,1)} %collective-permute-done.10.refs_6_), channel_id=1, source_target_pairs={{0,1},{1,0},{2,3},{3,2},{4,5},{5,4},{6,7},{7,6},{8,9},{9,8},{10,11... | collective-permute-start | bytes 4718600 | tf_op jit(solution)/shard_map/ppermute | solution.py:23
  84.9 13.2 %copy-start.3 = (s32[1280]{0:T(1024)S(1)}, s32[1280]{0:T(1024)}, u32[]{:S(2)}) copy-start(s32[1280]{0:T(1024)} %get-tuple-element.28.codes_ref) | copy-start | bytes 15364

commit v7 on v6

--- a/solution.py
+++ b/solution.py
@@ -269,7 +269,7 @@
                 block_id = (code >> V_BITS) & ((1 << BLOCK_BITS) - 1)
                 pltpu.make_async_copy(
                     a_ref.at[block_id], blocks.at[slot, s * per_source + n], sems.at[slot]
-                ).start()
+                ).start(priority=s)
 
     for ahead in range(DEPTH - 1):
         @pl.when(ahead < steps)

time: 129 us -> 129 us (level)
  no operation moved by 1% of the time
where the time goes in v7:
time: 129 us
  Pallas kernels  50.2 us (39%)
  waiting for transfers between devices  25 us (19%)
  starting transfers between devices  23.5 us (18%)
  blocking collectives  22.7 us (18%)
  local copies, waits for them, and re-layouts  6.63 us (5%)
    ppermute x16, waiting for transfers between devices, moved(): lax.ppermute(array, axis, [(i, j) for i, j in pairs if 0 <= j < count])  25 us
    ppermute x16, starting transfers between devices, moved(): lax.ppermute(array, axis, [(i, j) for i, j in pairs if 0 <= j < count])  23.5 us
    all_to_all x1, blocking collectives, shards(): received = lax.all_to_all(sent, EVERY, 0, 0, tiled=True)  22.7 us
    pallas_call x2, Pallas kernels, image_of(): pl.pallas_call(functools.partial(image_kernel, group, parts, fill_shapes)...  21.7 us
    pallas_call x1, Pallas kernels, later_image(): pl.pallas_call(functools.partial(later_kernel, len(v_pieces)), out_shape=...  10.5 us
    pallas_call x1, Pallas kernels, last_projected(): pl.pallas_call(functools.partial(last_kernel, len(v_pieces)), out_shape=j...  7.29 us
    pallas_call x1, Pallas kernels, lists_of(): pl.pallas_call(functools.partial(lists_kernel, rows, slots, plan), out_sh...  6.52 us
    unnamed x15, local copies, waits for them, and re-layouts  4.42 us
  transfers between devices with their start and end apart: 16, of which 7 were waited for; matrix products, arithmetic and copies ran while one was open for 4% of the time, Pallas kernels for 32%

profile of v7, /device:TPU:0, one launch (start us, length us, event | category | flops | bytes accessed | tf_op | source)
XLA Modules:
  0.0 128.9 jit_solution(3238284845742846782)
XLA Ops:
  0.0 2.0 %cut.2 = bf16[3072,128]{1,0:T(8,128)(2,1)} custom-call(s32[1]{0:T(128)} %bitcast.start_ref, bf16[6144,128]{1,0:T(8,128)(2,1)} %refs_0_.3), custom_call_target="tpu_custom_call" | custom-call | flops 1 | bytes 1 | tf_op jit(solution)/shard_map/cut/pallas_call | solution.py:184
  2.7 0.8 collective-permute-done
  3.9 2.6 %collective-permute-start.6 = (bf16[3072,128]{1,0:T(8,128)(2,1)}, bf16[3072,128]{1,0:T(8,128)(2,1)S(1)}, u32[]{:S(2)}, u32[]{:S(2)}) collective-permute-start(bf16[3072,128]{1,0:T(8,128)(2,1)} %cut.2), channel_id=1, source_target_pairs={{0,2},{1,3},{2,0},{3,1},{4,6},{5,7},{6,4},{7,5},{8,10},{9,11},{10,... | collective-permute-start | bytes 2359304 | tf_op jit(solution)/shard_map/ppermute | solution.py:23
  6.5 1.5 %collective-permute-start.1 = (bf16[3072,128]{1,0:T(8,128)(2,1)}, bf16[3072,128]{1,0:T(8,128)(2,1)S(1)}, u32[]{:S(2)}, u32[]{:S(2)}) collective-permute-start(bf16[3072,128]{1,0:T(8,128)(2,1)} %cut.2), channel_id=1, source_target_pairs={{0,4},{4,0},{8,12},{12,8},{16,20},{20,16},{24,28},{28,24},{1,5},{5... | collective-permute-start | bytes 2359304 | tf_op jit(solution)/shard_map/ppermute | solution.py:23
  8.3 2.1 %cut.3 = bf16[3072,128]{1,0:T(8,128)(2,1)} custom-call(s32[1]{0:T(128)} %bitcast.4.start_ref, bf16[6144,128]{1,0:T(8,128)(2,1)} %refs_0_.3), custom_call_target="tpu_custom_call" | custom-call | flops 1 | bytes 1 | tf_op jit(solution)/shard_map/cut/pallas_call | solution.py:184
  11.9 0.7 reshape.270.codes_ref
  12.6 2.7 %copy.24 = bf16[1536,512]{0,1:T(8,128)(2,1)} copy(bf16[1536,512]{1,0:T(8,128)(2,1)} %param.5) | data formatting | bytes 3145728 | tf_op args[1]
  15.3 6.5 %lists.1 = (s32[1280]{0:T(1024)}, s32[1280]{0:T(1024)}, s32[2]{0:T(128)}) custom-call(s32[2304]{0:T(1024)} %reshape.270.codes_ref), custom_call_target="tpu_custom_call" | custom-call | flops 1 | bytes 1 | tf_op jit(solution)/shard_map/lists/pallas_call | solution.py:243
  21.9 5.2 %collective-permute-done.1.refs_1_ = bf16[3072,128]{1,0:T(8,128)(2,1)S(1)} collective-permute-done((bf16[3072,128]{1,0:T(8,128)(2,1)}, bf16[3072,128]{1,0:T(8,128)(2,1)S(1)}, u32[]{:S(2)}, u32[]{:S(2)}) %collective-permute-start.1) | collective-permute-done | bytes 786464 | tf_op jit(solution)/shard_map/ppermute | solution.py:23
  27.1 4.4 %collective-permute-start.5 = (bf16[3072,128]{1,0:T(8,128)(2,1)S(1)}, bf16[3072,128]{1,0:T(8,128)(2,1)}, u32[]{:S(2)}, u32[]{:S(2)}) collective-permute-start(bf16[3072,128]{1,0:T(8,128)(2,1)S(1)} %collective-permute-done.1.refs_1_), channel_id=1, source_target_pairs={{0,8},{8,16},{12,4},{16,24},{20,12},{28,20},{1,9},{9,17},{13,5},{1... | collective-permute-start | bytes 2359304 | tf_op jit(solution)/shard_map/ppermute | solution.py:23
  31.5 10.3 %collective-permute-done.3.refs_5_.refs_6_ = bf16[3072,128]{1,0:T(8,128)(2,1)} collective-permute-done((bf16[3072,128]{1,0:T(8,128)(2,1)}, bf16[3072,128]{1,0:T(8,128)(2,1)}, u32[]{:S(2)}, u32[]{:S(2)}) %collective-permute-start.3) | collective-permute-done | bytes 786464 | tf_op jit(solution)/shard_map/ppermute | solution.py:23
  41.7 2.3 %collective-permute-done.2.refs_2_ = bf16[3072,128]{1,0:T(8,128)(2,1)} collective-permute-done((bf16[3072,128]{1,0:T(8,128)(2,1)}, bf16[3072,128]{1,0:T(8,128)(2,1)}, u32[]{:S(2)}, u32[]{:S(2)}) %collective-permute-start.2) | collective-permute-done | bytes 786464 | tf_op jit(solution)/shard_map/ppermute | solution.py:23
  44.1 1.3 collective-permute-start.8
  45.6 5.5 %collective-permute-start.9 = (bf16[3072,128]{1,0:T(8,128)(2,1)}, bf16[3072,128]{1,0:T(8,128)(2,1)}, u32[]{:S(2)}, u32[]{:S(2)}) collective-permute-start(bf16[3072,128]{1,0:T(8,128)(2,1)} %collective-permute-done.2.refs_2_), channel_id=1, source_target_pairs={{0,8},{8,16},{12,4},{16,24},{20,12},{28,20},{1,9},{9,17},{13,5},{1... | collective-permute-start | bytes 2359304 | tf_op jit(solution)/shard_map/ppermute | solution.py:23
  51.1 10.4 %image.2.refs_0_ = f32[2,24,128,128]{3,2,1,0:T(8,128)S(1)} custom-call(s32[48,24]{1,0:T(8,128)S(1)} %pad_add_fusion.cols_ref, s32[10]{0:T(128)S(1)} %stack.74.offs_ref, bf16[48,12,128,128]{3,2,1,0:T(8,128)(2,1)} %own_ref.3, bf16[48,12,128,128]{3,2,1,0:T(8,128)(2,1)} %collective-permute-done.4.other_ref, bf16[6144,128]{1,0:T(8,128)(2,1)S(1)} %copy-done, ...), custom_call_target="tpu_custom_call" | custom-call | flops 1 | bytes 1 | tf_op jit(solution)/shard_map/image/pallas_call | solution.py:149
  61.5 1.7 %copy-done.1 = f32[2,24,128,128]{3,2,1,0:T(8,128)} copy-done((f32[2,24,128,128]{3,2,1,0:T(8,128)}, f32[2,24,128,128]{3,2,1,0:T(8,128)S(1)}, u32[]{:S(2)}) %copy-start.1) | copy-done | bytes 3145752
  63.2 0.9 collective-permute-done.8
  64.7 5.3 %collective-permute-start.12 = (bf16[3072,128]{1,0:T(8,128)(2,1)}, bf16[3072,128]{1,0:T(8,128)(2,1)}, u32[]{:S(2)}, u32[]{:S(2)}) collective-permute-start(bf16[3072,128]{1,0:T(8,128)(2,1)} %collective-permute-done.7.refs_7_.refs_2_), channel_id=1, source_target_pairs={{0,8},{8,16},{12,4},{16,24},{20,12},{28,20},{1,9},{9,17},{13,5},{1... | collective-permute-start | bytes 2359304 | tf_op jit(solution)/shard_map/ppermute | solution.py:23
  70.2 11.3 %image.3.refs_1_ = f32[2,24,128,128]{3,2,1,0:T(8,128)S(1)} custom-call(s32[48,24]{1,0:T(8,128)S(1)} %pad_add_fusion.cols_ref, s32[11]{0:T(128)S(1)} %stack.75.offs_ref, bf16[48,12,128,128]{3,2,1,0:T(8,128)(2,1)} %own_ref.3, bf16[48,12,128,128]{3,2,1,0:T(8,128)(2,1)} %collective-permute-done.4.other_ref, bf16[6144,128]{1,0:T(8,128)(2,1)S(1)} %copy-done, ...), custom_call_target="tpu_custom_call" | custom-call | flops 1 | bytes 1 | tf_op jit(solution)/shard_map/image/pallas_call | solution.py:149
  82.1 2.8 %collective-permute-done.11.refs_3_ = bf16[3072,128]{1,0:T(8,128)(2,1)} collective-permute-done((bf16[3072,128]{1,0:T(8,128)(2,1)}, bf16[3072,128]{1,0:T(8,128)(2,1)}, u32[]{:S(2)}, u32[]{:S(2)}) %collective-permute-start.11) | collective-permute-done | bytes 786464 | tf_op jit(solution)/shard_map/ppermute | solution.py:23
  84.9 10.5 %later.1.refs_2_ = f32[48,128,128]{2,1,0:T(8,128)S(1)} custom-call(s32[1280]{0:T(1024)S(1)} %copy-done.5, s32[2]{0:T(128)S(1)} %copy-done.4, s32[3]{0:T(128)S(1)} %pad_add_fusion.2.me_ref, bf16[576,128,128]{2,1,0:T(8,128)(2,1)} %bitcast.21, bf16[576,128,128]{2,1,0:T(8,128)(2,1)} %bitcast.7.other_ref, f32[2,24,128,128]{3,2,1,0:T(8,128)S(1)} %copy-done.2, ...), custom_call_target="tpu_custom_call" | custom-call | flops 999999995904 | bytes 1000000000 | tf_op jit(solution)/shard_map/later/pallas_call | solution.py:359
  95.5 2.7 %collective-permute-done.13.refs_3_ = bf16[3072,128]{1,0:T(8,128)(2,1)} collective-permute-done((bf16[3072,128]{1,0:T(8,128)(2,1)}, bf16[3072,128]{1,0:T(8,128)(2,1)}, u32[]{:S(2)}, u32[]{:S(2)}) %collective-permute-start.13) | collective-permute-done | bytes 786464 | tf_op jit(solution)/shard_map/ppermute | solution.py:23
  98.1 7.3 %last_projected.1 = f32[32,2,16,128]{3,2,1,0:T(8,128)S(1)} custom-call(s32[1280]{0:T(1024)S(1)} %copy-done.3, s32[2]{0:T(128)S(1)} %copy-done.4, s32[3]{0:T(128)S(1)} %pad_add_fusion.2.me_ref, bf16[576,128,128]{2,1,0:T(8,128)(2,1)} %bitcast.22, bf16[576,128,128]{2,1,0:T(8,128)(2,1)} %bitcast.7.other_ref, f32[2,24,128,128]{3,2,1,0:T(8,128)S(1)} %copy-done.2, ...), custom_call_target="tpu_custom_call" | custom-call | flops 1 | bytes 1 | tf_op jit(solution)/shard_map/last_projected/pallas_call | solution.py:420
  105.4 22.7 %all_to_all.5 = f32[32,2,16,128]{3,2,1,0:T(8,128)S(1)} all-to-all(f32[32,2,16,128]{3,2,1,0:T(8,128)S(1)} %last_projected.1), channel_id=1, replica_groups=mesh['region'=8,'col'=4] {'region','col'}, dimensions={0} | all-to-all | bytes 1048576 | tf_op jit(solution)/shard_map/all_to_all | solution.py:518
  (57 shorter events, 5.0 us)
Async XLA Ops:
  0.0 2.1 %copy-start.6 = (s32[48,12]{0,1:T(8,128)S(1)}, s32[48,12]{0,1:T(8,128)}, u32[]{:S(2)}) copy-start(s32[48,12]{0,1:T(8,128)} %param.7) | copy-start | bytes 6916
  2.2 1.4 %collective-permute-start = (s32[48,12]{1,0:T(8,128)S(1)}, s32[48,12]{1,0:T(8,128)S(1)}, u32[]{:S(2)}, u32[]{:S(2)}) collective-permute-start(s32[48,12]{1,0:T(8,128)S(1)} %broadcast_subtract_fusion), channel_id=1, source_target_pairs={{0,1},{1,0},{2,3},{3,2},{4,5},{5,4},{6,7},{7,6},{8,9},{9,8},{10,11... | collective-permute-start | bytes 6920 | tf_op jit(solution)/shard_map/ppermute | solution.py:23
  3.5 40.6 %collective-permute-start.4 = (bf16[48,12,128,128]{3,2,1,0:T(8,128)(2,1)}, bf16[48,12,128,128]{3,2,1,0:T(8,128)(2,1)}, u32[]{:S(2)}, u32[]{:S(2)}) collective-permute-start(bf16[48,12,128,128]{3,2,1,0:T(8,128)(2,1)} %own_ref.3), channel_id=1, source_target_pairs={{0,1},{1,0},{2,3},{3,2},{4,5},{5,4},{6,7},{7,6},{8,9},{9,8},{10,11... | collective-permute-start | bytes 56623112 | tf_op jit(solution)/shard_map/ppermute | solution.py:23
  3.9 27.6 %collective-permute-start.6 = (bf16[3072,128]{1,0:T(8,128)(2,1)}, bf16[3072,128]{1,0:T(8,128)(2,1)S(1)}, u32[]{:S(2)}, u32[]{:S(2)}) collective-permute-start(bf16[3072,128]{1,0:T(8,128)(2,1)} %cut.2), channel_id=1, source_target_pairs={{0,2},{1,3},{2,0},{3,1},{4,6},{5,7},{6,4},{7,5},{8,10},{9,11},{10,... | collective-permute-start | bytes 2359304 | tf_op jit(solution)/shard_map/ppermute | solution.py:23
  6.5 20.6 %collective-permute-start.1 = (bf16[3072,128]{1,0:T(8,128)(2,1)}, bf16[3072,128]{1,0:T(8,128)(2,1)S(1)}, u32[]{:S(2)}, u32[]{:S(2)}) collective-permute-start(bf16[3072,128]{1,0:T(8,128)(2,1)} %cut.2), channel_id=1, source_target_pairs={{0,4},{4,0},{8,12},{12,8},{16,20},{20,16},{24,28},{28,24},{1,5},{5... | collective-permute-start | bytes 2359304 | tf_op jit(solution)/shard_map/ppermute | solution.py:23
  10.5 31.3 %collective-permute-start.3 = (bf16[3072,128]{1,0:T(8,128)(2,1)}, bf16[3072,128]{1,0:T(8,128)(2,1)}, u32[]{:S(2)}, u32[]{:S(2)}) collective-permute-start(bf16[3072,128]{1,0:T(8,128)(2,1)} %cut.3), channel_id=1, source_target_pairs={{0,2},{1,3},{2,0},{3,1},{4,6},{5,7},{6,4},{7,5},{8,10},{9,11},{10,... | collective-permute-start | bytes 2359304 | tf_op jit(solution)/shard_map/ppermute | solution.py:23
  11.1 33.0 %collective-permute-start.2 = (bf16[3072,128]{1,0:T(8,128)(2,1)}, bf16[3072,128]{1,0:T(8,128)(2,1)}, u32[]{:S(2)}, u32[]{:S(2)}) collective-permute-start(bf16[3072,128]{1,0:T(8,128)(2,1)} %cut.3), channel_id=1, source_target_pairs={{0,4},{4,0},{8,12},{12,8},{16,20},{20,16},{24,28},{28,24},{1,5},{5... | collective-permute-start | bytes 2359304 | tf_op jit(solution)/shard_map/ppermute | solution.py:23
  12.6 38.5 %copy-start = (bf16[6144,128]{1,0:T(8,128)(2,1)S(1)}, bf16[6144,128]{1,0:T(8,128)(2,1)}, u32[]{:S(2)}) copy-start(bf16[6144,128]{1,0:T(8,128)(2,1)} %refs_0_.3) | copy-start | bytes 4718596
  27.1 24.0 %collective-permute-start.5 = (bf16[3072,128]{1,0:T(8,128)(2,1)S(1)}, bf16[3072,128]{1,0:T(8,128)(2,1)}, u32[]{:S(2)}, u32[]{:S(2)}) collective-permute-start(bf16[3072,128]{1,0:T(8,128)(2,1)S(1)} %collective-permute-done.1.refs_1_), channel_id=1, source_target_pairs={{0,8},{8,16},{12,4},{16,24},{20,12},{28,20},{1,9},{9,17},{13,5},{1... | collective-permute-start | bytes 2359304 | tf_op jit(solution)/shard_map/ppermute | solution.py:23
  31.5 31.7 %collective-permute-start.7 = (bf16[3072,128]{1,0:T(8,128)(2,1)S(1)}, bf16[3072,128]{1,0:T(8,128)(2,1)}, u32[]{:S(2)}, u32[]{:S(2)}) collective-permute-start(bf16[3072,128]{1,0:T(8,128)(2,1)S(1)} %collective-permute-done.6.refs_4_.refs_5_), channel_id=1, source_target_pairs={{0,4},{4,0},{8,12},{12,8},{16,20},{20,16},{24,28},{28,24},{1,5},{5... | collective-permute-start | bytes 2359304 | tf_op jit(solution)/shard_map/ppermute | solution.py:23
  44.1 20.0 %collective-permute-start.8 = (bf16[3072,128]{1,0:T(8,128)(2,1)}, bf16[3072,128]{1,0:T(8,128)(2,1)}, u32[]{:S(2)}, u32[]{:S(2)}) collective-permute-start(bf16[3072,128]{1,0:T(8,128)(2,1)} %collective-permute-done.3.refs_5_.refs_6_), channel_id=1, source_target_pairs={{4,12},{8,0},{12,20},{16,8},{20,28},{24,16},{5,13},{9,1},{13,21},{... | collective-permute-start | bytes 2359304 | tf_op jit(solution)/shard_map/ppermute | solution.py:23
  45.4 36.1 %collective-permute-start.10 = (bf16[512,1536]{1,0:T(8,128)(2,1)}, bf16[512,1536]{1,0:T(8,128)(2,1)}, u32[]{:S(2)}, u32[]{:S(2)}) collective-permute-start(bf16[512,1536]{1,0:T(8,128)(2,1)} %bitcast.5.refs_4_), channel_id=1, source_target_pairs={{0,2},{1,3},{2,0},{3,1},{4,6},{5,7},{6,4},{7,5},{8,10},{9,11},{10,... | collective-permute-start | bytes 4718600 | tf_op jit(solution)/shard_map/ppermute | solution.py:23
  45.6 24.6 %collective-permute-start.9 = (bf16[3072,128]{1,0:T(8,128)(2,1)}, bf16[3072,128]{1,0:T(8,128)(2,1)}, u32[]{:S(2)}, u32[]{:S(2)}) collective-permute-start(bf16[3072,128]{1,0:T(8,128)(2,1)} %collective-permute-done.2.refs_2_), channel_id=1, source_target_pairs={{0,8},{8,16},{12,4},{16,24},{20,12},{28,20},{1,9},{9,17},{13,5},{1... | collective-permute-start | bytes 2359304 | tf_op jit(solution)/shard_map/ppermute | solution.py:23
  61.5 1.7 %copy-start.1 = (f32[2,24,128,128]{3,2,1,0:T(8,128)}, f32[2,24,128,128]{3,2,1,0:T(8,128)S(1)}, u32[]{:S(2)}) copy-start(f32[2,24,128,128]{3,2,1,0:T(8,128)S(1)} %image.2.refs_0_) | copy-start | bytes 9437188
  64.1 20.8 %collective-permute-start.11 = (bf16[3072,128]{1,0:T(8,128)(2,1)}, bf16[3072,128]{1,0:T(8,128)(2,1)}, u32[]{:S(2)}, u32[]{:S(2)}) collective-permute-start(bf16[3072,128]{1,0:T(8,128)(2,1)} %collective-permute-done.3.refs_5_.refs_6_), channel_id=1, source_target_pairs={{0,4},{4,0},{8,12},{12,8},{16,20},{20,16},{24,28},{28,24},{1,5},{5... | collective-permute-start | bytes 2359304 | tf_op jit(solution)/shard_map/ppermute | solution.py:23
  64.7 20.2 %collective-permute-start.12 = (bf16[3072,128]{1,0:T(8,128)(2,1)}, bf16[3072,128]{1,0:T(8,128)(2,1)}, u32[]{:S(2)}, u32[]{:S(2)}) collective-permute-start(bf16[3072,128]{1,0:T(8,128)(2,1)} %collective-permute-done.7.refs_7_.refs_2_), channel_id=1, source_target_pairs={{0,8},{8,16},{12,4},{16,24},{20,12},{28,20},{1,9},{9,17},{13,5},{1... | collective-permute-start | bytes 2359304 | tf_op jit(solution)/shard_map/ppermute | solution.py:23
  70.1 14.8 %copy-start.2 = (f32[2,24,128,128]{3,2,1,0:T(8,128)S(1)}, f32[2,24,128,128]{3,2,1,0:T(8,128)}, u32[]{:S(2)}) copy-start(f32[2,24,128,128]{3,2,1,0:T(8,128)} %copy-done.1) | copy-start | bytes 9437188
  70.1 14.8 %copy-start.4 = (s32[2]{0:T(128)S(1)}, s32[2]{0:T(128)}, u32[]{:S(2)}) copy-start(s32[2]{0:T(128)} %get-tuple-element.30.steps_ref) | copy-start | bytes 28
  70.1 14.8 %copy-start.5 = (s32[1280]{0:T(1024)S(1)}, s32[1280]{0:T(1024)}, u32[]{:S(2)}) copy-start(s32[1280]{0:T(1024)} %get-tuple-element.44.codes_ref) | copy-start | bytes 15364
  70.1 28.0 %collective-permute-start.13 = (bf16[3072,128]{1,0:T(8,128)(2,1)}, bf16[3072,128]{1,0:T(8,128)(2,1)}, u32[]{:S(2)}, u32[]{:S(2)}) collective-permute-start(bf16[3072,128]{1,0:T(8,128)(2,1)} %collective-permute-done.8), channel_id=1, source_target_pairs={{0,4},{4,0},{8,12},{12,8},{16,20},{20,16},{24,28},{28,24},{1,5},{5... | collective-permute-start | bytes 2359304 | tf_op jit(solution)/shard_map/ppermute | solution.py:23
  81.5 16.6 %collective-permute-start.14 = (bf16[512,1536]{1,0:T(8,128)(2,1)}, bf16[512,1536]{1,0:T(8,128)(2,1)}, u32[]{:S(2)}, u32[]{:S(2)}) collective-permute-start(bf16[512,1536]{1,0:T(8,128)(2,1)} %bitcast.5.refs_4_), channel_id=1, source_target_pairs={{0,1},{1,0},{2,3},{3,2},{4,5},{5,4},{6,7},{7,6},{8,9},{9,8},{10,11... | collective-permute-start | bytes 4718600 | tf_op jit(solution)/shard_map/ppermute | solution.py:23
  81.6 16.6 %collective-permute-start.15 = (bf16[512,1536]{1,0:T(8,128)(2,1)}, bf16[512,1536]{1,0:T(8,128)(2,1)}, u32[]{:S(2)}, u32[]{:S(2)}) collective-permute-start(bf16[512,1536]{1,0:T(8,128)(2,1)} %collective-permute-done.10.refs_6_), channel_id=1, source_target_pairs={{0,1},{1,0},{2,3},{3,2},{4,5},{5,4},{6,7},{7,6},{8,9},{9,8},{10,11... | collective-permute-start | bytes 4718600 | tf_op jit(solution)/shard_map/ppermute | solution.py:23
  84.9 13.2 %copy-start.3 = (s32[1280]{0:T(1024)S(1)}, s32[1280]{0:T(1024)}, u32[]{:S(2)}) copy-start(s32[1280]{0:T(1024)} %get-tuple-element.28.codes_ref) | copy-start | bytes 15364
